TPU v7x, 512 devices: a whole 4x8x8 slice. The times are simulated.
512 devices in a mesh: wide: 64 (over x, y, core), narrow: 8 (over z).
Axes of the slice: x: 4, y: 8, z: 8, core: 2. Of those that a mesh axis runs over, the one named last changes fastest.
Arguments:
- source: float32 [512, 32, 1024], P('wide', None, 'narrow'), may hold values from -60 to 60
- permeability: float32 [512, 32, 1024], P('wide', None, 'narrow'), may hold values from 0.1 to 10
- leakage: float32 [512, 32, 1024], P('wide', None, 'narrow'), may hold values from 0.02 to 0.5
Outputs:
- pressure: float32 [512, 32, 1024], P('wide', None, 'narrow')
All inputs are finite; a program needn't handle non-finite values.
Results may differ from a plain program's by a relative error of at most 0.000068.
Values sent between devices are 32-bit elements; how exact they have to be, the bound alone decides.
A program may use at most 64 MiB of HBM per device.

v0:
```python
import jax
import jax.numpy as jnp
from jax import lax
from jax.sharding import PartitionSpec as P

LEVELS = 4


OMEGA = 0.8


def extended(x, sides, width):
    for axis, dim in sides:
        peers, length = (lax.axis_size(axis), x.shape[dim])
        up = [(i, (i + 1) % peers) for i in range(peers - 1)]
        down = [(j, i) for i, j in up]
        last = lax.slice_in_dim(x, length - width, length, axis=dim)
        first = lax.slice_in_dim(x, 0, width, axis=dim)
        before = lax.ppermute(last, axis, up)
        after = lax.ppermute(first, axis, down)
        x = jnp.concatenate([before, x, after], axis=dim)
    return x


def offsets():
    table = []
    for a in (-1, 0, 1):
        for b in (-1, 0, 1):
            for c in (-1, 0, 1):
                count = abs(a) + abs(b) + abs(c)
                if count == 0:
                    continue
                base = (abs(a) * 1.0 + abs(b) * 0.7 + abs(c) * 0.4) / count
                factor = {1: 1.0, 2: 0.25, 3: 0.1}[count]
                table.append((a, b, c, base * factor))
    return table


def window(padded, a, b, c, shape):
    return padded[1 + a : 1 + a + shape[0], 1 + b : 1 + b + shape[1], 1 + c : 1 + c + shape[2]]


def extend(field):
    rimmed = extended(field, (("wide", 0), ("narrow", 2)), 1)
    return jnp.pad(rimmed, ((0, 0), (1, 1), (0, 0)))


def diagonal(perm_pad, leak, scale):
    shape = leak.shape
    center = window(perm_pad, 0, 0, 0, shape)
    total = leak
    for a, b, c, weight in offsets():
        total = total + weight * scale * 0.5 * (center + window(perm_pad, a, b, c, shape))
    return total


def apply_op(field_pad, perm_pad, leak, scale):
    shape = leak.shape
    center = window(perm_pad, 0, 0, 0, shape)
    field = window(field_pad, 0, 0, 0, shape)
    total = leak * field
    for a, b, c, weight in offsets():
        couple = weight * scale * 0.5 * (center + window(perm_pad, a, b, c, shape))
        total = total + couple * (field - window(field_pad, a, b, c, shape))
    return total


def mean_eight(v):
    nx, ny, nz = v.shape
    return v.reshape(nx // 2, 2, ny // 2, 2, nz // 2, 2).sum(axis=(1, 3, 5)) * 0.125


def expand(v):
    return jnp.repeat(jnp.repeat(jnp.repeat(v, 2, axis=0), 2, axis=1), 2, axis=2)


def coarse_part(resid, perm, leak, level):
    coarse_rhs = mean_eight(resid)
    coarse_perm = mean_eight(perm)
    coarse_leak = mean_eight(leak)
    return cycle(coarse_rhs, coarse_perm, coarse_leak, level + 1)


def cycle(rhs, perm, leak, level):
    scale = 0.25**level
    perm_pad = extend(perm)
    diag = diagonal(perm_pad, leak, scale)
    value = OMEGA * rhs / diag
    value = value + OMEGA * (rhs - apply_op(extend(value), perm_pad, leak, scale)) / diag
    if level < LEVELS - 1:
        resid = rhs - apply_op(extend(value), perm_pad, leak, scale)
        coarse = coarse_part(resid, perm, leak, level)
        value = value + expand(coarse)
        for sweep in range(2):
            value = value + OMEGA * (rhs - apply_op(extend(value), perm_pad, leak, scale)) / diag
    return value


def on_device(source, permeability, leakage):
    return cycle(source, permeability, leakage, 0)


def solution(mesh):
    return jax.shard_map(
        on_device,
        mesh=mesh,
        in_specs=(P("wide", None, "narrow"), P("wide", None, "narrow"), P("wide", None, "narrow")),
        out_specs=P("wide", None, "narrow"),
        check_vma=False,
    )
```

profile of v0, /device:TPU:6, one launch (start us, length us, event | category | flops | bytes accessed | tf_op | source)
XLA Modules:
  0.0 400.1 jit_solution(14546908280989067611)
XLA Ops:
  0.0 10.5 %reshape.97 = f32[4,2,16,2,64,2]{5,4,3,2,1,0:T(8,128)} reshape(f32[8,32,128]{2,1,0:T(8,128)} %param.4) | data formatting | bytes 262144 | tf_op jit(solution)/shard_map/reshape | solution.py:70
  17.2 5.1 %collective-permute-start.37 = (f32[1,4,16]{2,1,0:T(4,128)S(1)}, f32[1,4,16]{2,1,0:T(4,128)S(1)}, u32[]{:S(2)}, u32[]{:S(2)}) collective-permute-start(f32[1,4,16]{2,1,0:T(4,128)S(1)} %multiply_bitcast_fusion), channel_id=1, source_target_pairs={{8,0},{16,8},{24,16},{32,24},{40,32},{48,40},{56,48},{64,56},{72,6... | collective-permute-start | bytes 776 | tf_op jit(solution)/shard_map/ppermute | solution.py:20
  24.2 5.8 %collective-permute-start.1 = (f32[1,32,128]{2,1,0:T(8,128)S(1)}, f32[1,32,128]{2,1,0:T(8,128)S(1)}, u32[]{:S(2)}, u32[]{:S(2)}) collective-permute-start(f32[1,32,128]{2,1,0:T(8,128)S(1)} %get-tuple-element.106), channel_id=1, source_target_pairs={{8,0},{16,8},{24,16},{32,24},{40,32},{48,40},{56,48},{64,56},{72,6... | collective-permute-start | bytes 49160 | tf_op jit(solution)/shard_map/ppermute | solution.py:20
  32.5 5.7 %collective-permute-start.13 = (f32[1,16,64]{2,1,0:T(8,128)}, f32[1,16,64]{2,1,0:T(8,128)S(1)}, u32[]{:S(2)}, u32[]{:S(2)}) collective-permute-start(f32[1,16,64]{2,1,0:T(8,128)} %get-tuple-element.136), channel_id=1, source_target_pairs={{8,0},{16,8},{24,16},{32,24},{40,32},{48,40},{56,48},{64,56},{72,6... | collective-permute-start | bytes 12296 | tf_op jit(solution)/shard_map/ppermute | solution.py:20
  38.3 9.7 %reshape.96 = f32[4,2,16,2,64,2]{5,4,3,2,1,0:T(8,128)} reshape(f32[8,32,128]{2,1,0:T(8,128)S(1)} %copy-done.1) | data formatting | bytes 262144 | tf_op jit(solution)/shard_map/reshape | solution.py:70
  56.7 5.8 %collective-permute-start.25 = (f32[1,8,32]{2,1,0:T(8,128)}, f32[1,8,32]{2,1,0:T(8,128)}, u32[]{:S(2)}, u32[]{:S(2)}) collective-permute-start(f32[1,8,32]{2,1,0:T(8,128)} %get-tuple-element.168), channel_id=1, source_target_pairs={{8,0},{16,8},{24,16},{32,24},{40,32},{48,40},{56,48},{64,56},{72,6... | collective-permute-start | bytes 3080 | tf_op jit(solution)/shard_map/ppermute | solution.py:20
  62.6 4.3 %collective-permute-start.2 = (f32[10,32,1]{2,1,0:T(8,128)S(1)}, f32[10,32,1]{2,1,0:T(8,128)S(1)}, u32[]{:S(2)}, u32[]{:S(2)}) collective-permute-start(f32[10,32,1]{2,1,0:T(8,128)S(1)} %get-tuple-element.96), channel_id=1, source_target_pairs={{0,1},{1,2},{2,3},{3,4},{4,5},{5,6},{6,7},{8,9},{9,10},{10,11},{11... | collective-permute-start | bytes 3848 | tf_op jit(solution)/shard_map/ppermute | solution.py:19
  77.6 5.8 %collective-permute-start.5 = (f32[1,32,128]{2,1,0:T(8,128)S(1)}, f32[1,32,128]{2,1,0:T(8,128)S(1)}, u32[]{:S(2)}, u32[]{:S(2)}) collective-permute-start(f32[1,32,128]{2,1,0:T(8,128)S(1)} %get-tuple-element.105), channel_id=1, source_target_pairs={{8,0},{16,8},{24,16},{32,24},{40,32},{48,40},{56,48},{64,56},{72,6... | collective-permute-start | bytes 49160 | tf_op jit(solution)/shard_map/ppermute | solution.py:20
  84.9 4.3 %collective-permute-start.6 = (f32[10,32,1]{2,1,0:T(8,128)S(1)}, f32[10,32,1]{2,1,0:T(8,128)S(1)}, u32[]{:S(2)}, u32[]{:S(2)}) collective-permute-start(f32[10,32,1]{2,1,0:T(8,128)S(1)} %get-tuple-element.94), channel_id=1, source_target_pairs={{0,1},{1,2},{2,3},{3,4},{4,5},{5,6},{6,7},{8,9},{9,10},{10,11},{11... | collective-permute-start | bytes 3848 | tf_op jit(solution)/shard_map/ppermute | solution.py:19
  90.6 6.1 %collective-permute-start.14 = (f32[6,16,1]{2,1,0:T(8,128)S(1)}, f32[6,16,1]{2,1,0:T(8,128)S(1)}, u32[]{:S(2)}, u32[]{:S(2)}) collective-permute-start(f32[6,16,1]{2,1,0:T(8,128)S(1)} %get-tuple-element.126), channel_id=1, source_target_pairs={{0,1},{1,2},{2,3},{3,4},{4,5},{5,6},{6,7},{8,9},{9,10},{10,11},{11... | collective-permute-start | bytes 1160 | tf_op jit(solution)/shard_map/ppermute | solution.py:19
  101.2 5.8 %collective-permute-start.9 = (f32[1,32,128]{2,1,0:T(8,128)S(1)}, f32[1,32,128]{2,1,0:T(8,128)S(1)}, u32[]{:S(2)}, u32[]{:S(2)}) collective-permute-start(f32[1,32,128]{2,1,0:T(8,128)S(1)} %get-tuple-element.103), channel_id=1, source_target_pairs={{8,0},{16,8},{24,16},{32,24},{40,32},{48,40},{56,48},{64,56},{72,6... | collective-permute-start | bytes 49160 | tf_op jit(solution)/shard_map/ppermute | solution.py:20
  108.5 5.8 %collective-permute-start.10 = (f32[10,32,1]{2,1,0:T(8,128)S(1)}, f32[10,32,1]{2,1,0:T(8,128)S(1)}, u32[]{:S(2)}, u32[]{:S(2)}) collective-permute-start(f32[10,32,1]{2,1,0:T(8,128)S(1)} %get-tuple-element.90), channel_id=1, source_target_pairs={{0,1},{1,2},{2,3},{3,4},{4,5},{5,6},{6,7},{8,9},{9,10},{10,11},{11... | collective-permute-start | bytes 3848 | tf_op jit(solution)/shard_map/ppermute | solution.py:19
  117.1 4.4 %collective-permute-done.11 = f32[10,32,1]{2,1,0:T(8,128)S(1)} collective-permute-done((f32[10,32,1]{2,1,0:T(8,128)S(1)}, f32[10,32,1]{2,1,0:T(8,128)S(1)}, u32[]{:S(2)}, u32[]{:S(2)}) %collective-permute-start.11) | collective-permute-done | bytes 1312 | tf_op jit(solution)/shard_map/ppermute | solution.py:20
  124.1 10.5 %reshape.95 = f32[4,2,16,2,64,2]{5,4,3,2,1,0:T(8,128)} reshape(f32[8,32,128]{2,1,0:T(8,128)} %fusion.131) | data formatting | bytes 262144 | tf_op jit(solution)/shard_map/reshape | solution.py:70
  141.3 5.8 %collective-permute-start.17 = (f32[1,16,64]{2,1,0:T(8,128)S(1)}, f32[1,16,64]{2,1,0:T(8,128)S(1)}, u32[]{:S(2)}, u32[]{:S(2)}) collective-permute-start(f32[1,16,64]{2,1,0:T(8,128)S(1)} %get-tuple-element.135), channel_id=1, source_target_pairs={{8,0},{16,8},{24,16},{32,24},{40,32},{48,40},{56,48},{64,56},{72,6... | collective-permute-start | bytes 12296 | tf_op jit(solution)/shard_map/ppermute | solution.py:20
  153.8 5.2 %collective-permute-start.26 = (f32[4,8,1]{2,1,0:T(8,128)S(1)}, f32[4,8,1]{2,1,0:T(8,128)S(1)}, u32[]{:S(2)}, u32[]{:S(2)}) collective-permute-start(f32[4,8,1]{2,1,0:T(8,128)S(1)} %get-tuple-element.156), channel_id=1, source_target_pairs={{0,1},{1,2},{2,3},{3,4},{4,5},{5,6},{6,7},{8,9},{9,10},{10,11},{11... | collective-permute-start | bytes 392 | tf_op jit(solution)/shard_map/ppermute | solution.py:19
  162.7 5.8 %collective-permute-start.21 = (f32[1,16,64]{2,1,0:T(8,128)S(1)}, f32[1,16,64]{2,1,0:T(8,128)S(1)}, u32[]{:S(2)}, u32[]{:S(2)}) collective-permute-start(f32[1,16,64]{2,1,0:T(8,128)S(1)} %get-tuple-element.133), channel_id=1, source_target_pairs={{8,0},{16,8},{24,16},{32,24},{40,32},{48,40},{56,48},{64,56},{72,6... | collective-permute-start | bytes 12296 | tf_op jit(solution)/shard_map/ppermute | solution.py:20
  169.9 5.8 %collective-permute-start.22 = (f32[6,16,1]{2,1,0:T(8,128)S(1)}, f32[6,16,1]{2,1,0:T(8,128)S(1)}, u32[]{:S(2)}, u32[]{:S(2)}) collective-permute-start(f32[6,16,1]{2,1,0:T(8,128)S(1)} %get-tuple-element.118), channel_id=1, source_target_pairs={{0,1},{1,2},{2,3},{3,4},{4,5},{5,6},{6,7},{8,9},{9,10},{10,11},{11... | collective-permute-start | bytes 1160 | tf_op jit(solution)/shard_map/ppermute | solution.py:19
  189.2 5.8 %collective-permute-start.29 = (f32[1,8,32]{2,1,0:T(8,128)S(1)}, f32[1,8,32]{2,1,0:T(8,128)S(1)}, u32[]{:S(2)}, u32[]{:S(2)}) collective-permute-start(f32[1,8,32]{2,1,0:T(8,128)S(1)} %get-tuple-element.167), channel_id=1, source_target_pairs={{8,0},{16,8},{24,16},{32,24},{40,32},{48,40},{56,48},{64,56},{72,6... | collective-permute-start | bytes 3080 | tf_op jit(solution)/shard_map/ppermute | solution.py:20
  199.8 4.3 %collective-permute-start.30 = (f32[4,8,1]{2,1,0:T(8,128)S(1)}, f32[4,8,1]{2,1,0:T(8,128)S(1)}, u32[]{:S(2)}, u32[]{:S(2)}) collective-permute-start(f32[4,8,1]{2,1,0:T(8,128)S(1)} %get-tuple-element.152), channel_id=1, source_target_pairs={{0,1},{1,2},{2,3},{3,4},{4,5},{5,6},{6,7},{8,9},{9,10},{10,11},{11... | collective-permute-start | bytes 392 | tf_op jit(solution)/shard_map/ppermute | solution.py:19
  214.0 5.8 %collective-permute-start.33 = (f32[1,8,32]{2,1,0:T(8,128)S(1)}, f32[1,8,32]{2,1,0:T(8,128)S(1)}, u32[]{:S(2)}, u32[]{:S(2)}) collective-permute-start(f32[1,8,32]{2,1,0:T(8,128)S(1)} %get-tuple-element.165), channel_id=1, source_target_pairs={{8,0},{16,8},{24,16},{32,24},{40,32},{48,40},{56,48},{64,56},{72,6... | collective-permute-start | bytes 3080 | tf_op jit(solution)/shard_map/ppermute | solution.py:20
  242.7 5.1 %collective-permute-done.40 = f32[1,4,16]{2,1,0:T(4,128)S(1)} collective-permute-done((f32[1,4,16]{2,1,0:T(4,128)S(1)}, f32[1,4,16]{2,1,0:T(4,128)S(1)}, u32[]{:S(2)}, u32[]{:S(2)}) %collective-permute-start.40) | collective-permute-done | bytes 288 | tf_op jit(solution)/shard_map/ppermute | solution.py:19
  264.4 5.8 %collective-permute-start.45 = (f32[1,8,32]{2,1,0:T(8,128)S(1)}, f32[1,8,32]{2,1,0:T(8,128)S(1)}, u32[]{:S(2)}, u32[]{:S(2)}) collective-permute-start(f32[1,8,32]{2,1,0:T(8,128)S(1)} %get-tuple-element.161), channel_id=1, source_target_pairs={{8,0},{16,8},{24,16},{32,24},{40,32},{48,40},{56,48},{64,56},{72,6... | collective-permute-start | bytes 3080 | tf_op jit(solution)/shard_map/ppermute | solution.py:20
  284.3 5.8 %collective-permute-start.49 = (f32[1,8,32]{2,1,0:T(8,128)S(1)}, f32[1,8,32]{2,1,0:T(8,128)S(1)}, u32[]{:S(2)}, u32[]{:S(2)}) collective-permute-start(f32[1,8,32]{2,1,0:T(8,128)S(1)} %get-tuple-element.159), channel_id=1, source_target_pairs={{8,0},{16,8},{24,16},{32,24},{40,32},{48,40},{56,48},{64,56},{72,6... | collective-permute-start | bytes 3080 | tf_op jit(solution)/shard_map/ppermute | solution.py:20
  310.3 5.8 %collective-permute-start.53 = (f32[1,16,64]{2,1,0:T(8,128)S(1)}, f32[1,16,64]{2,1,0:T(8,128)S(1)}, u32[]{:S(2)}, u32[]{:S(2)}) collective-permute-start(f32[1,16,64]{2,1,0:T(8,128)S(1)} %get-tuple-element.131), channel_id=1, source_target_pairs={{8,0},{16,8},{24,16},{32,24},{40,32},{48,40},{56,48},{64,56},{72,6... | collective-permute-start | bytes 12296 | tf_op jit(solution)/shard_map/ppermute | solution.py:20
  323.0 4.3 %collective-permute-done.55 = f32[6,16,1]{2,1,0:T(8,128)S(1)} collective-permute-done((f32[6,16,1]{2,1,0:T(8,128)S(1)}, f32[6,16,1]{2,1,0:T(8,128)S(1)}, u32[]{:S(2)}, u32[]{:S(2)}) %collective-permute-start.55) | collective-permute-done | bytes 416 | tf_op jit(solution)/shard_map/ppermute | solution.py:20
  330.8 5.8 %collective-permute-start.57 = (f32[1,16,64]{2,1,0:T(8,128)S(1)}, f32[1,16,64]{2,1,0:T(8,128)S(1)}, u32[]{:S(2)}, u32[]{:S(2)}) collective-permute-start(f32[1,16,64]{2,1,0:T(8,128)S(1)} %get-tuple-element.129), channel_id=1, source_target_pairs={{8,0},{16,8},{24,16},{32,24},{40,32},{48,40},{56,48},{64,56},{72,6... | collective-permute-start | bytes 12296 | tf_op jit(solution)/shard_map/ppermute | solution.py:20
  342.8 4.3 %collective-permute-done.59 = f32[6,16,1]{2,1,0:T(8,128)S(1)} collective-permute-done((f32[6,16,1]{2,1,0:T(8,128)S(1)}, f32[6,16,1]{2,1,0:T(8,128)S(1)}, u32[]{:S(2)}, u32[]{:S(2)}) %collective-permute-start.59) | collective-permute-done | bytes 416 | tf_op jit(solution)/shard_map/ppermute | solution.py:20
  357.7 5.8 %collective-permute-start.61 = (f32[1,32,128]{2,1,0:T(8,128)S(1)}, f32[1,32,128]{2,1,0:T(8,128)S(1)}, u32[]{:S(2)}, u32[]{:S(2)}) collective-permute-start(f32[1,32,128]{2,1,0:T(8,128)S(1)} %get-tuple-element.101), channel_id=1, source_target_pairs={{8,0},{16,8},{24,16},{32,24},{40,32},{48,40},{56,48},{64,56},{72,6... | collective-permute-start | bytes 49160 | tf_op jit(solution)/shard_map/ppermute | solution.py:20
  370.9 4.4 %collective-permute-done.63 = f32[10,32,1]{2,1,0:T(8,128)S(1)} collective-permute-done((f32[10,32,1]{2,1,0:T(8,128)S(1)}, f32[10,32,1]{2,1,0:T(8,128)S(1)}, u32[]{:S(2)}, u32[]{:S(2)}) %collective-permute-start.63) | collective-permute-done | bytes 1312 | tf_op jit(solution)/shard_map/ppermute | solution.py:20
  379.6 5.8 %collective-permute-start.65 = (f32[1,32,128]{2,1,0:T(8,128)S(1)}, f32[1,32,128]{2,1,0:T(8,128)S(1)}, u32[]{:S(2)}, u32[]{:S(2)}) collective-permute-start(f32[1,32,128]{2,1,0:T(8,128)S(1)} %get-tuple-element.99), channel_id=1, source_target_pairs={{8,0},{16,8},{24,16},{32,24},{40,32},{48,40},{56,48},{64,56},{72,6... | collective-permute-start | bytes 49160 | tf_op jit(solution)/shard_map/ppermute | solution.py:20
  392.8 4.4 %collective-permute-done.67 = f32[10,32,1]{2,1,0:T(8,128)S(1)} collective-permute-done((f32[10,32,1]{2,1,0:T(8,128)S(1)}, f32[10,32,1]{2,1,0:T(8,128)S(1)}, u32[]{:S(2)}, u32[]{:S(2)}) %collective-permute-start.67) | collective-permute-done | bytes 1312 | tf_op jit(solution)/shard_map/ppermute | solution.py:20
  (428 shorter events, 212.9 us)
Async XLA Ops:
  17.2 45.4 %collective-permute-start.37 = (f32[1,4,16]{2,1,0:T(4,128)S(1)}, f32[1,4,16]{2,1,0:T(4,128)S(1)}, u32[]{:S(2)}, u32[]{:S(2)}) collective-permute-start(f32[1,4,16]{2,1,0:T(4,128)S(1)} %multiply_bitcast_fusion), channel_id=1, source_target_pairs={{8,0},{16,8},{24,16},{32,24},{40,32},{48,40},{56,48},{64,56},{72,6... | collective-permute-start | bytes 776 | tf_op jit(solution)/shard_map/ppermute | solution.py:20
  22.3 44.6 %collective-permute-start.36 = (f32[1,4,16]{2,1,0:T(4,128)S(1)}, f32[1,4,16]{2,1,0:T(4,128)S(1)}, u32[]{:S(2)}, u32[]{:S(2)}) collective-permute-start(f32[1,4,16]{2,1,0:T(4,128)S(1)} %multiply_bitcast_fusion), channel_id=1, source_target_pairs={{0,8},{8,16},{16,24},{24,32},{32,40},{40,48},{48,56},{56,64},{64,7... | collective-permute-start | bytes 776 | tf_op jit(solution)/shard_map/ppermute | solution.py:19
  24.2 32.4 %collective-permute-start.1 = (f32[1,32,128]{2,1,0:T(8,128)S(1)}, f32[1,32,128]{2,1,0:T(8,128)S(1)}, u32[]{:S(2)}, u32[]{:S(2)}) collective-permute-start(f32[1,32,128]{2,1,0:T(8,128)S(1)} %get-tuple-element.106), channel_id=1, source_target_pairs={{8,0},{16,8},{24,16},{32,24},{40,32},{48,40},{56,48},{64,56},{72,6... | collective-permute-start | bytes 49160 | tf_op jit(solution)/shard_map/ppermute | solution.py:20
  30.0 24.7 %collective-permute-start = (f32[1,32,128]{2,1,0:T(8,128)S(1)}, f32[1,32,128]{2,1,0:T(8,128)S(1)}, u32[]{:S(2)}, u32[]{:S(2)}) collective-permute-start(f32[1,32,128]{2,1,0:T(8,128)S(1)} %get-tuple-element.107), channel_id=1, source_target_pairs={{0,8},{8,16},{16,24},{24,32},{32,40},{40,48},{48,56},{56,64},{64,7... | collective-permute-start | bytes 49160 | tf_op jit(solution)/shard_map/ppermute | solution.py:19
  32.5 45.0 %collective-permute-start.13 = (f32[1,16,64]{2,1,0:T(8,128)}, f32[1,16,64]{2,1,0:T(8,128)S(1)}, u32[]{:S(2)}, u32[]{:S(2)}) collective-permute-start(f32[1,16,64]{2,1,0:T(8,128)} %get-tuple-element.136), channel_id=1, source_target_pairs={{8,0},{16,8},{24,16},{32,24},{40,32},{48,40},{56,48},{64,56},{72,6... | collective-permute-start | bytes 12296 | tf_op jit(solution)/shard_map/ppermute | solution.py:20
  54.7 28.6 %collective-permute-start.12 = (f32[1,16,64]{2,1,0:T(8,128)}, f32[1,16,64]{2,1,0:T(8,128)S(1)}, u32[]{:S(2)}, u32[]{:S(2)}) collective-permute-start(f32[1,16,64]{2,1,0:T(8,128)} %get-tuple-element.137), channel_id=1, source_target_pairs={{0,8},{8,16},{16,24},{24,32},{32,40},{40,48},{48,56},{56,64},{64,7... | collective-permute-start | bytes 12296 | tf_op jit(solution)/shard_map/ppermute | solution.py:19
  56.7 90.4 %collective-permute-start.25 = (f32[1,8,32]{2,1,0:T(8,128)}, f32[1,8,32]{2,1,0:T(8,128)}, u32[]{:S(2)}, u32[]{:S(2)}) collective-permute-start(f32[1,8,32]{2,1,0:T(8,128)} %get-tuple-element.168), channel_id=1, source_target_pairs={{8,0},{16,8},{24,16},{32,24},{40,32},{48,40},{56,48},{64,56},{72,6... | collective-permute-start | bytes 3080 | tf_op jit(solution)/shard_map/ppermute | solution.py:20
  69.7 77.4 %collective-permute-start.24 = (f32[1,8,32]{2,1,0:T(8,128)}, f32[1,8,32]{2,1,0:T(8,128)}, u32[]{:S(2)}, u32[]{:S(2)}) collective-permute-start(f32[1,8,32]{2,1,0:T(8,128)} %get-tuple-element.169), channel_id=1, source_target_pairs={{0,8},{8,16},{16,24},{24,32},{32,40},{40,48},{48,56},{56,64},{64,7... | collective-permute-start | bytes 3080 | tf_op jit(solution)/shard_map/ppermute | solution.py:19
  75.6 7.7 %collective-permute-start.4 = (f32[1,32,128]{2,1,0:T(8,128)S(1)}, f32[1,32,128]{2,1,0:T(8,128)S(1)}, u32[]{:S(2)}, u32[]{:S(2)}) collective-permute-start(f32[1,32,128]{2,1,0:T(8,128)S(1)} %get-tuple-element.104), channel_id=1, source_target_pairs={{0,8},{8,16},{16,24},{24,32},{32,40},{40,48},{48,56},{56,64},{64,7... | collective-permute-start | bytes 49160 | tf_op jit(solution)/shard_map/ppermute | solution.py:19
  84.9 11.8 %collective-permute-start.6 = (f32[10,32,1]{2,1,0:T(8,128)S(1)}, f32[10,32,1]{2,1,0:T(8,128)S(1)}, u32[]{:S(2)}, u32[]{:S(2)}) collective-permute-start(f32[10,32,1]{2,1,0:T(8,128)S(1)} %get-tuple-element.94), channel_id=1, source_target_pairs={{0,1},{1,2},{2,3},{3,4},{4,5},{5,6},{6,7},{8,9},{9,10},{10,11},{11... | collective-permute-start | bytes 3848 | tf_op jit(solution)/shard_map/ppermute | solution.py:19
  89.2 8.8 %collective-permute-start.7 = (f32[10,32,1]{2,1,0:T(8,128)S(1)}, f32[10,32,1]{2,1,0:T(8,128)S(1)}, u32[]{:S(2)}, u32[]{:S(2)}) collective-permute-start(f32[10,32,1]{2,1,0:T(8,128)S(1)} %get-tuple-element.95), channel_id=1, source_target_pairs={{1,0},{2,1},{3,2},{4,3},{5,4},{6,5},{7,6},{9,8},{10,9},{11,10},{12... | collective-permute-start | bytes 3848 | tf_op jit(solution)/shard_map/ppermute | solution.py:20
  90.6 10.6 %collective-permute-start.14 = (f32[6,16,1]{2,1,0:T(8,128)S(1)}, f32[6,16,1]{2,1,0:T(8,128)S(1)}, u32[]{:S(2)}, u32[]{:S(2)}) collective-permute-start(f32[6,16,1]{2,1,0:T(8,128)S(1)} %get-tuple-element.126), channel_id=1, source_target_pairs={{0,1},{1,2},{2,3},{3,4},{4,5},{5,6},{6,7},{8,9},{9,10},{10,11},{11... | collective-permute-start | bytes 1160 | tf_op jit(solution)/shard_map/ppermute | solution.py:19
  96.7 10.3 %collective-permute-start.15 = (f32[6,16,1]{2,1,0:T(8,128)S(1)}, f32[6,16,1]{2,1,0:T(8,128)S(1)}, u32[]{:S(2)}, u32[]{:S(2)}) collective-permute-start(f32[6,16,1]{2,1,0:T(8,128)S(1)} %get-tuple-element.127), channel_id=1, source_target_pairs={{1,0},{2,1},{3,2},{4,3},{5,4},{6,5},{7,6},{9,8},{10,9},{11,10},{12... | collective-permute-start | bytes 1160 | tf_op jit(solution)/shard_map/ppermute | solution.py:20
  99.3 8.4 %collective-permute-start.8 = (f32[1,32,128]{2,1,0:T(8,128)S(1)}, f32[1,32,128]{2,1,0:T(8,128)S(1)}, u32[]{:S(2)}, u32[]{:S(2)}) collective-permute-start(f32[1,32,128]{2,1,0:T(8,128)S(1)} %get-tuple-element.102), channel_id=1, source_target_pairs={{0,8},{8,16},{16,24},{24,32},{32,40},{40,48},{48,56},{56,64},{64,7... | collective-permute-start | bytes 49160 | tf_op jit(solution)/shard_map/ppermute | solution.py:19
  108.5 8.6 %collective-permute-start.10 = (f32[10,32,1]{2,1,0:T(8,128)S(1)}, f32[10,32,1]{2,1,0:T(8,128)S(1)}, u32[]{:S(2)}, u32[]{:S(2)}) collective-permute-start(f32[10,32,1]{2,1,0:T(8,128)S(1)} %get-tuple-element.90), channel_id=1, source_target_pairs={{0,1},{1,2},{2,3},{3,4},{4,5},{5,6},{6,7},{8,9},{9,10},{10,11},{11... | collective-permute-start | bytes 3848 | tf_op jit(solution)/shard_map/ppermute | solution.py:19
  139.2 8.5 %collective-permute-start.16 = (f32[1,16,64]{2,1,0:T(8,128)S(1)}, f32[1,16,64]{2,1,0:T(8,128)S(1)}, u32[]{:S(2)}, u32[]{:S(2)}) collective-permute-start(f32[1,16,64]{2,1,0:T(8,128)S(1)} %get-tuple-element.134), channel_id=1, source_target_pairs={{0,8},{8,16},{16,24},{24,32},{32,40},{40,48},{48,56},{56,64},{64,7... | collective-permute-start | bytes 12296 | tf_op jit(solution)/shard_map/ppermute | solution.py:19
  148.5 11.8 %collective-permute-start.18 = (f32[6,16,1]{2,1,0:T(8,128)S(1)}, f32[6,16,1]{2,1,0:T(8,128)S(1)}, u32[]{:S(2)}, u32[]{:S(2)}) collective-permute-start(f32[6,16,1]{2,1,0:T(8,128)S(1)} %get-tuple-element.122), channel_id=1, source_target_pairs={{0,1},{1,2},{2,3},{3,4},{4,5},{5,6},{6,7},{8,9},{9,10},{10,11},{11... | collective-permute-start | bytes 1160 | tf_op jit(solution)/shard_map/ppermute | solution.py:19
  152.4 7.9 %collective-permute-start.19 = (f32[6,16,1]{2,1,0:T(8,128)S(1)}, f32[6,16,1]{2,1,0:T(8,128)S(1)}, u32[]{:S(2)}, u32[]{:S(2)}) collective-permute-start(f32[6,16,1]{2,1,0:T(8,128)S(1)} %get-tuple-element.123), channel_id=1, source_target_pairs={{1,0},{2,1},{3,2},{4,3},{5,4},{6,5},{7,6},{9,8},{10,9},{11,10},{12... | collective-permute-start | bytes 1160 | tf_op jit(solution)/shard_map/ppermute | solution.py:20
  153.8 14.7 %collective-permute-start.26 = (f32[4,8,1]{2,1,0:T(8,128)S(1)}, f32[4,8,1]{2,1,0:T(8,128)S(1)}, u32[]{:S(2)}, u32[]{:S(2)}) collective-permute-start(f32[4,8,1]{2,1,0:T(8,128)S(1)} %get-tuple-element.156), channel_id=1, source_target_pairs={{0,1},{1,2},{2,3},{3,4},{4,5},{5,6},{6,7},{8,9},{9,10},{10,11},{11... | collective-permute-start | bytes 392 | tf_op jit(solution)/shard_map/ppermute | solution.py:19
  159.0 9.5 %collective-permute-start.27 = (f32[4,8,1]{2,1,0:T(8,128)S(1)}, f32[4,8,1]{2,1,0:T(8,128)S(1)}, u32[]{:S(2)}, u32[]{:S(2)}) collective-permute-start(f32[4,8,1]{2,1,0:T(8,128)S(1)} %get-tuple-element.157), channel_id=1, source_target_pairs={{1,0},{2,1},{3,2},{4,3},{5,4},{6,5},{7,6},{9,8},{10,9},{11,10},{12... | collective-permute-start | bytes 392 | tf_op jit(solution)/shard_map/ppermute | solution.py:20
  160.8 9.1 %collective-permute-start.20 = (f32[1,16,64]{2,1,0:T(8,128)S(1)}, f32[1,16,64]{2,1,0:T(8,128)S(1)}, u32[]{:S(2)}, u32[]{:S(2)}) collective-permute-start(f32[1,16,64]{2,1,0:T(8,128)S(1)} %get-tuple-element.132), channel_id=1, source_target_pairs={{0,8},{8,16},{16,24},{24,32},{32,40},{40,48},{48,56},{56,64},{64,7... | collective-permute-start | bytes 12296 | tf_op jit(solution)/shard_map/ppermute | solution.py:19
  169.9 8.5 %collective-permute-start.22 = (f32[6,16,1]{2,1,0:T(8,128)S(1)}, f32[6,16,1]{2,1,0:T(8,128)S(1)}, u32[]{:S(2)}, u32[]{:S(2)}) collective-permute-start(f32[6,16,1]{2,1,0:T(8,128)S(1)} %get-tuple-element.118), channel_id=1, source_target_pairs={{0,1},{1,2},{2,3},{3,4},{4,5},{5,6},{6,7},{8,9},{9,10},{10,11},{11... | collective-permute-start | bytes 1160 | tf_op jit(solution)/shard_map/ppermute | solution.py:19
  187.3 12.4 %collective-permute-start.28 = (f32[1,8,32]{2,1,0:T(8,128)S(1)}, f32[1,8,32]{2,1,0:T(8,128)S(1)}, u32[]{:S(2)}, u32[]{:S(2)}) collective-permute-start(f32[1,8,32]{2,1,0:T(8,128)S(1)} %get-tuple-element.166), channel_id=1, source_target_pairs={{0,8},{8,16},{16,24},{24,32},{32,40},{40,48},{48,56},{56,64},{64,7... | collective-permute-start | bytes 3080 | tf_op jit(solution)/shard_map/ppermute | solution.py:19
  189.2 10.5 %collective-permute-start.29 = (f32[1,8,32]{2,1,0:T(8,128)S(1)}, f32[1,8,32]{2,1,0:T(8,128)S(1)}, u32[]{:S(2)}, u32[]{:S(2)}) collective-permute-start(f32[1,8,32]{2,1,0:T(8,128)S(1)} %get-tuple-element.167), channel_id=1, source_target_pairs={{8,0},{16,8},{24,16},{32,24},{40,32},{48,40},{56,48},{64,56},{72,6... | collective-permute-start | bytes 3080 | tf_op jit(solution)/shard_map/ppermute | solution.py:20
  195.8 23.9 %collective-permute-start.38 = (f32[3,4,1]{2,1,0:T(4,128)S(1)}, f32[3,4,1]{2,1,0:T(4,128)S(1)}, u32[]{:S(2)}, u32[]{:S(2)}) collective-permute-start(f32[3,4,1]{2,1,0:T(4,128)S(1)} %get-tuple-element.176), channel_id=1, source_target_pairs={{0,1},{1,2},{2,3},{3,4},{4,5},{5,6},{6,7},{8,9},{9,10},{10,11},{11... | collective-permute-start | bytes 152 | tf_op jit(solution)/shard_map/ppermute | solution.py:19
  205.5 14.3 %collective-permute-start.39 = (f32[3,4,1]{2,1,0:T(4,128)S(1)}, f32[3,4,1]{2,1,0:T(4,128)S(1)}, u32[]{:S(2)}, u32[]{:S(2)}) collective-permute-start(f32[3,4,1]{2,1,0:T(4,128)S(1)} %get-tuple-element.177), channel_id=1, source_target_pairs={{1,0},{2,1},{3,2},{4,3},{5,4},{6,5},{7,6},{9,8},{10,9},{11,10},{12... | collective-permute-start | bytes 152 | tf_op jit(solution)/shard_map/ppermute | solution.py:20
  212.0 9.1 %collective-permute-start.32 = (f32[1,8,32]{2,1,0:T(8,128)S(1)}, f32[1,8,32]{2,1,0:T(8,128)S(1)}, u32[]{:S(2)}, u32[]{:S(2)}) collective-permute-start(f32[1,8,32]{2,1,0:T(8,128)S(1)} %get-tuple-element.164), channel_id=1, source_target_pairs={{0,8},{8,16},{16,24},{24,32},{32,40},{40,48},{48,56},{56,64},{64,7... | collective-permute-start | bytes 3080 | tf_op jit(solution)/shard_map/ppermute | solution.py:19
  282.4 7.7 %collective-permute-start.48 = (f32[1,8,32]{2,1,0:T(8,128)S(1)}, f32[1,8,32]{2,1,0:T(8,128)S(1)}, u32[]{:S(2)}, u32[]{:S(2)}) collective-permute-start(f32[1,8,32]{2,1,0:T(8,128)S(1)} %get-tuple-element.158), channel_id=1, source_target_pairs={{0,8},{8,16},{16,24},{24,32},{32,40},{40,48},{48,56},{56,64},{64,7... | collective-permute-start | bytes 3080 | tf_op jit(solution)/shard_map/ppermute | solution.py:19
  308.2 7.8 %collective-permute-start.52 = (f32[1,16,64]{2,1,0:T(8,128)S(1)}, f32[1,16,64]{2,1,0:T(8,128)S(1)}, u32[]{:S(2)}, u32[]{:S(2)}) collective-permute-start(f32[1,16,64]{2,1,0:T(8,128)S(1)} %get-tuple-element.130), channel_id=1, source_target_pairs={{0,8},{8,16},{16,24},{24,32},{32,40},{40,48},{48,56},{56,64},{64,7... | collective-permute-start | bytes 12296 | tf_op jit(solution)/shard_map/ppermute | solution.py:19
  328.8 7.7 %collective-permute-start.56 = (f32[1,16,64]{2,1,0:T(8,128)S(1)}, f32[1,16,64]{2,1,0:T(8,128)S(1)}, u32[]{:S(2)}, u32[]{:S(2)}) collective-permute-start(f32[1,16,64]{2,1,0:T(8,128)S(1)} %get-tuple-element.128), channel_id=1, source_target_pairs={{0,8},{8,16},{16,24},{24,32},{32,40},{40,48},{48,56},{56,64},{64,7... | collective-permute-start | bytes 12296 | tf_op jit(solution)/shard_map/ppermute | solution.py:19
  355.7 7.7 %collective-permute-start.60 = (f32[1,32,128]{2,1,0:T(8,128)S(1)}, f32[1,32,128]{2,1,0:T(8,128)S(1)}, u32[]{:S(2)}, u32[]{:S(2)}) collective-permute-start(f32[1,32,128]{2,1,0:T(8,128)S(1)} %get-tuple-element.100), channel_id=1, source_target_pairs={{0,8},{8,16},{16,24},{24,32},{32,40},{40,48},{48,56},{56,64},{64,7... | collective-permute-start | bytes 49160 | tf_op jit(solution)/shard_map/ppermute | solution.py:19
  377.7 7.7 %collective-permute-start.64 = (f32[1,32,128]{2,1,0:T(8,128)S(1)}, f32[1,32,128]{2,1,0:T(8,128)S(1)}, u32[]{:S(2)}, u32[]{:S(2)}) collective-permute-start(f32[1,32,128]{2,1,0:T(8,128)S(1)} %get-tuple-element.98), channel_id=1, source_target_pairs={{0,8},{8,16},{16,24},{24,32},{32,40},{40,48},{48,56},{56,64},{64,7... | collective-permute-start | bytes 49160 | tf_op jit(solution)/shard_map/ppermute | solution.py:19
  (127 other events, 5349.9 us)
where the time goes:
time: 404 us; the launch traced here: 400 us
  starting transfers between devices  222 us (55%)
  waiting for transfers between devices  68.8 us (17%)
  local copies, waits for them, and re-layouts  57.2 us (14%)
  other arithmetic  49.7 us (12%)
    ppermute x34, starting transfers between devices, extended(): after = lax.ppermute(first, axis, down)  118 us
    ppermute x34, starting transfers between devices, extended(): before = lax.ppermute(last, axis, up)  104 us
    ppermute x34, waiting for transfers between devices, extended(): after = lax.ppermute(first, axis, down)  58.3 us
    reshape x4, local copies, waits for them, and re-layouts, mean_eight(): v.reshape(nx // 2, 2, ny // 2, 2, nz // 2, 2).sum(axis=(1, 3, 5)) * 0.125  32.6 us
    reduce_sum x12, other arithmetic, mean_eight(): v.reshape(nx // 2, 2, ny // 2, 2, nz // 2, 2).sum(axis=(1, 3, 5)) * 0.125  16.9 us
    add x10, other arithmetic, cycle(): value + OMEGA * (rhs - apply_op(extend(value), perm_pad, leak, scale)) /...  12 us
    concatenate x49, other arithmetic, extended(): x = jnp.concatenate([before, x, after], axis=dim)  12 us
    ppermute x34, waiting for transfers between devices, extended(): before = lax.ppermute(last, axis, up)  10.5 us
  transfers between devices with their start and end apart: 68, of which 30 were waited for; matrix products, arithmetic and copies ran while one was open for 12% of the time, Pallas kernels for 0%

commit v1 on v0

v1 whole, which is shorter than its diff:
```python
import jax
import jax.numpy as jnp
from jax import lax
from jax.experimental import pallas as pl
from jax.experimental.pallas import tpu as pltpu
from jax.sharding import PartitionSpec as P

MESH = pl.DeviceIdType.MESH
OMEGA = 0.8
F32 = jnp.float32


def weight(a, b, c):
    n = a + b + c
    return (a * 1.0 + b * 0.7 + c * 0.4) / n * {1: 1.0, 2: 0.25, 3: 0.1}[n]


CX, CY, CZ = weight(1, 0, 0), weight(0, 1, 0), weight(0, 0, 1)
CXY, CXZ, CYZ, CXYZ = weight(1, 1, 0), weight(1, 0, 1), weight(0, 1, 1), weight(1, 1, 1)
CALL = 2 * (CX + CY + CZ) + 4 * (CXY + CXZ + CYZ) + 8 * CXYZ

SIDES = [(a, b) for b in (-1, 1) for a in (-1, 0, 1)]
FAR = [(a, b) for a in range(-4, 5) for b in (-1, 0, 1) if (a, b) != (0, 0)]


def iota(shape, dim):
    return lax.broadcasted_iota(jnp.int32, shape, dim)


def lanes():
    return iota((8, 128), 1)


def rot(x, shift, axis):
    shift %= x.shape[axis]
    return x if shift == 0 else pltpu.roll(x, shift, axis)


def ysum(t):
    axis = t.ndim - 2
    n = t.shape[axis]
    row = iota(t.shape, axis)
    up = jnp.where(row == 0, 0.0, rot(t, 1, axis))
    down = jnp.where(row == n - 1, 0.0, rot(t, n - 1, axis))
    return up + down


def planes_of(u, pz):
    g = CX * u + CXZ * pz + ysum(CXY * u + CXYZ * pz)
    h = CZ * pz + ysum(CY * u + CYZ * pz)
    return g, h


def zsum_pair(m, s):
    lane = iota(m.shape, 1)
    first, last = lane == 0, lane == 127
    rm, rs, lm, ls = rot(m, 1, 1), rot(s, 1, 1), rot(m, 127, 1), rot(s, 127, 1)
    pm = jnp.where(first, rs, rm) + jnp.where(last, ls, lm)
    ps = jnp.where(first, rm, rs) + jnp.where(last, lm, ls)
    return pm, ps


def zsum_main(m, s):
    lane = iota(m.shape, 1)
    return jnp.where(lane == 0, rot(s, 1, 1), rot(m, 1, 1)) + jnp.where(lane == 127, rot(s, 127, 1), rot(m, 127, 1))


def ring_sum(u):
    pz = rot(u, 1, 2) + rot(u, 127, 2)
    g, h = planes_of(u, pz)
    return g[:-2] + g[2:] + h[1:-1]


def ring_apply(v, k, diag, half):
    return diag * v[1:-1] - half * (k[1:-1] * ring_sum(v) + ring_sum(k * v))


def dot(a, b):
    return lax.dot_general(a, b, (((1,), (0,)), ((), ())), precision=lax.Precision.HIGHEST, preferred_element_type=F32)


def ring_map(fine_of, coarse_cut, transpose=False):
    f_dim = 1 if transpose else 0
    i, j = iota((128, 128), f_dim), iota((128, 128), 1 - f_dim)
    return ((fine_of(i) >> 1) == jnp.where(j < coarse_cut, j, j - 128)).astype(F32)


def cut(c):
    return lambda i: jnp.where(i < c, i, i - 128)


def main_z(i):
    return i


def side_z(i):
    return jnp.where(i < 64, 128 + i, i - 128)


def halve_rows(ref, n):
    return ref[pl.ds(0, n, stride=2), :] + ref[pl.ds(1, n, stride=2), :]


def double_rows(ref, x):
    n = x.shape[0]
    ref[pl.ds(0, n, stride=2), :] = x
    ref[pl.ds(1, n, stride=2), :] = x


def kernel(
    nw, nz, f_hbm, k_hbm, l_hbm, out_ref,
    km, ks, fm, fs, lm, ls, dgm, dgs, dm, ds_, v1m, v1s, v2m, v2s,
    g1m, g1s, h1m, h1s, g2m, g2s, h2m, h2s, tm, ts,
    pack0, rs0, packv, rsv, kd1, kd1x, gg1, gg1x, pack1, rs1, pv1, rsv1, vv1, vv1x,
    k1l, k1, dg1, f1, va1, t1, p2c, p2s, r2c, r2s, k2, dg2, f2, l2, t2, t3, loc_sem, send_sem, recv_sem,
):
    w, z = lax.axis_index("wide"), lax.axis_index("narrow")

    def device(a, b):
        return (lax.rem(w + (a + nw), nw), lax.rem(z + (b + nz), nz))

    has_left, has_right = (z > 0).astype(jnp.int32), (z < nz - 1).astype(jnp.int32)

    def inside(step):
        return jnp.logical_and(w + step >= 0, w + step < nw).astype(jnp.int32)

    started = []
    count = [0]

    def send(src, dst, a, b):
        n = count[0]
        count[0] += 1
        copy = pltpu.make_async_remote_copy(
            src_ref=src, dst_ref=dst, send_sem=send_sem.at[n], recv_sem=recv_sem.at[n],
            device_id=device(a, b), device_id_type=MESH,
        )
        copy.start()
        started.append(copy)
        return copy

    barrier = pltpu.get_barrier_semaphore()
    for a, b in FAR:
        pl.semaphore_signal(barrier, inc=1, device_id=device(a, b), device_id_type=MESH)
    loads = []
    for n, (src, dst) in enumerate(((k_hbm, km.at[4:12]), (f_hbm, fm.at[2:10]), (l_hbm, lm.at[2:10]))):
        loads.append(pltpu.make_async_copy(src, dst, loc_sem.at[n]))
        loads[-1].start()

    lane = lanes()

    def pack_sides(ref, off):
        left, right = jnp.zeros((8, 128), F32), jnp.zeros((8, 128), F32)
        for x in range(8):
            for t in range(4):
                j = 4 * x + t
                r = rot(ref[x + off, 8 * t : 8 * t + 8, :], 4 * j, 1)
                left = jnp.where((lane >> 2) == j, r, left)
                right = jnp.where((lane >> 2) == (j - 1) % 32, r, right)
        return left, right

    def unpack_sides(rs, n, ref, depth, masked):
        for p in range(8 + 2 * depth):
            x = p - depth
            step = (x + 8) // 8
            for t in range(4):
                j = 4 * (x % 8) + t
                from_right = rot(rs[step, 0, n], -4 * j, 1)
                from_left = rot(rs[step, 1, n], -4 * j, 1)
                tile = jnp.where(lane < 64, from_right, from_left)
                if masked:
                    there = inside(step - 1)
                    keep = jnp.logical_or(lane < 4 * has_right * there, lane >= 128 - 4 * has_left * there)
                    tile = jnp.where(keep, tile, 0.0)
                ref[p, 8 * t : 8 * t + 8, :] = tile

    for n, (ref, off) in enumerate(((km, 4), (fm, 2), (lm, 2))):
        loads[n].wait()
        pack0[0, n], pack0[1, n] = pack_sides(ref, off)

    pl.semaphore_wait(barrier, len(FAR))

    def send_planes(src_lo, dst_hi, src_hi, dst_lo):
        return [send(src_hi, dst_lo, 1, 0), send(src_lo, dst_hi, -1, 0)]

    def send_sides(pack, rs):
        return [send(pack.at[0 if b < 0 else 1], rs.at[1 - a, 0 if b < 0 else 1], a, b) for a, b in SIDES]

    e0k = send_planes(km.at[4:8], km.at[12:16], km.at[8:12], km.at[0:4])
    e0s = send_sides(pack0, rs0)
    e0f = send_planes(fm.at[2:4], fm.at[10:12], fm.at[8:10], fm.at[0:2])
    e0l = send_planes(lm.at[2:4], lm.at[10:12], lm.at[8:10], lm.at[0:2])

    rm01, rs01 = ring_map(main_z, 96), ring_map(side_z, 96)
    r12, r23 = ring_map(cut(96), 64), ring_map(cut(64), 64)

    for c in e0k + e0s:
        c.wait_recv()
    low, high = inside(-1).astype(F32), inside(1).astype(F32)
    km[0:4] = km[0:4] * low
    km[12:16] = km[12:16] * high
    unpack_sides(rs0, 0, ks, 4, True)

    def k_parts(p, c):
        m, s = km[p], ks[p]
        pm, ps = zsum_pair(m, s)
        g1m[p], h1m[p] = planes_of(m, pm)
        g1s[p], h1s[p] = planes_of(s, ps)
        return c

    lax.fori_loop(1, 15, k_parts, 0)

    def k_pairs(i, c):
        tm[pl.ds(pl.multiple_of(32 * i, 32), 32), :] = km[2 * i] + km[2 * i + 1]
        ts[pl.ds(pl.multiple_of(32 * i, 32), 32), :] = ks[2 * i] + ks[2 * i + 1]
        return c

    lax.fori_loop(0, 8, k_pairs, 0)
    coarse = dot(halve_rows(tm, 128), rm01) + dot(halve_rows(ts, 128), rs01)
    k1l[...] = (0.125 * coarse).reshape(8, 16, 128)

    def l_pairs(i, c):
        tm[pl.ds(pl.multiple_of(32 * i, 32), 32), :] = lm[2 * i + 2] + lm[2 * i + 3]
        return c

    lax.fori_loop(0, 4, l_pairs, 0)
    l1 = (0.125 * dot(halve_rows(tm, 64), rm01)).reshape(4, 16, 128)
    own1 = k1l[2:6]
    half1 = 0.5 * 0.25
    diag1 = l1 + half1 * (CALL * own1 + ring_sum(k1l[1:7]))
    lane16 = iota((4, 16, 128), 2)
    kd1[...] = jnp.where(lane16 < 64, own1, rot(diag1, 64, 2))
    ekd = send_planes(kd1.at[0:3], kd1x.at[1], kd1.at[1:4], kd1x.at[0])

    kk = k1l[...]
    for i in range(4):
        t1[16 * i : 16 * i + 16, :] = kk[2 * i] + kk[2 * i + 1]
    k2l = (0.125 * dot(halve_rows(t1, 32), r12)).reshape(4, 8, 128)
    for i in range(2):
        t1[16 * i : 16 * i + 16, :] = l1[2 * i] + l1[2 * i + 1]
    l2own = (0.125 * dot(halve_rows(t1, 16), r12)).reshape(2, 8, 128)
    half2 = 0.5 * 0.0625
    diag2 = l2own + half2 * (CALL * k2l[1:3] + ring_sum(k2l))
    lane8 = iota((2, 8, 128), 2)
    p2c[...] = jnp.where(
        lane8 < 64, rot(l2own, 32, 2), jnp.where(lane8 < 96, rot(k2l[1:3], 64, 2), rot(diag2, 96, 2))
    )

    for c in e0f + e0l:
        c.wait_recv()
    unpack_sides(rs0, 1, fs, 2, False)
    unpack_sides(rs0, 2, ls, 2, False)

    def there0(q):
        return jnp.where(q < 2, inside(-1), jnp.where(q >= 10, inside(1), 1))

    lane32 = iota((32, 128), 1)

    def first(q, c):
        there = there0(q)
        total = g1m[q + 1] + g1m[q + 3] + h1m[q + 2]
        diag = lm[q] + 0.5 * (CALL * km[q + 2] + total)
        inv = jnp.where(lane32 < 128 * there, OMEGA / diag, 0.0)
        dgm[q], dm[q] = diag, inv
        v1m[q] = inv * fm[q]
        total = g1s[q + 1] + g1s[q + 3] + h1s[q + 2]
        diag = ls[q] + 0.5 * (CALL * ks[q + 2] + total)
        keep = jnp.logical_or(lane32 < 4 * has_right * there, lane32 >= 128 - 4 * has_left * there)
        inv = jnp.where(keep, OMEGA / diag, 0.0)
        dgs[q], ds_[q] = diag, inv
        v1s[q] = inv * fs[q]
        return c

    lax.fori_loop(0, 12, first, 0)

    def parts(vm, vs):
        def body(q, c):
            m, s = vm[q], vs[q]
            pm, ps = zsum_pair(m, s)
            g1m[q], h1m[q] = planes_of(m, pm)
            g1s[q], h1s[q] = planes_of(s, ps)
            m, s = m * km[q + 2], s * ks[q + 2]
            pm, ps = zsum_pair(m, s)
            g2m[q], h2m[q] = planes_of(m, pm)
            g2s[q], h2s[q] = planes_of(s, ps)
            return c

        return body

    def parts_main(vm, vs):
        def body(q, c):
            m, s = vm[q], vs[q]
            g1m[q], h1m[q] = planes_of(m, zsum_main(m, s))
            m, s = m * km[q + 2], s * ks[q + 2]
            g2m[q], h2m[q] = planes_of(m, zsum_main(m, s))
            return c

        return body

    def resid(q, vm, f, dg, k, g1, h1, g2, h2):
        s1 = g1[q - 1] + g1[q + 1] + h1[q]
        s2 = g2[q - 1] + g2[q + 1] + h2[q]
        return f[q] - dg[q] * vm[q] + 0.5 * (k[q + 2] * s1 + s2)

    def sweep(vm, vs, om, os):
        def body(q, c):
            om[q] = vm[q] + dm[q] * resid(q, vm, fm, dgm, km, g1m, h1m, g2m, h2m)
            os[q] = vs[q] + ds_[q] * resid(q, vs, fs, dgs, ks, g1s, h1s, g2s, h2s)
            return c

        return body

    lax.fori_loop(0, 12, parts(v1m, v1s), 0)
    lax.fori_loop(1, 11, sweep(v1m, v1s, v2m, v2s), 0)
    lax.fori_loop(1, 11, parts_main(v2m, v2s), 0)

    def resid_pairs(i, c):
        r = [resid(2 * i + 2 + n, v2m, fm, dgm, km, g1m, h1m, g2m, h2m) for n in (0, 1)]
        tm[pl.ds(pl.multiple_of(32 * i, 32), 32), :] = r[0] + r[1]
        return c

    lax.fori_loop(0, 4, resid_pairs, 0)
    gg1[...] = (0.125 * dot(halve_rows(tm, 64), rm01)).reshape(4, 16, 128)

    def pack_sides1(arrays):
        left, right = jnp.zeros((8, 128), F32), jnp.zeros((8, 128), F32)
        for n, arr in enumerate(arrays):
            for x in range(4):
                for t in range(2):
                    slot = 8 * n + 2 * x + t
                    tile = arr[x, 8 * t : 8 * t + 8, :]
                    hit = (lane >> 2) == slot
                    left = jnp.where(hit, rot(tile, 4 * slot, 1), left)
                    right = jnp.where(hit, rot(tile, 4 * slot - 60, 1), right)
        return left, right

    e1x = send_planes(gg1.at[0:2], gg1x.at[1], gg1.at[2:4], gg1x.at[0])
    pack1[0], pack1[1] = pack_sides1([own1, diag1, gg1[...]])
    e1s = send_sides(pack1, rs1)

    packv[0, 0], packv[1, 0] = pack_sides(v2m, 2)
    evx = [send(v2m.at[8], v2m.at[0], 1, 0), send(v2m.at[3], v2m.at[11], -1, 0)]
    evs = send_sides(packv, rsv)

    for c in ekd + e1x + e1s:
        c.wait_recv()

    def keep1(step):
        there = inside(step)
        return jnp.logical_or(lane < (64 + 4 * has_right) * there, lane >= 128 - 4 * has_left * there)

    def fill1(ref, depth, center, rs, n, masked):
        for p in range(4 + 2 * depth):
            x = p - depth
            step = (x + 4) // 4
            for t in range(2):
                slot = 8 * n + 2 * (x % 4) + t
                tile = jnp.where(
                    lane < 64,
                    center(x, slice(8 * t, 8 * t + 8)),
                    jnp.where(lane < 96, rot(rs[step, 0], 64 - 4 * slot, 1), rot(rs[step, 1], 124 - 4 * slot, 1)),
                )
                if masked:
                    tile = jnp.where(keep1(step - 1), tile, 0.0)
                ref[p, 8 * t : 8 * t + 8, :] = tile

    def pick(own, x_ref, depth, x, rows, shift=0):
        if x < 0:
            return rot(x_ref[0, x + depth, rows, :], shift, 1)
        if x > 3:
            return rot(x_ref[1, x - 4, rows, :], shift, 1)
        return rot(own[x, rows, :], shift, 1)

    fill1(k1, 3, lambda x, r: pick(kd1, kd1x, 3, x, r), rs1, 0, True)
    fill1(dg1, 2, lambda x, r: pick(kd1, kd1x, 3, x, r, 64), rs1, 1, False)
    fill1(f1, 2, lambda x, r: pick(gg1, gg1x, 2, x, r), rs1, 2, False)

    lane1 = iota((2, 16, 128), 2)

    def inverse1(lo, hi, step):
        there = inside(step)
        keep = jnp.logical_or(lane1 < (64 + 4 * has_right) * there, lane1 >= 128 - 4 * has_left * there)
        return jnp.where(keep, OMEGA / dg1[lo:hi], 0.0)

    def level1_inverse():
        return jnp.concatenate([inverse1(0, 2, -1), inverse1(2, 4, 0), inverse1(4, 6, 0), inverse1(6, 8, 1)], axis=0)

    def sweep1(v, depth, inv):
        kk = k1[3 - depth : 7 + depth]
        lo, hi = 3 - depth, 5 + depth
        rest = f1[lo:hi] - ring_apply(v, kk, dg1[lo:hi], half1)
        return v[1:-1] + inv[lo:hi] * rest

    inv1 = level1_inverse()
    v = sweep1(inv1 * f1[...], 2, inv1)
    r = f1[2:6] - ring_apply(v, k1[2:8], dg1[2:6], half1)
    for i in range(2):
        t1[16 * i : 16 * i + 16, :] = r[2 * i] + r[2 * i + 1]
    rhs2 = (0.125 * dot(halve_rows(t1, 16), r12)).reshape(2, 8, 128)

    whole = jnp.where(lane8 < 32, rhs2, p2c[...])
    p2c[...] = whole
    left, right = jnp.zeros((8, 128), F32), jnp.zeros((8, 128), F32)
    for n in range(4):
        for x in range(2):
            slot = 2 * n + x
            hit = (lane >> 3) == slot
            left = jnp.where(hit, rot(whole[x], 8 * slot - 32 * n, 1), left)
            right = jnp.where(hit, rot(whole[x], 8 * slot - 32 * n - 24, 1), right)
    p2s[0], p2s[1] = left, right
    e2 = []
    for a, b in FAR:
        if b == 0:
            e2.append(send(p2c, r2c.at[4 - a], a, b))
        else:
            side = 0 if b < 0 else 1
            e2.append(send(p2s.at[side], r2s.at[4 - a, side], a, b))

    vv1[...] = v[1:5]
    pv1[0], pv1[1] = pack_sides1([v[1:5]])
    ev1x = send_planes(vv1.at[0:3], vv1x.at[1], vv1.at[1:4], vv1x.at[0])
    ev1s = send_sides(pv1, rsv1)
    r2c[4] = whole

    for c in e2:
        c.wait_recv()

    for step in range(9):
        there = inside(step - 4)
        keep = jnp.logical_or(lane < (32 + 8 * has_right) * there, lane >= 128 - 8 * has_left * there)
        for x in range(2):
            mid = r2c[step, x]
            for n, ref in enumerate((f2, l2, k2, dg2)):
                slot = 2 * n + x
                tile = jnp.where(
                    lane < 32,
                    rot(mid, -32 * n, 1),
                    jnp.where(
                        lane < 64, rot(r2s[step, 0], 32 - 8 * slot, 1), rot(r2s[step, 1], 120 - 8 * slot, 1)
                    ),
                )
                if ref is k2:
                    tile = jnp.where(keep, tile, 0.0)
                elif ref is dg2:
                    t2[2 * step + x] = jnp.where(keep, OMEGA / tile, 0.0)
                ref[2 * step + x] = tile

    def sweep2(v, depth):
        lo, hi = 9 - depth, 9 + depth
        rest = f2[lo:hi] - ring_apply(v, k2[lo - 1 : hi + 1], dg2[lo:hi], half2)
        return v[1:-1] + t2[lo:hi] * rest

    vb = sweep2(t2[...] * f2[...], 8)
    r = f2[2:16] - ring_apply(vb, k2[1:17], dg2[2:16], half2)

    def to_level3(x, planes):
        for i in range(planes):
            t1[8 * i : 8 * i + 8, :] = x[2 * i] + x[2 * i + 1]
        y = 0.125 * dot(halve_rows(t1, 4 * planes), r23)
        for i in range(planes):
            t3[i, 0:4, :] = y[4 * i : 4 * i + 4, :]
        return t3[0:planes]

    t3[...] = jnp.zeros_like(t3)
    half3 = 0.5 * 0.015625
    k3 = to_level3(k2[...], 9)
    l3 = to_level3(l2[2:16], 7)
    f3 = to_level3(r, 7)
    diag3 = l3 + half3 * (CALL * k3[1:-1] + ring_sum(k3))
    row = iota((8, 128), 0)
    inv3 = []
    for i in range(7):
        there = inside(i - 3)
        keep = jnp.logical_or(lane < (16 + 4 * has_right) * there, lane >= 128 - 4 * has_left * there)
        inv3.append(jnp.where(jnp.logical_and(keep, row < 4), OMEGA / diag3[i], 0.0)[None])
    inv3 = jnp.concatenate(inv3, axis=0)
    v3 = inv3 * f3
    rest = f3[1:-1] - ring_apply(v3, k3[1:-1], diag3[1:-1], half3)
    v3 = v3[1:-1] + inv3[1:-1] * rest

    p32 = ring_map(cut(64), 64, True)
    wide3 = dot(v3.reshape(40, 128), p32)
    for i in range(5):
        double_rows(t1.at[8 * i : 8 * i + 8, :], wide3[8 * i : 8 * i + 4, :])
    e3 = t1[0:40, :].reshape(5, 8, 128)
    e3 = jnp.concatenate([e3[i // 2][None] for i in range(10)], axis=0)
    vb = vb[3:13] + e3
    vb = sweep2(vb, 4)
    vb = sweep2(vb, 3)

    for c in ev1x + ev1s:
        c.wait_recv()
    fill1(va1, 3, lambda x, r: pick(vv1, vv1x, 3, x, r), rsv1, 0, True)
    p21 = ring_map(cut(96), 64, True)
    double_rows(tm.at[0:96, :], dot(vb.reshape(48, 128), p21))
    e2v = tm[0:96, :].reshape(6, 16, 128)
    v = jnp.concatenate([va1[p : p + 1] + e2v[((p - 3) // 2 + 2) : ((p - 3) // 2 + 3)] for p in range(10)], axis=0)
    keep_planes = jnp.concatenate(
        [jnp.where(keep1((p + 1) // 4 - 1), 1.0, 0.0)[None] for p in range(10)], axis=0
    )
    v = v * jnp.concatenate([keep_planes, keep_planes], axis=1)
    v = sweep1(v, 3, inv1)
    v = sweep1(v, 2, inv1)

    e1 = v.reshape(96, 128)
    double_rows(tm.at[0:192, :], dot(e1, ring_map(main_z, 96, True)))
    double_rows(ts.at[0:192, :], dot(e1, ring_map(side_z, 96, True)))
    for c in evx + evs:
        c.wait()
    unpack_sides(rsv, 0, v2s, 2, True)

    def correct(q, c):
        there = there0(q)
        rows = pl.ds(pl.multiple_of(32 * (q // 2), 32), 32)
        v1m[q] = jnp.where(lane32 < 128 * there, v2m[q] + tm[rows, :], 0.0)
        keep = jnp.logical_or(lane32 < 4 * has_right * there, lane32 >= 128 - 4 * has_left * there)
        v1s[q] = jnp.where(keep, v2s[q] + ts[rows, :], 0.0)
        return c

    lax.fori_loop(0, 12, correct, 0)
    lax.fori_loop(0, 12, parts(v1m, v1s), 0)
    lax.fori_loop(1, 11, sweep(v1m, v1s, v2m, v2s), 0)
    lax.fori_loop(1, 11, parts_main(v2m, v2s), 0)

    def last(q, c):
        out_ref[q - 2] = v2m[q] + dm[q] * resid(q, v2m, fm, dgm, km, g1m, h1m, g2m, h2m)
        return c

    lax.fori_loop(2, 10, last, 0)
    for c in started:
        if not any(c is done for done in evx + evs):
            c.wait_send()


def solution(mesh):
    nw, nz = mesh.shape["wide"], mesh.shape["narrow"]

    def on_device(source, permeability, leakage):
        def vm(*shape):
            return pltpu.VMEM(shape, F32)

        p16, p12 = vm(16, 32, 128), vm(12, 32, 128)
        scratch = [p16, p16, p12, p12, p12, p12, p12, p12, p12, p12, p12, p12, p12, p12]
        scratch += [p16, p16, p16, p16, p12, p12, p12, p12, vm(256, 128), vm(256, 128)]
        scratch += [vm(2, 3, 8, 128), vm(3, 2, 3, 8, 128), vm(2, 1, 8, 128), vm(3, 2, 1, 8, 128)]
        scratch += [vm(4, 16, 128), vm(2, 3, 16, 128), vm(4, 16, 128), vm(2, 2, 16, 128)]
        scratch += [vm(2, 8, 128), vm(3, 2, 8, 128), vm(2, 8, 128), vm(3, 2, 8, 128)]
        scratch += [vm(4, 16, 128), vm(2, 3, 16, 128)]
        scratch += [vm(8, 16, 128), vm(10, 16, 128), vm(8, 16, 128), vm(8, 16, 128), vm(10, 16, 128), vm(128, 128)]
        scratch += [vm(2, 8, 128), vm(2, 8, 128), vm(9, 2, 8, 128), vm(9, 2, 8, 128)]
        scratch += [vm(18, 8, 128), vm(18, 8, 128), vm(18, 8, 128), vm(18, 8, 128), vm(18, 8, 128), vm(9, 8, 128)]
        n = 12 + 2 + 8 + 8 + 26 + 8
        scratch += [pltpu.SemaphoreType.DMA((3,)), pltpu.SemaphoreType.DMA((n,)), pltpu.SemaphoreType.DMA((n,))]

        def body(*refs):
            kernel(nw, nz, *refs)

        return pl.pallas_call(
            body,
            out_shape=jax.ShapeDtypeStruct(source.shape, F32),
            in_specs=[pl.BlockSpec(memory_space=pl.ANY)] * 3,
            out_specs=pl.BlockSpec(memory_space=pltpu.VMEM),
            scratch_shapes=scratch,
            compiler_params=pltpu.CompilerParams(
                collective_id=0, has_side_effects=True, vmem_limit_bytes=48 * 2**20
            ),
            name="vcycle",
        )(source, permeability, leakage)

    spec = P("wide", None, "narrow")
    return jax.shard_map(on_device, mesh=mesh, in_specs=(spec, spec, spec), out_specs=spec, check_vma=False)
```

time: 404 us -> 48.4 us (0.12)
  the two profiles are of different devices: /device:TPU:6 before, /device:TPU:1 now
where the time goes in v1:
time: 48.4 us; the launch traced here: 48.2 us
  Pallas kernels  44.8 us (93%)
  local copies, waits for them, and re-layouts  3.37 us (7%)
    pallas_call x1, Pallas kernels, on_device(): pl.pallas_call(body, out_shape=jax.ShapeDtypeStruct(source.shape, F32), i...  44.8 us
    unnamed x7, local copies, waits for them, and re-layouts  3.37 us

profile of v1, /device:TPU:1, one launch (start us, length us, event | category | flops | bytes accessed | tf_op | source)
XLA Modules:
  0.0 48.2 jit_solution(11040678098571766214)
XLA Ops:
  0.0 0.0 copy-start
  0.0 0.9 %copy-done = f32[8,32,128]{2,1,0:T(8,128)S(1)} copy-done((f32[8,32,128]{2,1,0:T(8,128)S(1)}, f32[8,32,128]{2,1,0:T(8,128)}, u32[]{:S(2)}) %copy-start) | copy-done | bytes 131096
  0.9 0.0 copy-start.1
  0.9 0.9 %copy-done.1 = f32[8,32,128]{2,1,0:T(8,128)S(1)} copy-done((f32[8,32,128]{2,1,0:T(8,128)S(1)}, f32[8,32,128]{2,1,0:T(8,128)}, u32[]{:S(2)}) %copy-start.1) | copy-done | bytes 131096
  1.8 0.0 copy-start.2
  1.8 0.9 %copy-done.2 = f32[8,32,128]{2,1,0:T(8,128)S(1)} copy-done((f32[8,32,128]{2,1,0:T(8,128)S(1)}, f32[8,32,128]{2,1,0:T(8,128)}, u32[]{:S(2)}) %copy-start.2) | copy-done | bytes 131096
  2.7 44.8 %vcycle.1 = f32[8,32,128]{2,1,0:T(8,128)S(1)} custom-call(f32[8,32,128]{2,1,0:T(8,128)S(1)} %copy-done, f32[8,32,128]{2,1,0:T(8,128)S(1)} %copy-done.1, f32[8,32,128]{2,1,0:T(8,128)S(1)} %copy-done.2), custom_call_target="tpu_custom_call" | custom-call | tf_op jit(solution)/shard_map/vcycle/pallas_call | solution.py:557
  47.5 0.7 %copy.5 = f32[8,32,128]{2,1,0:T(8,128)} copy(f32[8,32,128]{2,1,0:T(8,128)S(1)} %vcycle.1) | data formatting | bytes 262144
Async XLA Ops:
  0.0 0.9 %copy-start = (f32[8,32,128]{2,1,0:T(8,128)S(1)}, f32[8,32,128]{2,1,0:T(8,128)}, u32[]{:S(2)}) copy-start(f32[8,32,128]{2,1,0:T(8,128)} %refs_0_.1) | copy-start | bytes 393220
  0.9 0.9 %copy-start.1 = (f32[8,32,128]{2,1,0:T(8,128)S(1)}, f32[8,32,128]{2,1,0:T(8,128)}, u32[]{:S(2)}) copy-start(f32[8,32,128]{2,1,0:T(8,128)} %refs_1_.1) | copy-start | bytes 393220
  1.8 0.9 %copy-start.2 = (f32[8,32,128]{2,1,0:T(8,128)S(1)}, f32[8,32,128]{2,1,0:T(8,128)}, u32[]{:S(2)}) copy-start(f32[8,32,128]{2,1,0:T(8,128)} %refs_2_.1) | copy-start | bytes 393220

commit v2 on v1

v2 whole, which is shorter than its diff:
```python
import jax
import jax.numpy as jnp
from jax import lax
from jax.experimental import pallas as pl
from jax.experimental.pallas import tpu as pltpu
from jax.sharding import PartitionSpec as P

MESH = pl.DeviceIdType.MESH
OMEGA = 0.8
F32 = jnp.float32


def weight(a, b, c):
    n = a + b + c
    return (a * 1.0 + b * 0.7 + c * 0.4) / n * {1: 1.0, 2: 0.25, 3: 0.1}[n]


CX, CY, CZ = weight(1, 0, 0), weight(0, 1, 0), weight(0, 0, 1)
CXY, CXZ, CYZ, CXYZ = weight(1, 1, 0), weight(1, 0, 1), weight(0, 1, 1), weight(1, 1, 1)
CALL = 2 * (CX + CY + CZ) + 4 * (CXY + CXZ + CYZ) + 8 * CXYZ

SIDES = [(a, b) for b in (-1, 1) for a in (-1, 0, 1)]
FAR = [(a, b) for a in range(-4, 5) for b in (-1, 0, 1) if (a, b) != (0, 0)]


def iota(shape, dim):
    return lax.broadcasted_iota(jnp.int32, shape, dim)


def lanes():
    return iota((8, 128), 1)


def rot(x, shift, axis):
    shift %= x.shape[axis]
    return x if shift == 0 else pltpu.roll(x, shift, axis)


def rows_beside(t):
    axis = t.ndim - 2
    n = t.shape[axis]
    row = iota(t.shape, axis)
    up = jnp.where(row == 0, 0.0, rot(t, 1, axis))
    down = jnp.where(row == n - 1, 0.0, rot(t, n - 1, axis))
    return up + down


def planes_of(u, pz):
    g = CX * u + CXZ * pz + rows_beside(CXY * u + CXYZ * pz)
    h = CZ * pz + rows_beside(CY * u + CYZ * pz)
    return g, h


def neighbours(u, p, y):
    x, xp = u[0] + u[2], p[0] + p[2]
    inner = CXY * x + CXYZ * xp + CY * u[1] + CYZ * p[1]
    return CX * x + CXZ * xp + CZ * p[1] + y(inner)


def lanes_main(m, s):
    lane = iota(m.shape, 1)
    below = jnp.concatenate([rot(s, 105 - 32 * t, 1) for t in range(4)], axis=0)
    above = jnp.concatenate([rot(s, 119 - 32 * t, 1) for t in range(4)], axis=0)
    return jnp.where(lane == 0, below, rot(m, 1, 1)) + jnp.where(lane == 127, above, rot(m, 127, 1))


def lanes_strip(s):
    return rot(s, 1, 1) + rot(s, 127, 1)


def rows_strip(c):
    row, lane = iota((8, 128), 0), iota((8, 128), 1)
    up, down = rot(c, 1, 0), rot(c, 7, 0)
    up = jnp.where(row == 0, jnp.where(lane < 32, 0.0, rot(up, 32, 1)), up)
    down = jnp.where(row == 7, jnp.where(lane >= 96, 0.0, rot(down, 96, 1)), down)
    return up + down


def ring_sum(u):
    pz = rot(u, 1, 2) + rot(u, 127, 2)
    g, h = planes_of(u, pz)
    return g[:-2] + g[2:] + h[1:-1]


def ring_apply(v, k, diag, half):
    return diag * v[1:-1] - half * (k[1:-1] * ring_sum(v) + ring_sum(k * v))


def dot(a, b):
    return lax.dot_general(a, b, (((1,), (0,)), ((), ())), precision=lax.Precision.HIGHEST, preferred_element_type=F32)


def ring_map(fine_of, coarse_cut, transpose=False):
    f_dim = 1 if transpose else 0
    i, j = iota((128, 128), f_dim), iota((128, 128), 1 - f_dim)
    return ((fine_of(i) >> 1) == jnp.where(j < coarse_cut, j, j - 128)).astype(F32)


def cut(c):
    return lambda i: jnp.where(i < c, i, i - 128)


def main_z(i):
    return i


def strip_z(i):
    r = i & 31
    return jnp.where(r < 16, r + 120, r - 24)


def strip_halo_z(i):
    r = i & 31
    return jnp.where(jnp.logical_or(r < 8, r >= 24), 4096, strip_z(i))


def halve_rows(ref, n):
    return ref[pl.ds(0, n, stride=2), :] + ref[pl.ds(1, n, stride=2), :]


def double_rows(ref, x):
    n = x.shape[0]
    ref[pl.ds(0, n, stride=2), :] = x
    ref[pl.ds(1, n, stride=2), :] = x


def kernel(
    nw, nz, f_hbm, k_hbm, l_hbm, out_ref,
    km, ks, pkm, pks, fm, fs, lm, ls, dgm, dgs, dm, ds_,
    avm, avs, apm, aps, aqm, aqs, arm, ars, bvm, bvs, bpm, bps, bqm, bqs, brm, brs, tm, ts,
    pack0, rs0, packv, rsv, kd1, kd1x, gg1, gg1x, pack1, rs1, pv1, rsv1, vv1, vv1x,
    k1l, k1, dg1, f1, va1, t1, kd2, kd2x, gl2, gl2x, k2, dg2, f2, l2, t2, t3, loc_sem, send_sem, recv_sem,
):
    w, z = lax.axis_index("wide"), lax.axis_index("narrow")

    def device(a, b):
        return (lax.rem(w + (a + nw), nw), lax.rem(z + (b + nz), nz))

    def in_grid(a, b):
        ok = jnp.logical_and(w + a >= 0, w + a < nw)
        return ok if b == 0 else jnp.logical_and(ok, jnp.logical_and(z + b >= 0, z + b < nz))

    has_left, has_right = (z > 0).astype(jnp.int32), (z < nz - 1).astype(jnp.int32)

    def inside(step):
        return jnp.logical_and(w + step >= 0, w + step < nw).astype(jnp.int32)

    class Message:
        def __init__(self, n, src, dst, a, b):
            self.to, self.origin = (a, b), (-a, -b)
            self.copy = pltpu.make_async_remote_copy(
                src_ref=src, dst_ref=dst, send_sem=send_sem.at[n], recv_sem=recv_sem.at[n],
                device_id=device(a, b), device_id_type=MESH,
            )
            pl.when(in_grid(*self.to))(self.copy.start)

        def arrived(self):
            pl.when(in_grid(*self.origin))(self.copy.wait_recv)

        def left(self):
            pl.when(in_grid(*self.to))(self.copy.wait_send)

    started = []

    def send(src, dst, a, b):
        started.append(Message(len(started), src, dst, a, b))
        return started[-1]

    lane, row = lanes(), iota((8, 128), 0)
    group, place = lane >> 5, lane & 31

    for ref in (rs0, rsv, rs1, rsv1, kd1x, gg1x, vv1x, kd2x, gl2x):
        ref[...] = jnp.zeros_like(ref)

    def clear(k_planes, planes, v_plane):
        def body():
            km[k_planes] = jnp.zeros((4, 32, 128), F32)
            fm[planes] = jnp.zeros((2, 32, 128), F32)
            lm[planes] = jnp.zeros((2, 32, 128), F32)
            bvm[v_plane] = jnp.zeros((32, 128), F32)

        return body

    pl.when(w == 0)(clear(slice(0, 4), slice(0, 2), 0))
    pl.when(w == nw - 1)(clear(slice(12, 16), slice(10, 12), 11))

    barrier = pltpu.get_barrier_semaphore()

    def greet(a, b):
        def body():
            pl.semaphore_signal(barrier, inc=1, device_id=device(a, b), device_id_type=MESH)

        return body

    for a, b in FAR:
        pl.when(in_grid(a, b))(greet(a, b))
    loads = []
    for n, (src, dst) in enumerate(((k_hbm, km.at[4:12]), (f_hbm, fm.at[2:10]), (l_hbm, lm.at[2:10]))):
        loads.append(pltpu.make_async_copy(src, dst, loc_sem.at[n]))
        loads[-1].start()

    def own_strip(m):
        out = None
        for t in range(4):
            tile = m[8 * t : 8 * t + 8, :]
            part = jnp.where(place < 16, rot(tile, 32 * t + 8, 1), rot(tile, 32 * t + 24, 1))
            out = part if out is None else jnp.where(group == t, part, out)
        return out

    def pack_strips(strips):
        left, right = jnp.zeros((8, 128), F32), jnp.zeros((8, 128), F32)
        for x, s in enumerate(strips):
            hit = (place >> 2) == x
            left = jnp.where(hit, rot(s, 4 * x - 24, 1), left)
            right = jnp.where(hit, rot(s, 4 * x - 4, 1), right)
        return left, right

    def whole_strip(own, rs, n, x):
        step, at = (x + 8) // 8, x % 8
        halo = jnp.where(place < 16, rot(rs[step, 0, n], 8 - 4 * at, 1), rot(rs[step, 1, n], 20 - 4 * at, 1))
        halo = jnp.where(jnp.logical_or(place < 12, place >= 20), halo, 0.0)
        return jnp.where(jnp.logical_or(place < 8, place >= 24), own, halo)

    for n, (ref, strip, off) in enumerate(((km, ks, 4), (fm, fs, 2), (lm, ls, 2))):
        loads[n].wait()
        own = [own_strip(ref[x + off]) for x in range(8)]
        for x in range(8):
            strip[x + off] = own[x]
        pack0[0, n], pack0[1, n] = pack_strips(own)

    def count(pos, reach, size):
        return jnp.minimum(pos, reach) + 1 + jnp.minimum(size - 1 - pos, reach)

    pl.semaphore_wait(barrier, count(w, 4, nw) * count(z, 1, nz) - 1)

    def send_planes(src_lo, dst_hi, src_hi, dst_lo):
        return [send(src_hi, dst_lo, 1, 0), send(src_lo, dst_hi, -1, 0)]

    def send_sides(pack, rs):
        return [send(pack.at[0 if b < 0 else 1], rs.at[1 - a, 0 if b < 0 else 1], a, b) for a, b in SIDES]

    def send_far(src, dst):
        return [send(src, dst.at[4 - a, 1 - b], a, b) for a, b in FAR]

    e0k = send_planes(km.at[4:8], km.at[12:16], km.at[8:12], km.at[0:4])
    e0s = send_sides(pack0, rs0)
    e0f = send_planes(fm.at[2:4], fm.at[10:12], fm.at[8:10], fm.at[0:2])
    e0l = send_planes(lm.at[2:4], lm.at[10:12], lm.at[8:10], lm.at[0:2])

    rm01, rs01 = ring_map(main_z, 96), ring_map(strip_halo_z, 96)
    r12, r23 = ring_map(cut(96), 64), ring_map(cut(64), 64)

    for c in e0k + e0s:
        c.arrived()
    for p in range(16):
        own = ks[p] if 4 <= p < 12 else own_strip(km[p])
        ks[p] = whole_strip(own, rs0, 0, p - 4)

    def k_lanes(i, c):
        for p in (2 * i, 2 * i + 1):
            m, s = km[p], ks[p]
            pkm[p], pks[p] = lanes_main(m, s), lanes_strip(s)
        tm[pl.ds(pl.multiple_of(32 * i, 32), 32), :] = km[2 * i] + km[2 * i + 1]
        pair = ks[2 * i] + ks[2 * i + 1]
        parts = [jnp.where(group == t, pair, 0.0) for t in range(4)]
        ts[pl.ds(pl.multiple_of(32 * i, 32), 32), :] = jnp.concatenate(parts, axis=0)
        return c

    lax.fori_loop(0, 8, k_lanes, 0)

    coarse = dot(halve_rows(tm, 128), rm01) + dot(halve_rows(ts, 128), rs01)
    k1l[...] = (0.125 * coarse).reshape(8, 16, 128)

    def l_pairs(i, c):
        tm[pl.ds(pl.multiple_of(32 * i, 32), 32), :] = lm[2 * i + 2] + lm[2 * i + 3]
        return c

    lax.fori_loop(0, 4, l_pairs, 0)
    l1 = (0.125 * dot(halve_rows(tm, 64), rm01)).reshape(4, 16, 128)
    own1 = k1l[2:6]
    half1 = 0.5 * 0.25
    diag1 = l1 + half1 * (CALL * own1 + ring_sum(k1l[1:7]))
    lane16 = iota((4, 16, 128), 2)
    kd1[...] = jnp.where(lane16 < 64, own1, rot(diag1, 64, 2))
    ekd = send_planes(kd1.at[0:3], kd1x.at[1], kd1.at[1:4], kd1x.at[0])

    for c in e0f + e0l:
        c.arrived()
    for n, (ref, strip) in ((1, (fm, fs)), (2, (lm, ls))):
        for p in range(12):
            own = strip[p] if 2 <= p < 10 else own_strip(ref[p])
            strip[p] = whole_strip(own, rs0, n, p - 2)

    lane32 = iota((32, 128), 1)

    def three(ref, i):
        return ref[i - 1], ref[i], ref[i + 1]

    def ready(v, i, m, s, strips):
        vm, vs, pm, ps, qm, qs, rm, rs = v
        vm[i], vs[i] = m, s
        pm[i] = lanes_main(m, s)
        m, s = m * km[i + 2], s * ks[i + 2]
        qm[i], rm[i] = m, lanes_main(m, s)
        if strips:
            ps[i] = lanes_strip(vs[i])
            qs[i], rs[i] = s, lanes_strip(s)

    field_a = (avm, avs, apm, aps, aqm, aqs, arm, ars)
    field_b = (bvm, bvs, bpm, bps, bqm, bqs, brm, brs)

    def resid_main(v, i):
        vm, vs, pm, ps, qm, qs, rm, rs = v
        s1 = neighbours(three(vm, i), three(pm, i), rows_beside)
        s2 = neighbours(three(qm, i), three(rm, i), rows_beside)
        return fm[i] - dgm[i] * vm[i] + 0.5 * (km[i + 2] * s1 + s2)

    def resid_strip(v, i):
        vm, vs, pm, ps, qm, qs, rm, rs = v
        s1 = neighbours(three(vs, i), three(ps, i), rows_strip)
        s2 = neighbours(three(qs, i), three(rs, i), rows_strip)
        return fs[i] - dgs[i] * vs[i] + 0.5 * (ks[i + 2] * s1 + s2)

    def loop(lo, hi, step, body):
        def go(n, c):
            for i in range(step):
                body(lo + step * n + i)
            return c

        lax.fori_loop(0, (hi - lo) // step, go, 0)

    def first(i):
        there = jnp.where(i < 2, inside(-1), jnp.where(i >= 10, inside(1), 1))
        around = neighbours(three(km, i + 2), three(pkm, i + 2), rows_beside)
        diag = lm[i] + 0.5 * (CALL * km[i + 2] + around)
        inv = jnp.where(lane32 < 128 * there, OMEGA / diag, 0.0)
        dgm[i], dm[i] = diag, inv
        m = inv * fm[i]
        around = neighbours(three(ks, i + 2), three(pks, i + 2), rows_strip)
        diag = ls[i] + 0.5 * (CALL * ks[i + 2] + around)
        keep = jnp.logical_or(place < (8 + 4 * has_right) * there, place >= 32 - (8 + 4 * has_left) * there)
        inv = jnp.where(keep, OMEGA / diag, 0.0)
        dgs[i], ds_[i] = diag, inv
        ready(field_a, i, m, inv * fs[i], True)

    loop(0, 12, 2, first)

    def sweep(i):
        m = avm[i] + dm[i] * resid_main(field_a, i)
        s = avs[i] + ds_[i] * resid_strip(field_a, i)
        ready(field_b, i, m, s, False)

    loop(1, 11, 2, sweep)

    def resid_pairs(i, c):
        pair = resid_main(field_b, 2 * i + 2) + resid_main(field_b, 2 * i + 3)
        tm[pl.ds(pl.multiple_of(32 * i, 32), 32), :] = pair
        return c

    lax.fori_loop(0, 4, resid_pairs, 0)
    gg1[...] = (0.125 * dot(halve_rows(tm, 64), rm01)).reshape(4, 16, 128)

    def pack_sides1(arrays):
        left, right = jnp.zeros((8, 128), F32), jnp.zeros((8, 128), F32)
        for n, arr in enumerate(arrays):
            for x in range(4):
                for t in range(2):
                    slot = 8 * n + 2 * x + t
                    tile = arr[x, 8 * t : 8 * t + 8, :]
                    hit = (lane >> 2) == slot
                    left = jnp.where(hit, rot(tile, 4 * slot, 1), left)
                    right = jnp.where(hit, rot(tile, 4 * slot - 60, 1), right)
        return left, right

    e1x = send_planes(gg1.at[0:2], gg1x.at[1], gg1.at[2:4], gg1x.at[0])
    pack1[0], pack1[1] = pack_sides1([own1, diag1, gg1[...]])
    e1s = send_sides(pack1, rs1)

    kk = k1l[...]
    for i in range(4):
        t1[16 * i : 16 * i + 16, :] = kk[2 * i] + kk[2 * i + 1]
    k2l = (0.125 * dot(halve_rows(t1, 32), r12)).reshape(4, 8, 128)
    for i in range(2):
        t1[16 * i : 16 * i + 16, :] = l1[2 * i] + l1[2 * i + 1]
    l2own = (0.125 * dot(halve_rows(t1, 16), r12)).reshape(2, 8, 128)
    half2 = 0.5 * 0.0625
    diag2 = l2own + half2 * (CALL * k2l[1:3] + ring_sum(k2l))
    both = (k2l[1], k2l[2], diag2[0], diag2[1])
    low = jnp.where(lane < 32, both[0], rot(both[1], 32, 1))
    high = jnp.where(lane < 96, rot(both[2], 64, 1), rot(both[3], 96, 1))
    kd2[...] = jnp.where(lane < 64, low, high)
    l2sum = rot(l2own[0] + l2own[1], 64, 1)
    ekd2 = send_far(kd2, kd2x)

    packv[0, 0], packv[1, 0] = pack_strips([bvs[x + 2] for x in range(8)])
    evx = [send(bvm.at[8], bvm.at[0], 1, 0), send(bvm.at[3], bvm.at[11], -1, 0)]
    evs = send_sides(packv, rsv)

    def fill1(ref, depth, center, rs, n):
        for p in range(4 + 2 * depth):
            x = p - depth
            step = (x + 4) // 4
            for t in range(2):
                slot = 8 * n + 2 * (x % 4) + t
                beside = jnp.where(lane < 96, rot(rs[step, 0], 64 - 4 * slot, 1), rot(rs[step, 1], 124 - 4 * slot, 1))
                beside = jnp.where(jnp.logical_or(lane < 68, lane >= 124), beside, 0.0)
                ref[p, 8 * t : 8 * t + 8, :] = jnp.where(lane < 64, center(x, slice(8 * t, 8 * t + 8)), beside)

    def pick(own, x_ref, depth, x, rows, shift=0):
        if x < 0:
            return rot(x_ref[0, x + depth, rows, :], shift, 1)
        if x > 3:
            return rot(x_ref[1, x - 4, rows, :], shift, 1)
        return rot(own[x, rows, :], shift, 1)

    for c in ekd + e1x + e1s:
        c.arrived()
    fill1(k1, 3, lambda x, r: pick(kd1, kd1x, 3, x, r), rs1, 0)
    fill1(dg1, 2, lambda x, r: pick(kd1, kd1x, 3, x, r, 64), rs1, 1)
    fill1(f1, 2, lambda x, r: pick(gg1, gg1x, 2, x, r), rs1, 2)

    lane1 = iota((2, 16, 128), 2)

    def inverse1(lo, hi, step):
        there = inside(step)
        keep = jnp.logical_or(lane1 < (64 + 4 * has_right) * there, lane1 >= 128 - 4 * has_left * there)
        return jnp.where(keep, OMEGA / dg1[lo:hi], 0.0)

    def sweep1(v, depth, inv):
        kk = k1[3 - depth : 7 + depth]
        lo, hi = 3 - depth, 5 + depth
        rest = f1[lo:hi] - ring_apply(v, kk, dg1[lo:hi], half1)
        return v[1:-1] + inv[lo:hi] * rest

    inv1 = jnp.concatenate([inverse1(0, 2, -1), inverse1(2, 4, 0), inverse1(4, 6, 0), inverse1(6, 8, 1)], axis=0)
    v = sweep1(inv1 * f1[...], 2, inv1)
    r = f1[2:6] - ring_apply(v, k1[2:8], dg1[2:6], half1)
    for i in range(2):
        t1[16 * i : 16 * i + 16, :] = r[2 * i] + r[2 * i + 1]
    rhs2 = (0.125 * dot(halve_rows(t1, 16), r12)).reshape(2, 8, 128)

    gl2[...] = jnp.where(lane < 32, rhs2[0], jnp.where(lane < 64, rot(rhs2[1], 32, 1), l2sum))
    e2 = send_far(gl2, gl2x)
    vv1[...] = v[1:5]
    pv1[0], pv1[1] = pack_sides1([v[1:5]])
    ev1x = send_planes(vv1.at[0:3], vv1x.at[1], vv1.at[1:4], vv1x.at[0])
    ev1s = send_sides(pv1, rsv1)

    def near2(own, ref, step, n):
        mid = own if step == 4 else ref[step, 1]
        beside = jnp.where(lane < 64, rot(ref[step, 2], 32 - 32 * n, 1), rot(ref[step, 0], 96 - 32 * n, 1))
        beside = jnp.where(jnp.logical_or(lane < 40, lane >= 120), beside, 0.0)
        return jnp.where(lane < 32, rot(mid, -32 * n, 1), beside)

    for c in ekd2:
        c.arrived()
    mine = kd2[...]
    for step in range(9):
        there = inside(step - 4)
        keep = jnp.logical_or(lane < (32 + 8 * has_right) * there, lane >= 128 - 8 * has_left * there)
        for x in range(2):
            k2[2 * step + x] = near2(mine, kd2x, step, x)
            diag = near2(mine, kd2x, step, 2 + x)
            dg2[2 * step + x] = diag
            t2[2 * step + x] = jnp.where(keep, OMEGA / diag, 0.0)

    def to_level3(pairs):
        n = len(pairs)
        for i, pair in enumerate(pairs):
            t1[8 * i : 8 * i + 8, :] = pair
        y = 0.125 * dot(halve_rows(t1, 4 * n), r23)
        for i in range(n):
            t3[i, 0:4, :] = y[4 * i : 4 * i + 4, :]
        return t3[0:n]

    t3[...] = jnp.zeros_like(t3)
    half3 = 0.5 * 0.015625
    k3 = to_level3([k2[2 * i] + k2[2 * i + 1] for i in range(9)])
    most3 = half3 * (CALL * k3[1:-1] + ring_sum(k3))

    for c in e2:
        c.arrived()
    mine = gl2[...]
    for step in range(9):
        for x in range(2):
            f2[2 * step + x] = near2(mine, gl2x, step, x)
        l2[step] = near2(mine, gl2x, step, 2)

    def sweep2(v, depth):
        lo, hi = 9 - depth, 9 + depth
        rest = f2[lo:hi] - ring_apply(v, k2[lo - 1 : hi + 1], dg2[lo:hi], half2)
        return v[1:-1] + t2[lo:hi] * rest

    vb = sweep2(t2[...] * f2[...], 8)
    r = f2[2:16] - ring_apply(vb, k2[1:17], dg2[2:16], half2)
    l3 = to_level3([l2[i + 1] for i in range(7)])
    f3 = to_level3([r[2 * i] + r[2 * i + 1] for i in range(7)])
    diag3 = l3 + most3
    inv3 = []
    for i in range(7):
        there = inside(i - 3)
        keep = jnp.logical_or(lane < (16 + 4 * has_right) * there, lane >= 128 - 4 * has_left * there)
        inv3.append(jnp.where(jnp.logical_and(keep, row < 4), OMEGA / diag3[i], 0.0)[None])
    inv3 = jnp.concatenate(inv3, axis=0)
    v3 = inv3 * f3
    rest = f3[1:-1] - ring_apply(v3, k3[1:-1], diag3[1:-1], half3)
    v3 = v3[1:-1] + inv3[1:-1] * rest

    p32 = ring_map(cut(64), 64, True)
    wide3 = dot(v3.reshape(40, 128), p32)
    for i in range(5):
        double_rows(t1.at[8 * i : 8 * i + 8, :], wide3[8 * i : 8 * i + 4, :])
    e3 = t1[0:40, :].reshape(5, 8, 128)
    e3 = jnp.concatenate([e3[i // 2][None] for i in range(10)], axis=0)
    vb = vb[3:13] + e3
    vb = sweep2(vb, 4)
    vb = sweep2(vb, 3)

    for c in ev1x + ev1s:
        c.arrived()
    fill1(va1, 3, lambda x, r: pick(vv1, vv1x, 3, x, r), rsv1, 0)
    p21 = ring_map(cut(96), 64, True)
    double_rows(tm.at[0:96, :], dot(vb.reshape(48, 128), p21))
    e2v = tm[0:96, :].reshape(6, 16, 128)
    inner = jnp.logical_or(lane < 68, lane >= 124)
    inner = jnp.concatenate([inner, inner], axis=0)
    v = [jnp.where(inner, va1[p] + e2v[(p - 3) // 2 + 2], 0.0)[None] for p in range(10)]
    v = sweep1(jnp.concatenate(v, axis=0), 3, inv1)
    v = sweep1(v, 2, inv1)

    e1 = v.reshape(96, 128)
    double_rows(tm.at[0:192, :], dot(e1, ring_map(main_z, 96, True)))
    double_rows(ts.at[0:192, :], dot(e1, ring_map(strip_z, 96, True)))
    for c in evx + evs:
        c.arrived()
        c.left()
    for p in range(12):
        own = bvs[p] if 1 <= p < 11 else own_strip(bvm[p])
        bvs[p] = whole_strip(own, rsv, 0, p - 2)

    def correct(i):
        at = 32 * (i // 2)
        m = bvm[i] + tm[pl.ds(pl.multiple_of(at, 32), 32), :]
        s = ts[pl.ds(pl.multiple_of(at, 8), 8), :]
        for t in range(1, 4):
            s = jnp.where(group == t, ts[pl.ds(pl.multiple_of(at + 8 * t, 8), 8), :], s)
        s = jnp.where(jnp.logical_or(place < 12, place >= 20), bvs[i] + s, 0.0)
        ready(field_a, i, m, s, True)

    loop(0, 12, 2, correct)
    loop(1, 11, 2, sweep)

    def last(i):
        out_ref[i - 2] = bvm[i] + dm[i] * resid_main(field_b, i)

    loop(2, 10, 2, last)
    for c in started:
        if not any(c is done for done in evx + evs):
            c.left()


def solution(mesh):
    nw, nz = mesh.shape["wide"], mesh.shape["narrow"]

    def on_device(source, permeability, leakage):
        def vm(*shape):
            return pltpu.VMEM(shape, F32)

        def pair(n):
            return [vm(n, 32, 128), vm(n, 8, 128)]

        scratch = pair(16) * 2 + pair(12) * 4 + pair(12) * 8 + [vm(256, 128), vm(256, 128)]
        scratch += [vm(2, 3, 8, 128), vm(3, 2, 3, 8, 128), vm(2, 1, 8, 128), vm(3, 2, 1, 8, 128)]
        scratch += [vm(4, 16, 128), vm(2, 3, 16, 128), vm(4, 16, 128), vm(2, 2, 16, 128)]
        scratch += [vm(2, 8, 128), vm(3, 2, 8, 128), vm(2, 8, 128), vm(3, 2, 8, 128)]
        scratch += [vm(4, 16, 128), vm(2, 3, 16, 128)]
        scratch += [vm(8, 16, 128), vm(10, 16, 128), vm(8, 16, 128), vm(8, 16, 128), vm(10, 16, 128), vm(128, 128)]
        scratch += [vm(8, 128), vm(9, 3, 8, 128), vm(8, 128), vm(9, 3, 8, 128)]
        scratch += [vm(18, 8, 128), vm(18, 8, 128), vm(18, 8, 128), vm(9, 8, 128), vm(18, 8, 128), vm(9, 8, 128)]
        n = 12 + 2 + 8 + 26 + 8 + 26 + 8
        scratch += [pltpu.SemaphoreType.DMA((3,)), pltpu.SemaphoreType.DMA((n,)), pltpu.SemaphoreType.DMA((n,))]

        def body(*refs):
            kernel(nw, nz, *refs)

        return pl.pallas_call(
            body,
            out_shape=jax.ShapeDtypeStruct(source.shape, F32),
            in_specs=[pl.BlockSpec(memory_space=pltpu.HBM)] * 3,
            out_specs=pl.BlockSpec(memory_space=pltpu.VMEM),
            scratch_shapes=scratch,
            compiler_params=pltpu.CompilerParams(
                collective_id=0, has_side_effects=True, vmem_limit_bytes=60 * 2**20
            ),
            name="vcycle",
        )(source, permeability, leakage)

    spec = P("wide", None, "narrow")
    return jax.shard_map(on_device, mesh=mesh, in_specs=(spec, spec, spec), out_specs=spec, check_vma=False)
```

time: 48.4 us -> 38.2 us (0.79)
  the two profiles are of different devices: /device:TPU:1 before, /device:TPU:15 now
where the time goes in v2:
time: 38.2 us; the launch traced here: 38 us
  Pallas kernels  36.4 us (95%)
  local copies, waits for them, and re-layouts  1.57 us (4%)
    pallas_call x1, Pallas kernels, on_device(): pl.pallas_call(body, out_shape=jax.ShapeDtypeStruct(source.shape, F32), i...  36.4 us
    unnamed x1, local copies, waits for them, and re-layouts  1.57 us

profile of v2, /device:TPU:15, one launch (start us, length us, event | category | flops | bytes accessed | tf_op | source)
XLA Modules:
  0.0 38.0 jit_solution(18294972332034495838)
XLA Ops:
  0.0 36.4 %vcycle.1 = f32[8,32,128]{2,1,0:T(8,128)} custom-call(f32[8,32,128]{2,1,0:T(8,128)} %refs_0_.1, f32[8,32,128]{2,1,0:T(8,128)} %refs_1_.1, f32[8,32,128]{2,1,0:T(8,128)} %refs_2_.1), custom_call_target="tpu_custom_call" | custom-call | tf_op jit(solution)/shard_map/vcycle/pallas_call | solution.py:586
  36.5 1.6 %copy.5 = f32[8,32,128]{2,1,0:T(8,128)} copy(f32[8,32,128]{2,1,0:T(8,128)} %vcycle.1) | data formatting | bytes 262144

commit v3 on v2

--- a/solution.py
+++ b/solution.py
@@ -45,27 +45,21 @@
     return up + down
 
 
-def planes_of(u, pz):
-    g = CX * u + CXZ * pz + rows_beside(CXY * u + CXYZ * pz)
-    h = CZ * pz + rows_beside(CY * u + CYZ * pz)
-    return g, h
-
-
 def neighbours(u, p, y):
     x, xp = u[0] + u[2], p[0] + p[2]
     inner = CXY * x + CXYZ * xp + CY * u[1] + CYZ * p[1]
     return CX * x + CXZ * xp + CZ * p[1] + y(inner)
 
 
-def lanes_main(m, s):
+def beside_main(m, s):
     lane = iota(m.shape, 1)
-    below = jnp.concatenate([rot(s, 105 - 32 * t, 1) for t in range(4)], axis=0)
-    above = jnp.concatenate([rot(s, 119 - 32 * t, 1) for t in range(4)], axis=0)
-    return jnp.where(lane == 0, below, rot(m, 1, 1)) + jnp.where(lane == 127, above, rot(m, 127, 1))
-
-
-def lanes_strip(s):
-    return rot(s, 1, 1) + rot(s, 127, 1)
+    edge = jnp.where((iota(s.shape, 1) & 31) < 7, s, rot(s, -18, 1))
+    edge = jnp.concatenate([rot(edge, 121 - 32 * t, 1) for t in range(4)], axis=0)
+    return jnp.where(lane == 0, edge, rot(m, 1, 1)), jnp.where(lane == 127, edge, rot(m, 127, 1))
+
+
+def beside(u, axis=1):
+    return rot(u, 1, axis), rot(u, 127, axis)
 
 
 def rows_strip(c):
@@ -76,14 +70,25 @@
     return up + down
 
 
+def slabs(u):
+    return u[:-2], u[1:-1], u[2:]
+
+
 def ring_sum(u):
-    pz = rot(u, 1, 2) + rot(u, 127, 2)
-    g, h = planes_of(u, pz)
-    return g[:-2] + g[2:] + h[1:-1]
+    below, above = beside(u, 2)
+    return neighbours(slabs(u), slabs(below + above), rows_beside)
 
 
 def ring_apply(v, k, diag, half):
-    return diag * v[1:-1] - half * (k[1:-1] * ring_sum(v) + ring_sum(k * v))
+    k, k_below, k_above = k
+    below, above = beside(v, 2)
+    s1 = neighbours(slabs(v), slabs(below + above), rows_beside)
+    s2 = neighbours(slabs(k * v), slabs(k_below * below + k_above * above), rows_beside)
+    return diag * v[1:-1] - half * (k[1:-1] * s1 + s2)
+
+
+def cut_planes(k, lo, hi):
+    return tuple(part[lo:hi] for part in k)
 
 
 def dot(a, b):
@@ -106,12 +111,12 @@
 
 def strip_z(i):
     r = i & 31
-    return jnp.where(r < 16, r + 120, r - 24)
+    return jnp.where(r < 16, r + 122, r - 26)
 
 
 def strip_halo_z(i):
     r = i & 31
-    return jnp.where(jnp.logical_or(r < 8, r >= 24), 4096, strip_z(i))
+    return jnp.where(jnp.logical_or(r < 6, r >= 26), 4096, strip_z(i))
 
 
 def halve_rows(ref, n):
@@ -126,7 +131,7 @@
 
 def kernel(
     nw, nz, f_hbm, k_hbm, l_hbm, out_ref,
-    km, ks, pkm, pks, fm, fs, lm, ls, dgm, dgs, dm, ds_,
+    km, ks, pkm, pks, kbm, kbs, kam, kas, fm, fs, lm, ls, dgm, dgs, dm, ds_,
     avm, avs, apm, aps, aqm, aqs, arm, ars, bvm, bvs, bpm, bps, bqm, bqs, brm, brs, tm, ts,
     pack0, rs0, packv, rsv, kd1, kd1x, gg1, gg1x, pack1, rs1, pv1, rsv1, vv1, vv1x,
     k1l, k1, dg1, f1, va1, t1, kd2, kd2x, gl2, gl2x, k2, dg2, f2, l2, t2, t3, loc_sem, send_sem, recv_sem,
@@ -166,6 +171,10 @@
         started.append(Message(len(started), src, dst, a, b))
         return started[-1]
 
+    def loop(lo, hi, body):
+        for i in range(lo, hi):
+            body(i)
+
     lane, row = lanes(), iota((8, 128), 0)
     group, place = lane >> 5, lane & 31
 
@@ -200,26 +209,33 @@
         loads[-1].start()
 
     def own_strip(m):
-        out = None
-        for t in range(4):
-            tile = m[8 * t : 8 * t + 8, :]
-            part = jnp.where(place < 16, rot(tile, 32 * t + 8, 1), rot(tile, 32 * t + 24, 1))
-            out = part if out is None else jnp.where(group == t, part, out)
-        return out
+        out = rot(m[0:8, :], 6, 1)
+        for t in range(1, 4):
+            out = jnp.where(group == t, rot(m[8 * t : 8 * t + 8, :], 32 * t + 6, 1), out)
+        return jnp.where(place < 16, out, rot(out, 20, 1))
 
     def pack_strips(strips):
         left, right = jnp.zeros((8, 128), F32), jnp.zeros((8, 128), F32)
         for x, s in enumerate(strips):
-            hit = (place >> 2) == x
-            left = jnp.where(hit, rot(s, 4 * x - 24, 1), left)
-            right = jnp.where(hit, rot(s, 4 * x - 4, 1), right)
+            r = rot(s, 4 * x - 26, 1)
+            left = jnp.where((place >> 2) == x, r, left)
+            right = jnp.where((place >> 2) == (x + 2) % 8, r, right)
         return left, right
 
-    def whole_strip(own, rs, n, x):
+    def halves(rs, n):
+        out = []
+        for step in range(3):
+            left, right = rs[step, 0, n], rot(rs[step, 1, n], 40, 1)
+            out.append((jnp.where(place < 16, left, right), jnp.where(place < 16, right, left)))
+        return out
+
+    own_lanes = jnp.logical_or(place < 6, place >= 26)
+    used_lanes = jnp.logical_or(place < 10, place >= 22)
+
+    def whole_strip(own, merged, x):
         step, at = (x + 8) // 8, x % 8
-        halo = jnp.where(place < 16, rot(rs[step, 0, n], 8 - 4 * at, 1), rot(rs[step, 1, n], 20 - 4 * at, 1))
-        halo = jnp.where(jnp.logical_or(place < 12, place >= 20), halo, 0.0)
-        return jnp.where(jnp.logical_or(place < 8, place >= 24), own, halo)
+        halo = rot(merged[step][at // 4], 6 - 4 * at, 1)
+        return jnp.where(own_lanes, own, jnp.where(used_lanes, halo, 0.0))
 
     for n, (ref, strip, off) in enumerate(((km, ks, 4), (fm, fs, 2), (lm, ls, 2))):
         loads[n].wait()
@@ -252,30 +268,32 @@
 
     for c in e0k + e0s:
         c.arrived()
+    merged = halves(rs0, 0)
     for p in range(16):
         own = ks[p] if 4 <= p < 12 else own_strip(km[p])
-        ks[p] = whole_strip(own, rs0, 0, p - 4)
-
-    def k_lanes(i, c):
+        ks[p] = whole_strip(own, merged, p - 4)
+
+    def k_lanes(i):
         for p in (2 * i, 2 * i + 1):
             m, s = km[p], ks[p]
-            pkm[p], pks[p] = lanes_main(m, s), lanes_strip(s)
-        tm[pl.ds(pl.multiple_of(32 * i, 32), 32), :] = km[2 * i] + km[2 * i + 1]
+            below, above = beside_main(m, s)
+            kbm[p], kam[p], pkm[p] = below, above, below + above
+            below, above = beside(s)
+            kbs[p], kas[p], pks[p] = below, above, below + above
+        tm[32 * i : 32 * i + 32, :] = km[2 * i] + km[2 * i + 1]
         pair = ks[2 * i] + ks[2 * i + 1]
         parts = [jnp.where(group == t, pair, 0.0) for t in range(4)]
-        ts[pl.ds(pl.multiple_of(32 * i, 32), 32), :] = jnp.concatenate(parts, axis=0)
-        return c
-
-    lax.fori_loop(0, 8, k_lanes, 0)
+        ts[32 * i : 32 * i + 32, :] = jnp.concatenate(parts, axis=0)
+
+    loop(0, 8, k_lanes)
 
     coarse = dot(halve_rows(tm, 128), rm01) + dot(halve_rows(ts, 128), rs01)
     k1l[...] = (0.125 * coarse).reshape(8, 16, 128)
 
-    def l_pairs(i, c):
-        tm[pl.ds(pl.multiple_of(32 * i, 32), 32), :] = lm[2 * i + 2] + lm[2 * i + 3]
-        return c
-
-    lax.fori_loop(0, 4, l_pairs, 0)
+    def l_pairs(i):
+        tm[32 * i : 32 * i + 32, :] = lm[2 * i + 2] + lm[2 * i + 3]
+
+    loop(0, 4, l_pairs)
     l1 = (0.125 * dot(halve_rows(tm, 64), rm01)).reshape(4, 16, 128)
     own1 = k1l[2:6]
     half1 = 0.5 * 0.25
@@ -287,9 +305,10 @@
     for c in e0f + e0l:
         c.arrived()
     for n, (ref, strip) in ((1, (fm, fs)), (2, (lm, ls))):
+        merged = halves(rs0, n)
         for p in range(12):
             own = strip[p] if 2 <= p < 10 else own_strip(ref[p])
-            strip[p] = whole_strip(own, rs0, n, p - 2)
+            strip[p] = whole_strip(own, merged, p - 2)
 
     lane32 = iota((32, 128), 1)
 
@@ -299,12 +318,13 @@
     def ready(v, i, m, s, strips):
         vm, vs, pm, ps, qm, qs, rm, rs = v
         vm[i], vs[i] = m, s
-        pm[i] = lanes_main(m, s)
-        m, s = m * km[i + 2], s * ks[i + 2]
-        qm[i], rm[i] = m, lanes_main(m, s)
+        below, above = beside_main(m, s)
+        pm[i], qm[i] = below + above, m * km[i + 2]
+        rm[i] = below * kbm[i + 2] + above * kam[i + 2]
         if strips:
-            ps[i] = lanes_strip(vs[i])
-            qs[i], rs[i] = s, lanes_strip(s)
+            below, above = beside(s)
+            ps[i], qs[i] = below + above, s * ks[i + 2]
+            rs[i] = below * kbs[i + 2] + above * kas[i + 2]
 
     field_a = (avm, avs, apm, aps, aqm, aqs, arm, ars)
     field_b = (bvm, bvs, bpm, bps, bqm, bqs, brm, brs)
@@ -321,16 +341,8 @@
         s2 = neighbours(three(qs, i), three(rs, i), rows_strip)
         return fs[i] - dgs[i] * vs[i] + 0.5 * (ks[i + 2] * s1 + s2)
 
-    def loop(lo, hi, step, body):
-        def go(n, c):
-            for i in range(step):
-                body(lo + step * n + i)
-            return c
-
-        lax.fori_loop(0, (hi - lo) // step, go, 0)
-
     def first(i):
-        there = jnp.where(i < 2, inside(-1), jnp.where(i >= 10, inside(1), 1))
+        there = inside(-1) if i < 2 else inside(1) if i >= 10 else 1
         around = neighbours(three(km, i + 2), three(pkm, i + 2), rows_beside)
         diag = lm[i] + 0.5 * (CALL * km[i + 2] + around)
         inv = jnp.where(lane32 < 128 * there, OMEGA / diag, 0.0)
@@ -338,26 +350,25 @@
         m = inv * fm[i]
         around = neighbours(three(ks, i + 2), three(pks, i + 2), rows_strip)
         diag = ls[i] + 0.5 * (CALL * ks[i + 2] + around)
-        keep = jnp.logical_or(place < (8 + 4 * has_right) * there, place >= 32 - (8 + 4 * has_left) * there)
+        keep = jnp.logical_or(place < (6 + 4 * has_right) * there, place >= 32 - (6 + 4 * has_left) * there)
         inv = jnp.where(keep, OMEGA / diag, 0.0)
         dgs[i], ds_[i] = diag, inv
         ready(field_a, i, m, inv * fs[i], True)
 
-    loop(0, 12, 2, first)
+    loop(0, 12, first)
 
     def sweep(i):
         m = avm[i] + dm[i] * resid_main(field_a, i)
         s = avs[i] + ds_[i] * resid_strip(field_a, i)
         ready(field_b, i, m, s, False)
 
-    loop(1, 11, 2, sweep)
-
-    def resid_pairs(i, c):
+    loop(1, 11, sweep)
+
+    def resid_pairs(i):
         pair = resid_main(field_b, 2 * i + 2) + resid_main(field_b, 2 * i + 3)
-        tm[pl.ds(pl.multiple_of(32 * i, 32), 32), :] = pair
-        return c
-
-    lax.fori_loop(0, 4, resid_pairs, 0)
+        tm[32 * i : 32 * i + 32, :] = pair
+
+    loop(0, 4, resid_pairs)
     gg1[...] = (0.125 * dot(halve_rows(tm, 64), rm01)).reshape(4, 16, 128)
 
     def pack_sides1(arrays):
@@ -367,9 +378,9 @@
                 for t in range(2):
                     slot = 8 * n + 2 * x + t
                     tile = arr[x, 8 * t : 8 * t + 8, :]
-                    hit = (lane >> 2) == slot
-                    left = jnp.where(hit, rot(tile, 4 * slot, 1), left)
-                    right = jnp.where(hit, rot(tile, 4 * slot - 60, 1), right)
+                    r = rot(tile, 4 * slot, 1)
+                    left = jnp.where((lane >> 2) == slot, r, left)
+                    right = jnp.where((lane >> 2) == (slot + 15) % 32, r, right)
         return left, right
 
     e1x = send_planes(gg1.at[0:2], gg1x.at[1], gg1.at[2:4], gg1x.at[0])
@@ -396,28 +407,30 @@
     evx = [send(bvm.at[8], bvm.at[0], 1, 0), send(bvm.at[3], bvm.at[11], -1, 0)]
     evs = send_sides(packv, rsv)
 
-    def fill1(ref, depth, center, rs, n):
+    def fill1(ref, depth, own, x_ref, x_depth, shift, rs, n):
+        merged = [jnp.where(group == n, rs[step, 0], rs[step, 1]) for step in range(3)]
         for p in range(4 + 2 * depth):
             x = p - depth
-            step = (x + 4) // 4
             for t in range(2):
                 slot = 8 * n + 2 * (x % 4) + t
-                beside = jnp.where(lane < 96, rot(rs[step, 0], 64 - 4 * slot, 1), rot(rs[step, 1], 124 - 4 * slot, 1))
-                beside = jnp.where(jnp.logical_or(lane < 68, lane >= 124), beside, 0.0)
-                ref[p, 8 * t : 8 * t + 8, :] = jnp.where(lane < 64, center(x, slice(8 * t, 8 * t + 8)), beside)
-
-    def pick(own, x_ref, depth, x, rows, shift=0):
-        if x < 0:
-            return rot(x_ref[0, x + depth, rows, :], shift, 1)
-        if x > 3:
-            return rot(x_ref[1, x - 4, rows, :], shift, 1)
-        return rot(own[x, rows, :], shift, 1)
+                side = rot(merged[(x + 4) // 4], 64 - 4 * slot, 1)
+                rows = slice(8 * t, 8 * t + 8)
+                if x < 0:
+                    center = rot(x_ref[0, x + x_depth, rows, :], shift, 1)
+                elif x > 3:
+                    center = rot(x_ref[1, x - 4, rows, :], shift, 1)
+                else:
+                    center = own[x, rows, :]
+                side = jnp.where(jnp.logical_or(lane < 68, lane >= 124), side, 0.0)
+                ref[p, 8 * t : 8 * t + 8, :] = jnp.where(lane < 64, center, side)
 
     for c in ekd + e1x + e1s:
         c.arrived()
-    fill1(k1, 3, lambda x, r: pick(kd1, kd1x, 3, x, r), rs1, 0)
-    fill1(dg1, 2, lambda x, r: pick(kd1, kd1x, 3, x, r, 64), rs1, 1)
-    fill1(f1, 2, lambda x, r: pick(gg1, gg1x, 2, x, r), rs1, 2)
+    fill1(k1, 3, own1, kd1x, 3, 0, rs1, 0)
+    fill1(dg1, 2, diag1, kd1x, 3, 64, rs1, 1)
+    fill1(f1, 2, gg1, gg1x, 2, 0, rs1, 2)
+    k1_all = k1[...]
+    k1_all = (k1_all,) + beside(k1_all, 2)
 
     lane1 = iota((2, 16, 128), 2)
 
@@ -427,14 +440,14 @@
         return jnp.where(keep, OMEGA / dg1[lo:hi], 0.0)
 
     def sweep1(v, depth, inv):
-        kk = k1[3 - depth : 7 + depth]
+        kk = cut_planes(k1_all, 3 - depth, 7 + depth)
         lo, hi = 3 - depth, 5 + depth
         rest = f1[lo:hi] - ring_apply(v, kk, dg1[lo:hi], half1)
         return v[1:-1] + inv[lo:hi] * rest
 
     inv1 = jnp.concatenate([inverse1(0, 2, -1), inverse1(2, 4, 0), inverse1(4, 6, 0), inverse1(6, 8, 1)], axis=0)
     v = sweep1(inv1 * f1[...], 2, inv1)
-    r = f1[2:6] - ring_apply(v, k1[2:8], dg1[2:6], half1)
+    r = f1[2:6] - ring_apply(v, cut_planes(k1_all, 2, 8), dg1[2:6], half1)
     for i in range(2):
         t1[16 * i : 16 * i + 16, :] = r[2 * i] + r[2 * i + 1]
     rhs2 = (0.125 * dot(halve_rows(t1, 16), r12)).reshape(2, 8, 128)
@@ -446,11 +459,15 @@
     ev1x = send_planes(vv1.at[0:3], vv1x.at[1], vv1.at[1:4], vv1x.at[0])
     ev1s = send_sides(pv1, rsv1)
 
-    def near2(own, ref, step, n):
-        mid = own if step == 4 else ref[step, 1]
-        beside = jnp.where(lane < 64, rot(ref[step, 2], 32 - 32 * n, 1), rot(ref[step, 0], 96 - 32 * n, 1))
-        beside = jnp.where(jnp.logical_or(lane < 40, lane >= 120), beside, 0.0)
-        return jnp.where(lane < 32, rot(mid, -32 * n, 1), beside)
+    def around2(mine, ref, step):
+        mid = mine if step == 4 else ref[step, 1]
+        return mid, rot(ref[step, 2], 32, 1), rot(ref[step, 0], -32, 1)
+
+    def near2(parts, n):
+        mid, right, left = parts
+        at = (lane - 32 * n) & 127
+        side = jnp.where(at < 40, right, jnp.where(at >= 120, left, 0.0))
+        return rot(jnp.where(at < 32, mid, side), -32 * n, 1)
 
     for c in ekd2:
         c.arrived()
@@ -458,9 +475,10 @@
     for step in range(9):
         there = inside(step - 4)
         keep = jnp.logical_or(lane < (32 + 8 * has_right) * there, lane >= 128 - 8 * has_left * there)
+        parts = around2(mine, kd2x, step)
         for x in range(2):
-            k2[2 * step + x] = near2(mine, kd2x, step, x)
-            diag = near2(mine, kd2x, step, 2 + x)
+            k2[2 * step + x] = near2(parts, x)
+            diag = near2(parts, 2 + x)
             dg2[2 * step + x] = diag
             t2[2 * step + x] = jnp.where(keep, OMEGA / diag, 0.0)
 
@@ -473,6 +491,8 @@
             t3[i, 0:4, :] = y[4 * i : 4 * i + 4, :]
         return t3[0:n]
 
+    k2_all = k2[...]
+    k2_all = (k2_all,) + beside(k2_all, 2)
     t3[...] = jnp.zeros_like(t3)
     half3 = 0.5 * 0.015625
     k3 = to_level3([k2[2 * i] + k2[2 * i + 1] for i in range(9)])
@@ -482,17 +502,18 @@
         c.arrived()
     mine = gl2[...]
     for step in range(9):
+        parts = around2(mine, gl2x, step)
         for x in range(2):
-            f2[2 * step + x] = near2(mine, gl2x, step, x)
-        l2[step] = near2(mine, gl2x, step, 2)
+            f2[2 * step + x] = near2(parts, x)
+        l2[step] = near2(parts, 2)
 
     def sweep2(v, depth):
         lo, hi = 9 - depth, 9 + depth
-        rest = f2[lo:hi] - ring_apply(v, k2[lo - 1 : hi + 1], dg2[lo:hi], half2)
+        rest = f2[lo:hi] - ring_apply(v, cut_planes(k2_all, lo - 1, hi + 1), dg2[lo:hi], half2)
         return v[1:-1] + t2[lo:hi] * rest
 
     vb = sweep2(t2[...] * f2[...], 8)
-    r = f2[2:16] - ring_apply(vb, k2[1:17], dg2[2:16], half2)
+    r = f2[2:16] - ring_apply(vb, cut_planes(k2_all, 1, 17), dg2[2:16], half2)
     l3 = to_level3([l2[i + 1] for i in range(7)])
     f3 = to_level3([r[2 * i] + r[2 * i + 1] for i in range(7)])
     diag3 = l3 + most3
@@ -503,7 +524,7 @@
         inv3.append(jnp.where(jnp.logical_and(keep, row < 4), OMEGA / diag3[i], 0.0)[None])
     inv3 = jnp.concatenate(inv3, axis=0)
     v3 = inv3 * f3
-    rest = f3[1:-1] - ring_apply(v3, k3[1:-1], diag3[1:-1], half3)
+    rest = f3[1:-1] - ring_apply(v3, cut_planes((k3,) + beside(k3, 2), 1, 8), diag3[1:-1], half3)
     v3 = v3[1:-1] + inv3[1:-1] * rest
 
     p32 = ring_map(cut(64), 64, True)
@@ -518,7 +539,7 @@
 
     for c in ev1x + ev1s:
         c.arrived()
-    fill1(va1, 3, lambda x, r: pick(vv1, vv1x, 3, x, r), rsv1, 0)
+    fill1(va1, 3, vv1, vv1x, 3, 0, rsv1, 0)
     p21 = ring_map(cut(96), 64, True)
     double_rows(tm.at[0:96, :], dot(vb.reshape(48, 128), p21))
     e2v = tm[0:96, :].reshape(6, 16, 128)
@@ -534,26 +555,27 @@
     for c in evx + evs:
         c.arrived()
         c.left()
+    merged = halves(rsv, 0)
     for p in range(12):
         own = bvs[p] if 1 <= p < 11 else own_strip(bvm[p])
-        bvs[p] = whole_strip(own, rsv, 0, p - 2)
+        bvs[p] = whole_strip(own, merged, p - 2)
 
     def correct(i):
         at = 32 * (i // 2)
-        m = bvm[i] + tm[pl.ds(pl.multiple_of(at, 32), 32), :]
-        s = ts[pl.ds(pl.multiple_of(at, 8), 8), :]
+        m = bvm[i] + tm[at : at + 32, :]
+        s = ts[at : at + 8, :]
         for t in range(1, 4):
-            s = jnp.where(group == t, ts[pl.ds(pl.multiple_of(at + 8 * t, 8), 8), :], s)
-        s = jnp.where(jnp.logical_or(place < 12, place >= 20), bvs[i] + s, 0.0)
+            s = jnp.where(group == t, ts[at + 8 * t : at + 8 * t + 8, :], s)
+        s = jnp.where(used_lanes, bvs[i] + s, 0.0)
         ready(field_a, i, m, s, True)
 
-    loop(0, 12, 2, correct)
-    loop(1, 11, 2, sweep)
+    loop(0, 12, correct)
+    loop(1, 11, sweep)
 
     def last(i):
         out_ref[i - 2] = bvm[i] + dm[i] * resid_main(field_b, i)
 
-    loop(2, 10, 2, last)
+    loop(2, 10, last)
     for c in started:
         if not any(c is done for done in evx + evs):
             c.left()
@@ -569,7 +591,7 @@
         def pair(n):
             return [vm(n, 32, 128), vm(n, 8, 128)]
 
-        scratch = pair(16) * 2 + pair(12) * 4 + pair(12) * 8 + [vm(256, 128), vm(256, 128)]
+        scratch = pair(16) * 4 + pair(12) * 4 + pair(12) * 8 + [vm(256, 128), vm(256, 128)]
         scratch += [vm(2, 3, 8, 128), vm(3, 2, 3, 8, 128), vm(2, 1, 8, 128), vm(3, 2, 1, 8, 128)]
         scratch += [vm(4, 16, 128), vm(2, 3, 16, 128), vm(4, 16, 128), vm(2, 2, 16, 128)]
         scratch += [vm(2, 8, 128), vm(3, 2, 8, 128), vm(2, 8, 128), vm(3, 2, 8, 128)]

time: 38.2 us -> 34.3 us (0.90)
  Pallas kernels: 36.4 us -> 32.6 us
    pallas_call x1, Pallas kernels: 36.4 us -> 32.6 us  [on_device(): pl.pallas_call(body, out_shape=jax.ShapeDtypeStruct(source.shape, F32), i...]
where the time goes in v3:
time: 34.3 us; the launch traced here: 34.1 us
  Pallas kernels  32.6 us (95%)
  local copies, waits for them, and re-layouts  1.57 us (5%)
    pallas_call x1, Pallas kernels, on_device(): pl.pallas_call(body, out_shape=jax.ShapeDtypeStruct(source.shape, F32), i...  32.6 us
    unnamed x1, local copies, waits for them, and re-layouts  1.57 us

profile of v3, /device:TPU:15, one launch (start us, length us, event | category | flops | bytes accessed | tf_op | source)
XLA Modules:
  0.0 34.1 jit_solution(406760714165423271)
XLA Ops:
  0.0 32.6 %vcycle.1 = f32[8,32,128]{2,1,0:T(8,128)} custom-call(f32[8,32,128]{2,1,0:T(8,128)} %refs_0_.1, f32[8,32,128]{2,1,0:T(8,128)} %refs_1_.1, f32[8,32,128]{2,1,0:T(8,128)} %refs_2_.1), custom_call_target="tpu_custom_call" | custom-call | tf_op jit(solution)/shard_map/vcycle/pallas_call | solution.py:608
  32.6 1.6 %copy.5 = f32[8,32,128]{2,1,0:T(8,128)} copy(f32[8,32,128]{2,1,0:T(8,128)} %vcycle.1) | data formatting | bytes 262144

commit v4 on v3

--- a/solution.py
+++ b/solution.py
@@ -607,7 +607,7 @@
 
         return pl.pallas_call(
             body,
-            out_shape=jax.ShapeDtypeStruct(source.shape, F32),
+            out_shape=pltpu.VMEM(source.shape, F32),
             in_specs=[pl.BlockSpec(memory_space=pltpu.HBM)] * 3,
             out_specs=pl.BlockSpec(memory_space=pltpu.VMEM),
             scratch_shapes=scratch,

time: 34.3 us -> 32.7 us (0.953)
  local copies, waits for them, and re-layouts: 1.57 us -> 0.66 us
  Pallas kernels: 32.6 us -> 31.9 us
    unnamed x1, local copies, waits for them, and re-layouts: 1.57 us -> 0.66 us
    pallas_call x1, Pallas kernels: 32.6 us -> 31.9 us  [on_device(): pl.pallas_call(body, out_shape=pltpu.VMEM(source.shape, F32), in_specs=[p...]
where the time goes in v4:
time: 32.7 us; the launch traced here: 32.6 us
  Pallas kernels  31.9 us (98%)
  local copies, waits for them, and re-layouts  0.66 us (2%)
    pallas_call x1, Pallas kernels, on_device(): pl.pallas_call(body, out_shape=pltpu.VMEM(source.shape, F32), in_specs=[p...  31.9 us
    unnamed x1, local copies, waits for them, and re-layouts  0.66 us

profile of v4, /device:TPU:15, one launch (start us, length us, event | category | flops | bytes accessed | tf_op | source)
XLA Modules:
  0.0 32.6 jit_solution(1727416280633881159)
XLA Ops:
  0.0 31.9 %vcycle.1 = f32[8,32,128]{2,1,0:T(8,128)S(1)} custom-call(f32[8,32,128]{2,1,0:T(8,128)} %refs_0_.1, f32[8,32,128]{2,1,0:T(8,128)} %refs_1_.1, f32[8,32,128]{2,1,0:T(8,128)} %refs_2_.1), custom_call_target="tpu_custom_call" | custom-call | tf_op jit(solution)/shard_map/vcycle/pallas_call | solution.py:608
  31.9 0.7 %copy.5 = f32[8,32,128]{2,1,0:T(8,128)} copy(f32[8,32,128]{2,1,0:T(8,128)S(1)} %vcycle.1) | data formatting | bytes 262144

commit v5 on v4

--- a/solution.py
+++ b/solution.py
@@ -53,8 +53,8 @@
 
 def beside_main(m, s):
     lane = iota(m.shape, 1)
-    edge = jnp.where((iota(s.shape, 1) & 31) < 7, s, rot(s, -18, 1))
-    edge = jnp.concatenate([rot(edge, 121 - 32 * t, 1) for t in range(4)], axis=0)
+    edge = jnp.where((iota(s.shape, 1) & 31) < 9, s, rot(s, -14, 1))
+    edge = jnp.concatenate([rot(edge, 119 - 32 * t, 1) for t in range(4)], axis=0)
     return jnp.where(lane == 0, edge, rot(m, 1, 1)), jnp.where(lane == 127, edge, rot(m, 127, 1))
 
 
@@ -111,12 +111,12 @@
 
 def strip_z(i):
     r = i & 31
-    return jnp.where(r < 16, r + 122, r - 26)
+    return jnp.where(r < 16, r + 120, r - 24)
 
 
 def strip_halo_z(i):
     r = i & 31
-    return jnp.where(jnp.logical_or(r < 6, r >= 26), 4096, strip_z(i))
+    return jnp.where(jnp.logical_or(r < 8, r >= 24), 4096, strip_z(i))
 
 
 def halve_rows(ref, n):
@@ -133,7 +133,7 @@
     nw, nz, f_hbm, k_hbm, l_hbm, out_ref,
     km, ks, pkm, pks, kbm, kbs, kam, kas, fm, fs, lm, ls, dgm, dgs, dm, ds_,
     avm, avs, apm, aps, aqm, aqs, arm, ars, bvm, bvs, bpm, bps, bqm, bqs, brm, brs, tm, ts,
-    pack0, rs0, packv, rsv, kd1, kd1x, gg1, gg1x, pack1, rs1, pv1, rsv1, vv1, vv1x,
+    pack0, rs0, kd1, kd1x, gg1, gg1x, pv1, rsv1, vv1, vv1x,
     k1l, k1, dg1, f1, va1, t1, kd2, kd2x, gl2, gl2x, k2, dg2, f2, l2, t2, t3, loc_sem, send_sem, recv_sem,
 ):
     w, z = lax.axis_index("wide"), lax.axis_index("narrow")
@@ -178,7 +178,7 @@
     lane, row = lanes(), iota((8, 128), 0)
     group, place = lane >> 5, lane & 31
 
-    for ref in (rs0, rsv, rs1, rsv1, kd1x, gg1x, vv1x, kd2x, gl2x):
+    for ref in (rs0, rsv1, kd1x, gg1x, vv1x, kd2x, gl2x):
         ref[...] = jnp.zeros_like(ref)
 
     def clear(k_planes, planes, v_plane):
@@ -187,6 +187,7 @@
             fm[planes] = jnp.zeros((2, 32, 128), F32)
             lm[planes] = jnp.zeros((2, 32, 128), F32)
             bvm[v_plane] = jnp.zeros((32, 128), F32)
+            bvs[v_plane] = jnp.zeros((8, 128), F32)
 
         return body
 
@@ -209,40 +210,44 @@
         loads[-1].start()
 
     def own_strip(m):
-        out = rot(m[0:8, :], 6, 1)
+        out = rot(m[0:8, :], 8, 1)
         for t in range(1, 4):
-            out = jnp.where(group == t, rot(m[8 * t : 8 * t + 8, :], 32 * t + 6, 1), out)
-        return jnp.where(place < 16, out, rot(out, 20, 1))
+            out = jnp.where(group == t, rot(m[8 * t : 8 * t + 8, :], 32 * t + 8, 1), out)
+        return jnp.where(place < 16, out, rot(out, 16, 1))
+
+    eighth = place >> 3
+    even = (eighth & 1) == 0
+    spot = (0, 16, 8, 24)
 
     def pack_strips(strips):
         left, right = jnp.zeros((8, 128), F32), jnp.zeros((8, 128), F32)
         for x, s in enumerate(strips):
-            r = rot(s, 4 * x - 26, 1)
-            left = jnp.where((place >> 2) == x, r, left)
-            right = jnp.where((place >> 2) == (x + 2) % 8, r, right)
-        return left, right
-
-    def halves(rs, n):
-        out = []
-        for step in range(3):
-            left, right = rs[step, 0, n], rot(rs[step, 1, n], 40, 1)
-            out.append((jnp.where(place < 16, left, right), jnp.where(place < 16, right, left)))
+            r = rot(s, spot[x] - 24, 1)
+            left = jnp.where(eighth == spot[x] // 8, r, left)
+            right = jnp.where(eighth == (spot[x] // 8 + 1) % 4, r, right)
+        return left, rot(right, 32, 1)
+
+    def merge(rs, n):
+        out = {}
+        for step, half in ((0, 1), (1, 0), (1, 1), (2, 0)):
+            left, right = rs[step, 0, half, n], rs[step, 1, half, n]
+            out[step, half] = (jnp.where(even, left, right), jnp.where(even, right, left))
         return out
 
-    own_lanes = jnp.logical_or(place < 6, place >= 26)
-    used_lanes = jnp.logical_or(place < 10, place >= 22)
+    own_lanes = jnp.logical_or(place < 8, place >= 24)
 
     def whole_strip(own, merged, x):
-        step, at = (x + 8) // 8, x % 8
-        halo = rot(merged[step][at // 4], 6 - 4 * at, 1)
-        return jnp.where(own_lanes, own, jnp.where(used_lanes, halo, 0.0))
+        at = x % 8
+        halo = merged[(x + 8) // 8, at // 4][at % 4 // 2]
+        return jnp.where(own_lanes, own, rot(halo, 8 - spot[at % 4], 1))
 
     for n, (ref, strip, off) in enumerate(((km, ks, 4), (fm, fs, 2), (lm, ls, 2))):
         loads[n].wait()
         own = [own_strip(ref[x + off]) for x in range(8)]
         for x in range(8):
             strip[x + off] = own[x]
-        pack0[0, n], pack0[1, n] = pack_strips(own)
+        for half in range(2):
+            pack0[0, half, n], pack0[1, half, n] = pack_strips(own[4 * half : 4 * half + 4])
 
     def count(pos, reach, size):
         return jnp.minimum(pos, reach) + 1 + jnp.minimum(size - 1 - pos, reach)
@@ -259,7 +264,14 @@
         return [send(src, dst.at[4 - a, 1 - b], a, b) for a, b in FAR]
 
     e0k = send_planes(km.at[4:8], km.at[12:16], km.at[8:12], km.at[0:4])
-    e0s = send_sides(pack0, rs0)
+    e0s = []
+    for a, b in SIDES:
+        side = 0 if b < 0 else 1
+        if a == 0:
+            e0s.append(send(pack0.at[side], rs0.at[1, side], a, b))
+        else:
+            half = 0 if a < 0 else 1
+            e0s.append(send(pack0.at[side, half], rs0.at[1 - a, side, half], a, b))
     e0f = send_planes(fm.at[2:4], fm.at[10:12], fm.at[8:10], fm.at[0:2])
     e0l = send_planes(lm.at[2:4], lm.at[10:12], lm.at[8:10], lm.at[0:2])
 
@@ -268,10 +280,13 @@
 
     for c in e0k + e0s:
         c.arrived()
-    merged = halves(rs0, 0)
+    merged = merge(rs0, 0)
     for p in range(16):
         own = ks[p] if 4 <= p < 12 else own_strip(km[p])
         ks[p] = whole_strip(own, merged, p - 4)
+
+    def spread(strip):
+        return jnp.concatenate([jnp.where(group == t, strip, 0.0) for t in range(4)], axis=0)
 
     def k_lanes(i):
         for p in (2 * i, 2 * i + 1):
@@ -281,34 +296,33 @@
             below, above = beside(s)
             kbs[p], kas[p], pks[p] = below, above, below + above
         tm[32 * i : 32 * i + 32, :] = km[2 * i] + km[2 * i + 1]
-        pair = ks[2 * i] + ks[2 * i + 1]
-        parts = [jnp.where(group == t, pair, 0.0) for t in range(4)]
-        ts[32 * i : 32 * i + 32, :] = jnp.concatenate(parts, axis=0)
+        ts[32 * i : 32 * i + 32, :] = spread(ks[2 * i] + ks[2 * i + 1])
 
     loop(0, 8, k_lanes)
 
     coarse = dot(halve_rows(tm, 128), rm01) + dot(halve_rows(ts, 128), rs01)
     k1l[...] = (0.125 * coarse).reshape(8, 16, 128)
 
+    for c in e0f + e0l:
+        c.arrived()
+    for n, (ref, strip) in ((1, (fm, fs)), (2, (lm, ls))):
+        merged = merge(rs0, n)
+        for p in range(12):
+            own = strip[p] if 2 <= p < 10 else own_strip(ref[p])
+            strip[p] = whole_strip(own, merged, p - 2)
+
     def l_pairs(i):
         tm[32 * i : 32 * i + 32, :] = lm[2 * i + 2] + lm[2 * i + 3]
+        ts[32 * i : 32 * i + 32, :] = spread(ls[2 * i + 2] + ls[2 * i + 3])
 
     loop(0, 4, l_pairs)
-    l1 = (0.125 * dot(halve_rows(tm, 64), rm01)).reshape(4, 16, 128)
+    l1 = dot(halve_rows(tm, 64), rm01) + dot(halve_rows(ts, 64), rs01)
+    l1 = (0.125 * l1).reshape(4, 16, 128)
     own1 = k1l[2:6]
     half1 = 0.5 * 0.25
     diag1 = l1 + half1 * (CALL * own1 + ring_sum(k1l[1:7]))
-    lane16 = iota((4, 16, 128), 2)
-    kd1[...] = jnp.where(lane16 < 64, own1, rot(diag1, 64, 2))
+    kd1[:, 0], kd1[:, 1] = own1, diag1
     ekd = send_planes(kd1.at[0:3], kd1x.at[1], kd1.at[1:4], kd1x.at[0])
-
-    for c in e0f + e0l:
-        c.arrived()
-    for n, (ref, strip) in ((1, (fm, fs)), (2, (lm, ls))):
-        merged = halves(rs0, n)
-        for p in range(12):
-            own = strip[p] if 2 <= p < 10 else own_strip(ref[p])
-            strip[p] = whole_strip(own, merged, p - 2)
 
     lane32 = iota((32, 128), 1)
 
@@ -350,42 +364,31 @@
         m = inv * fm[i]
         around = neighbours(three(ks, i + 2), three(pks, i + 2), rows_strip)
         diag = ls[i] + 0.5 * (CALL * ks[i + 2] + around)
-        keep = jnp.logical_or(place < (6 + 4 * has_right) * there, place >= 32 - (6 + 4 * has_left) * there)
+        keep = jnp.logical_or(place < (8 + 8 * has_right) * there, place >= 32 - (8 + 8 * has_left) * there)
         inv = jnp.where(keep, OMEGA / diag, 0.0)
         dgs[i], ds_[i] = diag, inv
         ready(field_a, i, m, inv * fs[i], True)
 
     loop(0, 12, first)
 
-    def sweep(i):
+    def sweep(i, strips):
         m = avm[i] + dm[i] * resid_main(field_a, i)
         s = avs[i] + ds_[i] * resid_strip(field_a, i)
-        ready(field_b, i, m, s, False)
-
-    loop(1, 11, sweep)
+        ready(field_b, i, m, s, strips)
+
+    loop(1, 11, lambda i: sweep(i, True))
 
     def resid_pairs(i):
         pair = resid_main(field_b, 2 * i + 2) + resid_main(field_b, 2 * i + 3)
         tm[32 * i : 32 * i + 32, :] = pair
+        pair = resid_strip(field_b, 2 * i + 2) + resid_strip(field_b, 2 * i + 3)
+        ts[32 * i : 32 * i + 32, :] = spread(pair)
 
     loop(0, 4, resid_pairs)
-    gg1[...] = (0.125 * dot(halve_rows(tm, 64), rm01)).reshape(4, 16, 128)
-
-    def pack_sides1(arrays):
-        left, right = jnp.zeros((8, 128), F32), jnp.zeros((8, 128), F32)
-        for n, arr in enumerate(arrays):
-            for x in range(4):
-                for t in range(2):
-                    slot = 8 * n + 2 * x + t
-                    tile = arr[x, 8 * t : 8 * t + 8, :]
-                    r = rot(tile, 4 * slot, 1)
-                    left = jnp.where((lane >> 2) == slot, r, left)
-                    right = jnp.where((lane >> 2) == (slot + 15) % 32, r, right)
-        return left, right
+    rhs1 = dot(halve_rows(tm, 64), rm01) + dot(halve_rows(ts, 64), rs01)
+    gg1[...] = (0.125 * rhs1).reshape(4, 16, 128)
 
     e1x = send_planes(gg1.at[0:2], gg1x.at[1], gg1.at[2:4], gg1x.at[0])
-    pack1[0], pack1[1] = pack_sides1([own1, diag1, gg1[...]])
-    e1s = send_sides(pack1, rs1)
 
     kk = k1l[...]
     for i in range(4):
@@ -403,32 +406,36 @@
     l2sum = rot(l2own[0] + l2own[1], 64, 1)
     ekd2 = send_far(kd2, kd2x)
 
-    packv[0, 0], packv[1, 0] = pack_strips([bvs[x + 2] for x in range(8)])
-    evx = [send(bvm.at[8], bvm.at[0], 1, 0), send(bvm.at[3], bvm.at[11], -1, 0)]
-    evs = send_sides(packv, rsv)
-
-    def fill1(ref, depth, own, x_ref, x_depth, shift, rs, n):
-        merged = [jnp.where(group == n, rs[step, 0], rs[step, 1]) for step in range(3)]
-        for p in range(4 + 2 * depth):
-            x = p - depth
+    evx = []
+    for ref in (bvm, bvs):
+        evx += [send(ref.at[8], ref.at[0], 1, 0), send(ref.at[3], ref.at[11], -1, 0)]
+
+    def pack_sides1(arr):
+        left, right = jnp.zeros((8, 128), F32), jnp.zeros((8, 128), F32)
+        for x in range(4):
             for t in range(2):
-                slot = 8 * n + 2 * (x % 4) + t
-                side = rot(merged[(x + 4) // 4], 64 - 4 * slot, 1)
+                slot = 2 * x + t
+                r = rot(arr[x, 8 * t : 8 * t + 8, :], 4 * slot, 1)
+                left = jnp.where((lane >> 2) == slot, r, left)
+                right = jnp.where((lane >> 2) == slot + 15, r, right)
+        return left, right
+
+    def fill1(ref, own, x_ref, rs):
+        merged = [jnp.where(group == 0, rs[step, 0], rs[step, 1]) for step in range(3)]
+        for p in range(10):
+            x = p - 3
+            for t in range(2):
+                side = rot(merged[(x + 4) // 4], 64 - 4 * (2 * (x % 4) + t), 1)
+                side = jnp.where(jnp.logical_or(lane < 68, lane >= 124), side, 0.0)
                 rows = slice(8 * t, 8 * t + 8)
-                if x < 0:
-                    center = rot(x_ref[0, x + x_depth, rows, :], shift, 1)
-                elif x > 3:
-                    center = rot(x_ref[1, x - 4, rows, :], shift, 1)
-                else:
-                    center = own[x, rows, :]
-                side = jnp.where(jnp.logical_or(lane < 68, lane >= 124), side, 0.0)
+                center = x_ref[0, x + 3, rows, :] if x < 0 else x_ref[1, x - 4, rows, :] if x > 3 else own[x, rows, :]
                 ref[p, 8 * t : 8 * t + 8, :] = jnp.where(lane < 64, center, side)
 
-    for c in ekd + e1x + e1s:
+    for c in ekd + e1x:
         c.arrived()
-    fill1(k1, 3, own1, kd1x, 3, 0, rs1, 0)
-    fill1(dg1, 2, diag1, kd1x, 3, 64, rs1, 1)
-    fill1(f1, 2, gg1, gg1x, 2, 0, rs1, 2)
+    k1[0:3], k1[3:7], k1[7:10] = kd1x[0, :, 0], own1, kd1x[1, :, 0]
+    dg1[0:2], dg1[2:6], dg1[6:8] = kd1x[0, 1:3, 1], diag1, kd1x[1, 0:2, 1]
+    f1[0:2], f1[2:6], f1[6:8] = gg1x[0], gg1[...], gg1x[1]
     k1_all = k1[...]
     k1_all = (k1_all,) + beside(k1_all, 2)
 
@@ -455,7 +462,7 @@
     gl2[...] = jnp.where(lane < 32, rhs2[0], jnp.where(lane < 64, rot(rhs2[1], 32, 1), l2sum))
     e2 = send_far(gl2, gl2x)
     vv1[...] = v[1:5]
-    pv1[0], pv1[1] = pack_sides1([v[1:5]])
+    pv1[0], pv1[1] = pack_sides1(v[1:5])
     ev1x = send_planes(vv1.at[0:3], vv1x.at[1], vv1.at[1:4], vv1x.at[0])
     ev1s = send_sides(pv1, rsv1)
 
@@ -539,7 +546,7 @@
 
     for c in ev1x + ev1s:
         c.arrived()
-    fill1(va1, 3, vv1, vv1x, 3, 0, rsv1, 0)
+    fill1(va1, vv1, vv1x, rsv1)
     p21 = ring_map(cut(96), 64, True)
     double_rows(tm.at[0:96, :], dot(vb.reshape(48, 128), p21))
     e2v = tm[0:96, :].reshape(6, 16, 128)
@@ -552,32 +559,26 @@
     e1 = v.reshape(96, 128)
     double_rows(tm.at[0:192, :], dot(e1, ring_map(main_z, 96, True)))
     double_rows(ts.at[0:192, :], dot(e1, ring_map(strip_z, 96, True)))
-    for c in evx + evs:
+    for c in evx:
         c.arrived()
         c.left()
-    merged = halves(rsv, 0)
-    for p in range(12):
-        own = bvs[p] if 1 <= p < 11 else own_strip(bvm[p])
-        bvs[p] = whole_strip(own, merged, p - 2)
-
     def correct(i):
         at = 32 * (i // 2)
         m = bvm[i] + tm[at : at + 32, :]
         s = ts[at : at + 8, :]
         for t in range(1, 4):
             s = jnp.where(group == t, ts[at + 8 * t : at + 8 * t + 8, :], s)
-        s = jnp.where(used_lanes, bvs[i] + s, 0.0)
-        ready(field_a, i, m, s, True)
+        ready(field_a, i, m, bvs[i] + s, True)
 
     loop(0, 12, correct)
-    loop(1, 11, sweep)
+    loop(1, 11, lambda i: sweep(i, False))
 
     def last(i):
         out_ref[i - 2] = bvm[i] + dm[i] * resid_main(field_b, i)
 
     loop(2, 10, last)
     for c in started:
-        if not any(c is done for done in evx + evs):
+        if not any(c is done for done in evx):
             c.left()
 
 
@@ -592,14 +593,14 @@
             return [vm(n, 32, 128), vm(n, 8, 128)]
 
         scratch = pair(16) * 4 + pair(12) * 4 + pair(12) * 8 + [vm(256, 128), vm(256, 128)]
-        scratch += [vm(2, 3, 8, 128), vm(3, 2, 3, 8, 128), vm(2, 1, 8, 128), vm(3, 2, 1, 8, 128)]
-        scratch += [vm(4, 16, 128), vm(2, 3, 16, 128), vm(4, 16, 128), vm(2, 2, 16, 128)]
-        scratch += [vm(2, 8, 128), vm(3, 2, 8, 128), vm(2, 8, 128), vm(3, 2, 8, 128)]
+        scratch += [vm(2, 2, 3, 8, 128), vm(3, 2, 2, 3, 8, 128)]
+        scratch += [vm(4, 2, 16, 128), vm(2, 3, 2, 16, 128), vm(4, 16, 128), vm(2, 2, 16, 128)]
+        scratch += [vm(2, 8, 128), vm(3, 2, 8, 128)]
         scratch += [vm(4, 16, 128), vm(2, 3, 16, 128)]
         scratch += [vm(8, 16, 128), vm(10, 16, 128), vm(8, 16, 128), vm(8, 16, 128), vm(10, 16, 128), vm(128, 128)]
         scratch += [vm(8, 128), vm(9, 3, 8, 128), vm(8, 128), vm(9, 3, 8, 128)]
         scratch += [vm(18, 8, 128), vm(18, 8, 128), vm(18, 8, 128), vm(9, 8, 128), vm(18, 8, 128), vm(9, 8, 128)]
-        n = 12 + 2 + 8 + 26 + 8 + 26 + 8
+        n = 12 + 2 + 2 + 26 + 4 + 26 + 8
         scratch += [pltpu.SemaphoreType.DMA((3,)), pltpu.SemaphoreType.DMA((n,)), pltpu.SemaphoreType.DMA((n,))]
 
         def body(*refs):

time: 32.7 us -> 31.5 us (0.963)
  the two profiles are of different devices: /device:TPU:15 before, /device:TPU:79 now
where the time goes in v5:
time: 31.5 us; the launch traced here: 31.4 us
  Pallas kernels  30.7 us (97%)
  local copies, waits for them, and re-layouts  0.66 us (2%)
    pallas_call x1, Pallas kernels, on_device(): pl.pallas_call(body, out_shape=pltpu.VMEM(source.shape, F32), in_specs=[p...  30.7 us
    unnamed x1, local copies, waits for them, and re-layouts  0.66 us

profile of v5, /device:TPU:79, one launch (start us, length us, event | category | flops | bytes accessed | tf_op | source)
XLA Modules:
  0.0 31.4 jit_solution(13681524845166767369)
XLA Ops:
  0.0 30.7 %vcycle.1 = f32[8,32,128]{2,1,0:T(8,128)S(1)} custom-call(f32[8,32,128]{2,1,0:T(8,128)} %refs_0_.1, f32[8,32,128]{2,1,0:T(8,128)} %refs_1_.1, f32[8,32,128]{2,1,0:T(8,128)} %refs_2_.1), custom_call_target="tpu_custom_call" | custom-call | tf_op jit(solution)/shard_map/vcycle/pallas_call | solution.py:609
  30.7 0.7 %copy.5 = f32[8,32,128]{2,1,0:T(8,128)} copy(f32[8,32,128]{2,1,0:T(8,128)S(1)} %vcycle.1) | data formatting | bytes 262144

commit v6 on v5

--- a/solution.py
+++ b/solution.py
@@ -134,7 +134,7 @@
     km, ks, pkm, pks, kbm, kbs, kam, kas, fm, fs, lm, ls, dgm, dgs, dm, ds_,
     avm, avs, apm, aps, aqm, aqs, arm, ars, bvm, bvs, bpm, bps, bqm, bqs, brm, brs, tm, ts,
     pack0, rs0, kd1, kd1x, gg1, gg1x, pv1, rsv1, vv1, vv1x,
-    k1l, k1, dg1, f1, va1, t1, kd2, kd2x, gl2, gl2x, k2, dg2, f2, l2, t2, t3, loc_sem, send_sem, recv_sem,
+    k1l, k1, dg1, f1, va1, t1, kd2, kd2x, gl2, gl2x, k2, dg2, f2, l2, t2, t3, hello, loc_sem, send_sem, recv_sem,
 ):
     w, z = lax.axis_index("wide"), lax.axis_index("narrow")
 
@@ -203,7 +203,8 @@
         return body
 
     for a, b in FAR:
-        pl.when(in_grid(a, b))(greet(a, b))
+        if b >= 0:
+            pl.when(in_grid(a, b))(greet(a, b))
     loads = []
     for n, (src, dst) in enumerate(((k_hbm, km.at[4:12]), (f_hbm, fm.at[2:10]), (l_hbm, lm.at[2:10]))):
         loads.append(pltpu.make_async_copy(src, dst, loc_sem.at[n]))
@@ -241,6 +242,29 @@
         halo = merged[(x + 8) // 8, at // 4][at % 4 // 2]
         return jnp.where(own_lanes, own, rot(halo, 8 - spot[at % 4], 1))
 
+    def count(pos, reach, size):
+        return jnp.minimum(pos, reach) + 1 + jnp.minimum(size - 1 - pos, reach)
+
+    pl.semaphore_wait(barrier, count(w, 4, nw) * (1 + has_left) - 1)
+
+    def say_hello():
+        pl.semaphore_signal(hello, inc=1, device_id=device(0, -1), device_id_type=MESH)
+
+    pl.when(z > 0)(say_hello)
+
+    def send_planes(src_lo, dst_hi, src_hi, dst_lo):
+        return [send(src_hi, dst_lo, 1, 0), send(src_lo, dst_hi, -1, 0)]
+
+    def send_sides(pack, rs):
+        return [send(pack.at[0 if b < 0 else 1], rs.at[1 - a, 0 if b < 0 else 1], a, b) for a, b in SIDES]
+
+    def send_far(src, dst):
+        return [send(src, dst.at[4 - a, 1 - b], a, b) for a, b in FAR]
+
+    e0k = send_planes(k_hbm.at[0:4], km.at[12:16], k_hbm.at[4:8], km.at[0:4])
+    e0f = send_planes(f_hbm.at[0:2], fm.at[10:12], f_hbm.at[6:8], fm.at[0:2])
+    e0l = send_planes(l_hbm.at[0:2], lm.at[10:12], l_hbm.at[6:8], lm.at[0:2])
+
     for n, (ref, strip, off) in enumerate(((km, ks, 4), (fm, fs, 2), (lm, ls, 2))):
         loads[n].wait()
         own = [own_strip(ref[x + off]) for x in range(8)]
@@ -249,31 +273,23 @@
         for half in range(2):
             pack0[0, half, n], pack0[1, half, n] = pack_strips(own[4 * half : 4 * half + 4])
 
-    def count(pos, reach, size):
-        return jnp.minimum(pos, reach) + 1 + jnp.minimum(size - 1 - pos, reach)
-
-    pl.semaphore_wait(barrier, count(w, 4, nw) * count(z, 1, nz) - 1)
-
-    def send_planes(src_lo, dst_hi, src_hi, dst_lo):
-        return [send(src_hi, dst_lo, 1, 0), send(src_lo, dst_hi, -1, 0)]
-
-    def send_sides(pack, rs):
-        return [send(pack.at[0 if b < 0 else 1], rs.at[1 - a, 0 if b < 0 else 1], a, b) for a, b in SIDES]
-
-    def send_far(src, dst):
-        return [send(src, dst.at[4 - a, 1 - b], a, b) for a, b in FAR]
-
-    e0k = send_planes(km.at[4:8], km.at[12:16], km.at[8:12], km.at[0:4])
-    e0s = []
-    for a, b in SIDES:
+    def send_strips(b):
         side = 0 if b < 0 else 1
-        if a == 0:
-            e0s.append(send(pack0.at[side], rs0.at[1, side], a, b))
-        else:
-            half = 0 if a < 0 else 1
-            e0s.append(send(pack0.at[side, half], rs0.at[1 - a, side, half], a, b))
-    e0f = send_planes(fm.at[2:4], fm.at[10:12], fm.at[8:10], fm.at[0:2])
-    e0l = send_planes(lm.at[2:4], lm.at[10:12], lm.at[8:10], lm.at[0:2])
+        out = []
+        for a in (0, -1, 1):
+            if a == 0:
+                out.append(send(pack0.at[side], rs0.at[1, side], a, b))
+            else:
+                half = 0 if a < 0 else 1
+                out.append(send(pack0.at[side, half], rs0.at[1 - a, side, half], a, b))
+        return out
+
+    e0s = send_strips(-1)
+    def hear_hello():
+        pl.semaphore_wait(hello, 1)
+
+    pl.when(z < nz - 1)(hear_hello)
+    e0s += send_strips(1)
 
     rm01, rs01 = ring_map(main_z, 96), ring_map(strip_halo_z, 96)
     r12, r23 = ring_map(cut(96), 64), ring_map(cut(64), 64)
@@ -601,7 +617,7 @@
         scratch += [vm(8, 128), vm(9, 3, 8, 128), vm(8, 128), vm(9, 3, 8, 128)]
         scratch += [vm(18, 8, 128), vm(18, 8, 128), vm(18, 8, 128), vm(9, 8, 128), vm(18, 8, 128), vm(9, 8, 128)]
         n = 12 + 2 + 2 + 26 + 4 + 26 + 8
-        scratch += [pltpu.SemaphoreType.DMA((3,)), pltpu.SemaphoreType.DMA((n,)), pltpu.SemaphoreType.DMA((n,))]
+        scratch += [pltpu.SemaphoreType.REGULAR, pltpu.SemaphoreType.DMA((3,)), pltpu.SemaphoreType.DMA((n,)), pltpu.SemaphoreType.DMA((n,))]
 
         def body(*refs):
             kernel(nw, nz, *refs)

time: 31.5 us -> 30.5 us (0.968)
  the two profiles are of different devices: /device:TPU:79 before, /device:TPU:143 now
where the time goes in v6:
time: 30.5 us; the launch traced here: 30.4 us
  Pallas kernels  29.7 us (97%)
  local copies, waits for them, and re-layouts  0.66 us (2%)
    pallas_call x1, Pallas kernels, on_device(): pl.pallas_call(body, out_shape=pltpu.VMEM(source.shape, F32), in_specs=[p...  29.7 us
    unnamed x1, local copies, waits for them, and re-layouts  0.66 us

profile of v6, /device:TPU:143, one launch (start us, length us, event | category | flops | bytes accessed | tf_op | source)
XLA Modules:
  0.0 30.4 jit_solution(12174381278971249877)
XLA Ops:
  0.0 29.7 %vcycle.1 = f32[8,32,128]{2,1,0:T(8,128)S(1)} custom-call(f32[8,32,128]{2,1,0:T(8,128)} %refs_0_.1, f32[8,32,128]{2,1,0:T(8,128)} %refs_1_.1, f32[8,32,128]{2,1,0:T(8,128)} %refs_2_.1), custom_call_target="tpu_custom_call" | custom-call | tf_op jit(solution)/shard_map/vcycle/pallas_call | solution.py:625
  29.7 0.7 %copy.5 = f32[8,32,128]{2,1,0:T(8,128)} copy(f32[8,32,128]{2,1,0:T(8,128)S(1)} %vcycle.1) | data formatting | bytes 262144

commit v7 on v6

--- a/solution.py
+++ b/solution.py
@@ -51,13 +51,6 @@
     return CX * x + CXZ * xp + CZ * p[1] + y(inner)
 
 
-def beside_main(m, s):
-    lane = iota(m.shape, 1)
-    edge = jnp.where((iota(s.shape, 1) & 31) < 9, s, rot(s, -14, 1))
-    edge = jnp.concatenate([rot(edge, 119 - 32 * t, 1) for t in range(4)], axis=0)
-    return jnp.where(lane == 0, edge, rot(m, 1, 1)), jnp.where(lane == 127, edge, rot(m, 127, 1))
-
-
 def beside(u, axis=1):
     return rot(u, 1, axis), rot(u, 127, axis)
 
@@ -109,14 +102,18 @@
     return i
 
 
+def inner_z(i):
+    return jnp.where(jnp.logical_and(i >= 4, i < 124), i, 4096)
+
+
 def strip_z(i):
     r = i & 31
     return jnp.where(r < 16, r + 120, r - 24)
 
 
-def strip_halo_z(i):
+def outer_z(i):
     r = i & 31
-    return jnp.where(jnp.logical_or(r < 8, r >= 24), 4096, strip_z(i))
+    return jnp.where(jnp.logical_or(r < 4, r >= 28), 4096, strip_z(i))
 
 
 def halve_rows(ref, n):
@@ -132,7 +129,7 @@
 def kernel(
     nw, nz, f_hbm, k_hbm, l_hbm, out_ref,
     km, ks, pkm, pks, kbm, kbs, kam, kas, fm, fs, lm, ls, dgm, dgs, dm, ds_,
-    avm, avs, apm, aps, aqm, aqs, arm, ars, bvm, bvs, bpm, bps, bqm, bqs, brm, brs, tm, ts,
+    avm, avs, apm, aps, aqm, aqs, arm, ars, bvm, bvs, bpm, bps, bqm, bqs, brm, brs, tm, ts, tlm, tls,
     pack0, rs0, kd1, kd1x, gg1, gg1x, pv1, rsv1, vv1, vv1x,
     k1l, k1, dg1, f1, va1, t1, kd2, kd2x, gl2, gl2x, k2, dg2, f2, l2, t2, t3, hello, loc_sem, send_sem, recv_sem,
 ):
@@ -291,8 +288,80 @@
     pl.when(z < nz - 1)(hear_hello)
     e0s += send_strips(1)
 
-    rm01, rs01 = ring_map(main_z, 96), ring_map(strip_halo_z, 96)
+    def three(ref, i):
+        return ref[i - 1], ref[i], ref[i + 1]
+
+    field_a = ((avm, apm, aqm, arm), (avs, aps, aqs, ars))
+    field_b = ((bvm, bpm, bqm, brm), (bvs, bps, bqs, brs))
+    on_main = ((fm, dgm, dm), (km, kbm, kam), rows_beside)
+    on_strip = ((fs, dgs, ds_), (ks, kbs, kas), rows_strip)
+
+    def ready(field, part, i, value):
+        v, p, q, r = field
+        k, k_below, k_above = part[1]
+        v[i] = value
+        below, above = beside(value)
+        p[i], q[i] = below + above, value * k[i + 2]
+        r[i] = below * k_below[i + 2] + above * k_above[i + 2]
+
+    def resid(field, part, i):
+        v, p, q, r = field
+        (f, dg, _), (k, _, _), rows = part
+        s1 = neighbours(three(v, i), three(p, i), rows)
+        s2 = neighbours(three(q, i), three(r, i), rows)
+        return f[i] - dg[i] * v[i] + 0.5 * (k[i + 2] * s1 + s2)
+
+    def sweep(i, side):
+        part = (on_main, on_strip)[side]
+        source = field_a[side]
+        ready(field_b[side], part, i, source[0][i] + part[0][2][i] * resid(source, part, i))
+
+    def there0(i):
+        return inside(-1) if i < 2 else inside(1) if i >= 10 else 1
+
+    lane32 = iota((32, 128), 1)
+
+    def first_main(i):
+        around = neighbours(three(km, i + 2), three(pkm, i + 2), rows_beside)
+        diag = lm[i] + 0.5 * (CALL * km[i + 2] + around)
+        inv = OMEGA / diag
+        if not 2 <= i < 10:
+            inv = jnp.where(lane32 < 128 * there0(i), inv, 0.0)
+        dgm[i], dm[i] = diag, inv
+        ready(field_a[0], on_main, i, inv * fm[i])
+
+    def first_strip(i):
+        there = there0(i)
+        around = neighbours(three(ks, i + 2), three(pks, i + 2), rows_strip)
+        diag = ls[i] + 0.5 * (CALL * ks[i + 2] + around)
+        keep = jnp.logical_or(place < (8 + 8 * has_right) * there, place >= 32 - (8 + 8 * has_left) * there)
+        inv = jnp.where(keep, OMEGA / diag, 0.0)
+        dgs[i], ds_[i] = diag, inv
+        ready(field_a[1], on_strip, i, inv * fs[i])
+
+    def spread(s):
+        return jnp.concatenate([jnp.where(group == t, s, 0.0) for t in range(4)], axis=0)
+
+    def k_main(p):
+        below, above = beside(km[p])
+        kbm[p], kam[p], pkm[p] = below, above, below + above
+
+    def k_pair(i):
+        tm[32 * i : 32 * i + 32, :] = km[2 * i] + km[2 * i + 1]
+
+    rm01, rs01 = ring_map(inner_z, 96), ring_map(outer_z, 96)
     r12, r23 = ring_map(cut(96), 64), ring_map(cut(64), 64)
+
+    for p in range(4, 12):
+        k_main(p)
+    for i in range(2, 6):
+        k_pair(i)
+    for i in range(4):
+        tlm[32 * i : 32 * i + 32, :] = lm[2 * i + 2] + lm[2 * i + 3]
+    loop(3, 9, first_main)
+    for i in range(4, 8):
+        sweep(i, 0)
+    early = {i: resid(field_b[0], on_main, i) for i in (5, 6)}
 
     for c in e0k + e0s:
         c.arrived()
@@ -301,20 +370,15 @@
         own = ks[p] if 4 <= p < 12 else own_strip(km[p])
         ks[p] = whole_strip(own, merged, p - 4)
 
-    def spread(strip):
-        return jnp.concatenate([jnp.where(group == t, strip, 0.0) for t in range(4)], axis=0)
-
-    def k_lanes(i):
-        for p in (2 * i, 2 * i + 1):
-            m, s = km[p], ks[p]
-            below, above = beside_main(m, s)
-            kbm[p], kam[p], pkm[p] = below, above, below + above
-            below, above = beside(s)
-            kbs[p], kas[p], pks[p] = below, above, below + above
-        tm[32 * i : 32 * i + 32, :] = km[2 * i] + km[2 * i + 1]
+    for p in range(16):
+        below, above = beside(ks[p])
+        kbs[p], kas[p], pks[p] = below, above, below + above
+    for p in (1, 2, 3, 12, 13, 14):
+        k_main(p)
+    for i in (0, 1, 6, 7):
+        k_pair(i)
+    for i in range(8):
         ts[32 * i : 32 * i + 32, :] = spread(ks[2 * i] + ks[2 * i + 1])
-
-    loop(0, 8, k_lanes)
 
     coarse = dot(halve_rows(tm, 128), rm01) + dot(halve_rows(ts, 128), rs01)
     k1l[...] = (0.125 * coarse).reshape(8, 16, 128)
@@ -327,12 +391,9 @@
             own = strip[p] if 2 <= p < 10 else own_strip(ref[p])
             strip[p] = whole_strip(own, merged, p - 2)
 
-    def l_pairs(i):
-        tm[32 * i : 32 * i + 32, :] = lm[2 * i + 2] + lm[2 * i + 3]
-        ts[32 * i : 32 * i + 32, :] = spread(ls[2 * i + 2] + ls[2 * i + 3])
-
-    loop(0, 4, l_pairs)
-    l1 = dot(halve_rows(tm, 64), rm01) + dot(halve_rows(ts, 64), rs01)
+    for i in range(4):
+        tls[32 * i : 32 * i + 32, :] = spread(ls[2 * i + 2] + ls[2 * i + 3])
+    l1 = dot(halve_rows(tlm, 64), rm01) + dot(halve_rows(tls, 64), rs01)
     l1 = (0.125 * l1).reshape(4, 16, 128)
     own1 = k1l[2:6]
     half1 = 0.5 * 0.25
@@ -340,67 +401,18 @@
     kd1[:, 0], kd1[:, 1] = own1, diag1
     ekd = send_planes(kd1.at[0:3], kd1x.at[1], kd1.at[1:4], kd1x.at[0])
 
-    lane32 = iota((32, 128), 1)
-
-    def three(ref, i):
-        return ref[i - 1], ref[i], ref[i + 1]
-
-    def ready(v, i, m, s, strips):
-        vm, vs, pm, ps, qm, qs, rm, rs = v
-        vm[i], vs[i] = m, s
-        below, above = beside_main(m, s)
-        pm[i], qm[i] = below + above, m * km[i + 2]
-        rm[i] = below * kbm[i + 2] + above * kam[i + 2]
-        if strips:
-            below, above = beside(s)
-            ps[i], qs[i] = below + above, s * ks[i + 2]
-            rs[i] = below * kbs[i + 2] + above * kas[i + 2]
-
-    field_a = (avm, avs, apm, aps, aqm, aqs, arm, ars)
-    field_b = (bvm, bvs, bpm, bps, bqm, bqs, brm, brs)
-
-    def resid_main(v, i):
-        vm, vs, pm, ps, qm, qs, rm, rs = v
-        s1 = neighbours(three(vm, i), three(pm, i), rows_beside)
-        s2 = neighbours(three(qm, i), three(rm, i), rows_beside)
-        return fm[i] - dgm[i] * vm[i] + 0.5 * (km[i + 2] * s1 + s2)
-
-    def resid_strip(v, i):
-        vm, vs, pm, ps, qm, qs, rm, rs = v
-        s1 = neighbours(three(vs, i), three(ps, i), rows_strip)
-        s2 = neighbours(three(qs, i), three(rs, i), rows_strip)
-        return fs[i] - dgs[i] * vs[i] + 0.5 * (ks[i + 2] * s1 + s2)
-
-    def first(i):
-        there = inside(-1) if i < 2 else inside(1) if i >= 10 else 1
-        around = neighbours(three(km, i + 2), three(pkm, i + 2), rows_beside)
-        diag = lm[i] + 0.5 * (CALL * km[i + 2] + around)
-        inv = jnp.where(lane32 < 128 * there, OMEGA / diag, 0.0)
-        dgm[i], dm[i] = diag, inv
-        m = inv * fm[i]
-        around = neighbours(three(ks, i + 2), three(pks, i + 2), rows_strip)
-        diag = ls[i] + 0.5 * (CALL * ks[i + 2] + around)
-        keep = jnp.logical_or(place < (8 + 8 * has_right) * there, place >= 32 - (8 + 8 * has_left) * there)
-        inv = jnp.where(keep, OMEGA / diag, 0.0)
-        dgs[i], ds_[i] = diag, inv
-        ready(field_a, i, m, inv * fs[i], True)
-
-    loop(0, 12, first)
-
-    def sweep(i, strips):
-        m = avm[i] + dm[i] * resid_main(field_a, i)
-        s = avs[i] + ds_[i] * resid_strip(field_a, i)
-        ready(field_b, i, m, s, strips)
-
-    loop(1, 11, lambda i: sweep(i, True))
-
-    def resid_pairs(i):
-        pair = resid_main(field_b, 2 * i + 2) + resid_main(field_b, 2 * i + 3)
-        tm[32 * i : 32 * i + 32, :] = pair
-        pair = resid_strip(field_b, 2 * i + 2) + resid_strip(field_b, 2 * i + 3)
-        ts[32 * i : 32 * i + 32, :] = spread(pair)
-
-    loop(0, 4, resid_pairs)
+    for i in (0, 1, 2, 9, 10, 11):
+        first_main(i)
+    loop(0, 12, first_strip)
+    for i in (1, 2, 3, 8, 9, 10):
+        sweep(i, 0)
+    for i in range(1, 11):
+        sweep(i, 1)
+    for i in range(4):
+        pair = [early[n] if n in early else resid(field_b[0], on_main, n) for n in (2 * i + 2, 2 * i + 3)]
+        tm[32 * i : 32 * i + 32, :] = pair[0] + pair[1]
+        pair = [resid(field_b[1], on_strip, n) for n in (2 * i + 2, 2 * i + 3)]
+        ts[32 * i : 32 * i + 32, :] = spread(pair[0] + pair[1])
     rhs1 = dot(halve_rows(tm, 64), rm01) + dot(halve_rows(ts, 64), rs01)
     gg1[...] = (0.125 * rhs1).reshape(4, 16, 128)
 
@@ -584,13 +596,20 @@
         s = ts[at : at + 8, :]
         for t in range(1, 4):
             s = jnp.where(group == t, ts[at + 8 * t : at + 8 * t + 8, :], s)
-        ready(field_a, i, m, bvs[i] + s, True)
+        ready(field_a[0], on_main, i, m)
+        ready(field_a[1], on_strip, i, bvs[i] + s)
 
     loop(0, 12, correct)
-    loop(1, 11, lambda i: sweep(i, False))
+    for i in range(1, 11):
+        sweep(i, 0)
+        sweep(i, 1)
 
     def last(i):
-        out_ref[i - 2] = bvm[i] + dm[i] * resid_main(field_b, i)
+        m = bvm[i] + dm[i] * resid(field_b[0], on_main, i)
+        s = bvs[i] + ds_[i] * resid(field_b[1], on_strip, i)
+        s = jnp.where(place < 8, s, rot(s, -16, 1))
+        ends = jnp.concatenate([rot(s, 120 - 32 * t, 1) for t in range(4)], axis=0)
+        out_ref[i - 2] = jnp.where(jnp.logical_or(lane32 < 4, lane32 >= 124), ends, m)
 
     loop(2, 10, last)
     for c in started:
@@ -608,7 +627,7 @@
         def pair(n):
             return [vm(n, 32, 128), vm(n, 8, 128)]
 
-        scratch = pair(16) * 4 + pair(12) * 4 + pair(12) * 8 + [vm(256, 128), vm(256, 128)]
+        scratch = pair(16) * 4 + pair(12) * 4 + pair(12) * 8 + [vm(256, 128), vm(256, 128), vm(128, 128), vm(128, 128)]
         scratch += [vm(2, 2, 3, 8, 128), vm(3, 2, 2, 3, 8, 128)]
         scratch += [vm(4, 2, 16, 128), vm(2, 3, 2, 16, 128), vm(4, 16, 128), vm(2, 2, 16, 128)]
         scratch += [vm(2, 8, 128), vm(3, 2, 8, 128)]

time: 30.5 us -> 29 us (0.951)
  Pallas kernels: 29.7 us -> 28.2 us
    pallas_call x1, Pallas kernels: 29.7 us -> 28.2 us  [on_device(): pl.pallas_call(body, out_shape=pltpu.VMEM(source.shape, F32), in_specs=[p...]
where the time goes in v7:
time: 29 us; the launch traced here: 28.9 us
  Pallas kernels  28.2 us (97%)
  local copies, waits for them, and re-layouts  0.66 us (2%)
    pallas_call x1, Pallas kernels, on_device(): pl.pallas_call(body, out_shape=pltpu.VMEM(source.shape, F32), in_specs=[p...  28.2 us
    unnamed x1, local copies, waits for them, and re-layouts  0.66 us

profile of v7, /device:TPU:143, one launch (start us, length us, event | category | flops | bytes accessed | tf_op | source)
XLA Modules:
  0.0 28.9 jit_solution(4855831787973973916)
XLA Ops:
  0.0 28.2 %vcycle.1 = f32[8,32,128]{2,1,0:T(8,128)S(1)} custom-call(f32[8,32,128]{2,1,0:T(8,128)} %refs_0_.1, f32[8,32,128]{2,1,0:T(8,128)} %refs_1_.1, f32[8,32,128]{2,1,0:T(8,128)} %refs_2_.1), custom_call_target="tpu_custom_call" | custom-call | tf_op jit(solution)/shard_map/vcycle/pallas_call | solution.py:644
  28.2 0.7 %copy.5 = f32[8,32,128]{2,1,0:T(8,128)} copy(f32[8,32,128]{2,1,0:T(8,128)S(1)} %vcycle.1) | data formatting | bytes 262144

commit v8 on v7

--- a/solution.py
+++ b/solution.py
@@ -20,7 +20,7 @@
 CALL = 2 * (CX + CY + CZ) + 4 * (CXY + CXZ + CYZ) + 8 * CXYZ
 
 SIDES = [(a, b) for b in (-1, 1) for a in (-1, 0, 1)]
-FAR = [(a, b) for a in range(-4, 5) for b in (-1, 0, 1) if (a, b) != (0, 0)]
+FAR = [(a, b) for n in (4, 3, 2, 1, 0) for a in sorted({-n, n}) for b in (-1, 1, 0) if (a, b) != (0, 0)]
 
 
 def iota(shape, dim):
@@ -88,18 +88,13 @@
     return lax.dot_general(a, b, (((1,), (0,)), ((), ())), precision=lax.Precision.HIGHEST, preferred_element_type=F32)
 
 
-def ring_map(fine_of, coarse_cut, transpose=False):
-    f_dim = 1 if transpose else 0
-    i, j = iota((128, 128), f_dim), iota((128, 128), 1 - f_dim)
+def ring_map(fine_of, coarse_cut):
+    i, j = iota((128, 128), 0), iota((128, 128), 1)
     return ((fine_of(i) >> 1) == jnp.where(j < coarse_cut, j, j - 128)).astype(F32)
 
 
 def cut(c):
     return lambda i: jnp.where(i < c, i, i - 128)
-
-
-def main_z(i):
-    return i
 
 
 def inner_z(i):
@@ -114,6 +109,13 @@
 def outer_z(i):
     r = i & 31
     return jnp.where(jnp.logical_or(r < 4, r >= 28), 4096, strip_z(i))
+
+
+def from_lanes(x, index):
+    index = index if isinstance(index, tuple) else (index,)
+    tiles = [x[8 * i : 8 * i + 8] for i in range(x.shape[0] // 8)]
+    tiles = [jnp.take_along_axis(t, index[i % len(index)], axis=1) for i, t in enumerate(tiles)]
+    return jnp.concatenate(tiles, axis=0)
 
 
 def halve_rows(ref, n):
@@ -136,7 +138,7 @@
     w, z = lax.axis_index("wide"), lax.axis_index("narrow")
 
     def device(a, b):
-        return (lax.rem(w + (a + nw), nw), lax.rem(z + (b + nz), nz))
+        return (w + a, z + b)
 
     def in_grid(a, b):
         ok = jnp.logical_and(w + a >= 0, w + a < nw)
@@ -175,6 +177,11 @@
     lane, row = lanes(), iota((8, 128), 0)
     group, place = lane >> 5, lane & 31
 
+    loads = []
+    for n, (src, dst) in enumerate(((k_hbm, km.at[4:12]), (f_hbm, fm.at[2:10]), (l_hbm, lm.at[2:10]))):
+        loads.append(pltpu.make_async_copy(src, dst, loc_sem.at[n]))
+        loads[-1].start()
+
     for ref in (rs0, rsv1, kd1x, gg1x, vv1x, kd2x, gl2x):
         ref[...] = jnp.zeros_like(ref)
 
@@ -202,11 +209,6 @@
     for a, b in FAR:
         if b >= 0:
             pl.when(in_grid(a, b))(greet(a, b))
-    loads = []
-    for n, (src, dst) in enumerate(((k_hbm, km.at[4:12]), (f_hbm, fm.at[2:10]), (l_hbm, lm.at[2:10]))):
-        loads.append(pltpu.make_async_copy(src, dst, loc_sem.at[n]))
-        loads[-1].start()
-
     def own_strip(m):
         out = rot(m[0:8, :], 8, 1)
         for t in range(1, 4):
@@ -412,8 +414,20 @@
         pair = [early[n] if n in early else resid(field_b[0], on_main, n) for n in (2 * i + 2, 2 * i + 3)]
         tm[32 * i : 32 * i + 32, :] = pair[0] + pair[1]
         pair = [resid(field_b[1], on_strip, n) for n in (2 * i + 2, 2 * i + 3)]
-        ts[32 * i : 32 * i + 32, :] = spread(pair[0] + pair[1])
-    rhs1 = dot(halve_rows(tm, 64), rm01) + dot(halve_rows(ts, 64), rs01)
+        pair = pair[0] + pair[1]
+        ts[32 * i : 32 * i + 32, :] = jnp.concatenate([pair] * 4, axis=0)
+    cell = jnp.where(lane < 96, 2 * lane, 2 * lane - 256)
+    pairs = halve_rows(tm, 64)
+    inner = from_lanes(pairs, cell & 127) + from_lanes(pairs, (cell + 1) & 127)
+    at = jnp.where(cell >= 64, cell - 120, cell + 24) & 31
+    tile = 32 * (row >> 2)
+    even_at, odd_at = (tile + at, tile + 64 + at), (tile + at + 1, tile + 65 + at)
+    pairs = halve_rows(ts, 64)
+    outer = from_lanes(pairs, even_at) + from_lanes(pairs, odd_at)
+    lane64 = iota((64, 128), 1)
+    use_inner = jnp.logical_and(lane64 >= 2, lane64 < 62)
+    use_outer = jnp.logical_or(lane64 < 68, lane64 >= 124)
+    rhs1 = jnp.where(use_inner, inner, jnp.where(use_outer, outer, 0.0))
     gg1[...] = (0.125 * rhs1).reshape(4, 16, 128)
 
     e1x = send_planes(gg1.at[0:2], gg1x.at[1], gg1.at[2:4], gg1x.at[0])
@@ -485,7 +499,9 @@
     r = f1[2:6] - ring_apply(v, cut_planes(k1_all, 2, 8), dg1[2:6], half1)
     for i in range(2):
         t1[16 * i : 16 * i + 16, :] = r[2 * i] + r[2 * i + 1]
-    rhs2 = (0.125 * dot(halve_rows(t1, 16), r12)).reshape(2, 8, 128)
+    pairs = halve_rows(t1, 16)
+    rhs2 = from_lanes(pairs, (2 * lane) & 127) + from_lanes(pairs, (2 * lane + 1) & 127)
+    rhs2 = (0.125 * rhs2).reshape(2, 8, 128)
 
     gl2[...] = jnp.where(lane < 32, rhs2[0], jnp.where(lane < 64, rot(rhs2[1], 32, 1), l2sum))
     e2 = send_far(gl2, gl2x)
@@ -550,7 +566,15 @@
     vb = sweep2(t2[...] * f2[...], 8)
     r = f2[2:16] - ring_apply(vb, cut_planes(k2_all, 1, 17), dg2[2:16], half2)
     l3 = to_level3([l2[i + 1] for i in range(7)])
-    f3 = to_level3([r[2 * i] + r[2 * i + 1] for i in range(7)])
+    f3 = []
+    for i in range(7):
+        pair = r[2 * i] + r[2 * i + 1]
+        f3.append(from_lanes(pair, (2 * lane) & 127) + from_lanes(pair, (2 * lane + 1) & 127))
+    t1[0:56, :] = jnp.concatenate(f3, axis=0)
+    f3 = 0.125 * halve_rows(t1, 28)
+    for i in range(7):
+        t3[i, 0:4, :] = f3[4 * i : 4 * i + 4, :]
+    f3 = t3[0:7]
     diag3 = l3 + most3
     inv3 = []
     for i in range(7):
@@ -562,8 +586,7 @@
     rest = f3[1:-1] - ring_apply(v3, cut_planes((k3,) + beside(k3, 2), 1, 8), diag3[1:-1], half3)
     v3 = v3[1:-1] + inv3[1:-1] * rest
 
-    p32 = ring_map(cut(64), 64, True)
-    wide3 = dot(v3.reshape(40, 128), p32)
+    wide3 = from_lanes(v3.reshape(40, 128), jnp.where(lane < 64, lane >> 1, ((lane - 128) >> 1) + 128))
     for i in range(5):
         double_rows(t1.at[8 * i : 8 * i + 8, :], wide3[8 * i : 8 * i + 4, :])
     e3 = t1[0:40, :].reshape(5, 8, 128)
@@ -575,8 +598,8 @@
     for c in ev1x + ev1s:
         c.arrived()
     fill1(va1, vv1, vv1x, rsv1)
-    p21 = ring_map(cut(96), 64, True)
-    double_rows(tm.at[0:96, :], dot(vb.reshape(48, 128), p21))
+    wide2 = from_lanes(vb.reshape(48, 128), jnp.where(lane < 96, lane >> 1, ((lane - 128) >> 1) + 128))
+    double_rows(tm.at[0:96, :], wide2)
     e2v = tm[0:96, :].reshape(6, 16, 128)
     inner = jnp.logical_or(lane < 68, lane >= 124)
     inner = jnp.concatenate([inner, inner], axis=0)
@@ -585,8 +608,8 @@
     v = sweep1(v, 2, inv1)
 
     e1 = v.reshape(96, 128)
-    double_rows(tm.at[0:192, :], dot(e1, ring_map(main_z, 96, True)))
-    double_rows(ts.at[0:192, :], dot(e1, ring_map(strip_z, 96, True)))
+    double_rows(tm.at[0:192, :], from_lanes(e1, lane >> 1))
+    double_rows(ts.at[0:192, :], from_lanes(e1, (strip_z(lane) >> 1) & 127))
     for c in evx:
         c.arrived()
         c.left()

time: 29 us -> 28 us (0.966)
  the two profiles are of different devices: /device:TPU:143 before, /device:TPU:134 now
where the time goes in v8:
time: 28 us; the launch traced here: 27.9 us
  Pallas kernels  27.2 us (97%)
  local copies, waits for them, and re-layouts  0.66 us (2%)
    pallas_call x1, Pallas kernels, on_device(): pl.pallas_call(body, out_shape=pltpu.VMEM(source.shape, F32), in_specs=[p...  27.2 us
    unnamed x1, local copies, waits for them, and re-layouts  0.66 us

profile of v8, /device:TPU:134, one launch (start us, length us, event | category | flops | bytes accessed | tf_op | source)
XLA Modules:
  0.0 27.9 jit_solution(8867996117481356673)
XLA Ops:
  0.0 27.2 %vcycle.1 = f32[8,32,128]{2,1,0:T(8,128)S(1)} custom-call(f32[8,32,128]{2,1,0:T(8,128)} %refs_0_.1, f32[8,32,128]{2,1,0:T(8,128)} %refs_1_.1, f32[8,32,128]{2,1,0:T(8,128)} %refs_2_.1), custom_call_target="tpu_custom_call" | custom-call | tf_op jit(solution)/shard_map/vcycle/pallas_call | solution.py:667
  27.2 0.7 %copy.5 = f32[8,32,128]{2,1,0:T(8,128)} copy(f32[8,32,128]{2,1,0:T(8,128)S(1)} %vcycle.1) | data formatting | bytes 262144

commit v9 on v8

--- a/solution.py
+++ b/solution.py
@@ -132,7 +132,7 @@
     nw, nz, f_hbm, k_hbm, l_hbm, out_ref,
     km, ks, pkm, pks, kbm, kbs, kam, kas, fm, fs, lm, ls, dgm, dgs, dm, ds_,
     avm, avs, apm, aps, aqm, aqs, arm, ars, bvm, bvs, bpm, bps, bqm, bqs, brm, brs, tm, ts, tlm, tls,
-    pack0, rs0, kd1, kd1x, gg1, gg1x, pv1, rsv1, vv1, vv1x,
+    pack0, rs0, pv1, rsv1, vv1, vv1x,
     k1l, k1, dg1, f1, va1, t1, kd2, kd2x, gl2, gl2x, k2, dg2, f2, l2, t2, t3, hello, loc_sem, send_sem, recv_sem,
 ):
     w, z = lax.axis_index("wide"), lax.axis_index("narrow")
@@ -178,25 +178,23 @@
     group, place = lane >> 5, lane & 31
 
     loads = []
-    for n, (src, dst) in enumerate(((k_hbm, km.at[4:12]), (f_hbm, fm.at[2:10]), (l_hbm, lm.at[2:10]))):
+    for n, (src, dst) in enumerate(((k_hbm, km.at[8:16]), (f_hbm, fm.at[6:14]), (l_hbm, lm.at[6:14]))):
         loads.append(pltpu.make_async_copy(src, dst, loc_sem.at[n]))
         loads[-1].start()
 
-    for ref in (rs0, rsv1, kd1x, gg1x, vv1x, kd2x, gl2x):
+    for ref in (rs0, rsv1, vv1x, kd2x, gl2x):
         ref[...] = jnp.zeros_like(ref)
 
-    def clear(k_planes, planes, v_plane):
+    def clear(k_planes, planes):
         def body():
-            km[k_planes] = jnp.zeros((4, 32, 128), F32)
-            fm[planes] = jnp.zeros((2, 32, 128), F32)
-            lm[planes] = jnp.zeros((2, 32, 128), F32)
-            bvm[v_plane] = jnp.zeros((32, 128), F32)
-            bvs[v_plane] = jnp.zeros((8, 128), F32)
+            km[k_planes] = jnp.zeros((8, 32, 128), F32)
+            fm[planes] = jnp.zeros((6, 32, 128), F32)
+            lm[planes] = jnp.zeros((6, 32, 128), F32)
 
         return body
 
-    pl.when(w == 0)(clear(slice(0, 4), slice(0, 2), 0))
-    pl.when(w == nw - 1)(clear(slice(12, 16), slice(10, 12), 11))
+    pl.when(w == 0)(clear(slice(0, 8), slice(0, 6)))
+    pl.when(w == nw - 1)(clear(slice(16, 24), slice(14, 20)))
 
     barrier = pltpu.get_barrier_semaphore()
 
@@ -219,17 +217,19 @@
     even = (eighth & 1) == 0
     spot = (0, 16, 8, 24)
 
-    def pack_strips(strips):
+    def pack_strips(planes):
         left, right = jnp.zeros((8, 128), F32), jnp.zeros((8, 128), F32)
-        for x, s in enumerate(strips):
-            r = rot(s, spot[x] - 24, 1)
-            left = jnp.where(eighth == spot[x] // 8, r, left)
-            right = jnp.where(eighth == (spot[x] // 8 + 1) % 4, r, right)
-        return left, rot(right, 32, 1)
+        for x, m in enumerate(planes):
+            for t in range(4):
+                r = rot(m[8 * t : 8 * t + 8, :], 32 * t + spot[x], 1)
+                at = 4 * t + spot[x] // 8
+                left = jnp.where((lane >> 3) == at, r, left)
+                right = jnp.where((lane >> 3) == (at - 1) % 16, r, right)
+        return left, rot(right, 16, 1)
 
     def merge(rs, n):
         out = {}
-        for step, half in ((0, 1), (1, 0), (1, 1), (2, 0)):
+        for step, half in [(step, half) for step in range(3) for half in range(2)]:
             left, right = rs[step, 0, half, n], rs[step, 1, half, n]
             out[step, half] = (jnp.where(even, left, right), jnp.where(even, right, left))
         return out
@@ -260,30 +260,22 @@
     def send_far(src, dst):
         return [send(src, dst.at[4 - a, 1 - b], a, b) for a, b in FAR]
 
-    e0k = send_planes(k_hbm.at[0:4], km.at[12:16], k_hbm.at[4:8], km.at[0:4])
-    e0f = send_planes(f_hbm.at[0:2], fm.at[10:12], f_hbm.at[6:8], fm.at[0:2])
-    e0l = send_planes(l_hbm.at[0:2], lm.at[10:12], l_hbm.at[6:8], lm.at[0:2])
-
-    for n, (ref, strip, off) in enumerate(((km, ks, 4), (fm, fs, 2), (lm, ls, 2))):
-        loads[n].wait()
-        own = [own_strip(ref[x + off]) for x in range(8)]
-        for x in range(8):
-            strip[x + off] = own[x]
+    e0k = send_planes(k_hbm, km.at[16:24], k_hbm, km.at[0:8])
+
+    for load in loads:
+        load.wait()
+    for n, (ref, off) in enumerate(((km, 8), (fm, 6), (lm, 6))):
         for half in range(2):
-            pack0[0, half, n], pack0[1, half, n] = pack_strips(own[4 * half : 4 * half + 4])
+            planes = [ref[x + off] for x in range(4 * half, 4 * half + 4)]
+            pack0[0, half, n], pack0[1, half, n] = pack_strips(planes)
 
     def send_strips(b):
         side = 0 if b < 0 else 1
-        out = []
-        for a in (0, -1, 1):
-            if a == 0:
-                out.append(send(pack0.at[side], rs0.at[1, side], a, b))
-            else:
-                half = 0 if a < 0 else 1
-                out.append(send(pack0.at[side, half], rs0.at[1 - a, side, half], a, b))
-        return out
+        return [send(pack0.at[side], rs0.at[1 - a, side], a, b) for a in (0, -1, 1)]
 
     e0s = send_strips(-1)
+    e0f = send_planes(f_hbm.at[0:6], fm.at[14:20], f_hbm.at[2:8], fm.at[0:6])
+    e0l = send_planes(l_hbm.at[0:6], lm.at[14:20], l_hbm.at[2:8], lm.at[0:6])
     def hear_hello():
         pl.semaphore_wait(hello, 1)
 
@@ -319,7 +311,7 @@
         ready(field_b[side], part, i, source[0][i] + part[0][2][i] * resid(source, part, i))
 
     def there0(i):
-        return inside(-1) if i < 2 else inside(1) if i >= 10 else 1
+        return inside(-1) if i < 6 else inside(1) if i >= 14 else 1
 
     lane32 = iota((32, 128), 1)
 
@@ -327,7 +319,7 @@
         around = neighbours(three(km, i + 2), three(pkm, i + 2), rows_beside)
         diag = lm[i] + 0.5 * (CALL * km[i + 2] + around)
         inv = OMEGA / diag
-        if not 2 <= i < 10:
+        if not 6 <= i < 14:
             inv = jnp.where(lane32 < 128 * there0(i), inv, 0.0)
         dgm[i], dm[i] = diag, inv
         ready(field_a[0], on_main, i, inv * fm[i])
@@ -354,90 +346,62 @@
     rm01, rs01 = ring_map(inner_z, 96), ring_map(outer_z, 96)
     r12, r23 = ring_map(cut(96), 64), ring_map(cut(64), 64)
 
-    for p in range(4, 12):
+    for ref, held, off in ((km, ks, 8), (fm, fs, 6), (lm, ls, 6)):
+        for x in range(8):
+            held[x + off] = own_strip(ref[x + off])
+    for p in range(8, 16):
         k_main(p)
+    for i in range(4, 8):
+        k_pair(i)
     for i in range(2, 6):
-        k_pair(i)
-    for i in range(4):
         tlm[32 * i : 32 * i + 32, :] = lm[2 * i + 2] + lm[2 * i + 3]
-    loop(3, 9, first_main)
-    for i in range(4, 8):
+    loop(7, 13, first_main)
+    for i in range(8, 12):
         sweep(i, 0)
-    early = {i: resid(field_b[0], on_main, i) for i in (5, 6)}
+    early = {i: resid(field_b[0], on_main, i) for i in (9, 10)}
 
     for c in e0k + e0s:
         c.arrived()
     merged = merge(rs0, 0)
-    for p in range(16):
-        own = ks[p] if 4 <= p < 12 else own_strip(km[p])
-        ks[p] = whole_strip(own, merged, p - 4)
-
-    for p in range(16):
+    for p in range(24):
+        own = ks[p] if 8 <= p < 16 else own_strip(km[p])
+        ks[p] = whole_strip(own, merged, p - 8)
+
+    for p in range(24):
         below, above = beside(ks[p])
         kbs[p], kas[p], pks[p] = below, above, below + above
-    for p in (1, 2, 3, 12, 13, 14):
+    for p in (*range(1, 8), *range(16, 23)):
         k_main(p)
-    for i in (0, 1, 6, 7):
+    for i in (0, 1, 2, 3, 8, 9, 10, 11):
         k_pair(i)
-    for i in range(8):
+    for i in range(12):
         ts[32 * i : 32 * i + 32, :] = spread(ks[2 * i] + ks[2 * i + 1])
 
-    coarse = dot(halve_rows(tm, 128), rm01) + dot(halve_rows(ts, 128), rs01)
-    k1l[...] = (0.125 * coarse).reshape(8, 16, 128)
-
+    coarse = dot(halve_rows(tm, 192), rm01) + dot(halve_rows(ts, 192), rs01)
+    k1l[...] = (0.125 * coarse).reshape(12, 16, 128)
+
+    kk = k1l[2:10]
+    for i in range(4):
+        t1[16 * i : 16 * i + 16, :] = kk[2 * i] + kk[2 * i + 1]
+    k2l = (0.125 * dot(halve_rows(t1, 32), r12)).reshape(4, 8, 128)
     for c in e0f + e0l:
         c.arrived()
     for n, (ref, strip) in ((1, (fm, fs)), (2, (lm, ls))):
         merged = merge(rs0, n)
-        for p in range(12):
-            own = strip[p] if 2 <= p < 10 else own_strip(ref[p])
-            strip[p] = whole_strip(own, merged, p - 2)
-
-    for i in range(4):
+        for p in range(20):
+            own = strip[p] if 6 <= p < 14 else own_strip(ref[p])
+            strip[p] = whole_strip(own, merged, p - 6)
+
+    for i in (0, 1, 6, 7):
+        tlm[32 * i : 32 * i + 32, :] = lm[2 * i + 2] + lm[2 * i + 3]
+    for i in range(8):
         tls[32 * i : 32 * i + 32, :] = spread(ls[2 * i + 2] + ls[2 * i + 3])
-    l1 = dot(halve_rows(tlm, 64), rm01) + dot(halve_rows(tls, 64), rs01)
-    l1 = (0.125 * l1).reshape(4, 16, 128)
-    own1 = k1l[2:6]
+    l1 = dot(halve_rows(tlm, 128), rm01) + dot(halve_rows(tls, 128), rs01)
+    l1 = (0.125 * l1).reshape(8, 16, 128)
     half1 = 0.5 * 0.25
-    diag1 = l1 + half1 * (CALL * own1 + ring_sum(k1l[1:7]))
-    kd1[:, 0], kd1[:, 1] = own1, diag1
-    ekd = send_planes(kd1.at[0:3], kd1x.at[1], kd1.at[1:4], kd1x.at[0])
-
-    for i in (0, 1, 2, 9, 10, 11):
-        first_main(i)
-    loop(0, 12, first_strip)
-    for i in (1, 2, 3, 8, 9, 10):
-        sweep(i, 0)
-    for i in range(1, 11):
-        sweep(i, 1)
-    for i in range(4):
-        pair = [early[n] if n in early else resid(field_b[0], on_main, n) for n in (2 * i + 2, 2 * i + 3)]
-        tm[32 * i : 32 * i + 32, :] = pair[0] + pair[1]
-        pair = [resid(field_b[1], on_strip, n) for n in (2 * i + 2, 2 * i + 3)]
-        pair = pair[0] + pair[1]
-        ts[32 * i : 32 * i + 32, :] = jnp.concatenate([pair] * 4, axis=0)
-    cell = jnp.where(lane < 96, 2 * lane, 2 * lane - 256)
-    pairs = halve_rows(tm, 64)
-    inner = from_lanes(pairs, cell & 127) + from_lanes(pairs, (cell + 1) & 127)
-    at = jnp.where(cell >= 64, cell - 120, cell + 24) & 31
-    tile = 32 * (row >> 2)
-    even_at, odd_at = (tile + at, tile + 64 + at), (tile + at + 1, tile + 65 + at)
-    pairs = halve_rows(ts, 64)
-    outer = from_lanes(pairs, even_at) + from_lanes(pairs, odd_at)
-    lane64 = iota((64, 128), 1)
-    use_inner = jnp.logical_and(lane64 >= 2, lane64 < 62)
-    use_outer = jnp.logical_or(lane64 < 68, lane64 >= 124)
-    rhs1 = jnp.where(use_inner, inner, jnp.where(use_outer, outer, 0.0))
-    gg1[...] = (0.125 * rhs1).reshape(4, 16, 128)
-
-    e1x = send_planes(gg1.at[0:2], gg1x.at[1], gg1.at[2:4], gg1x.at[0])
-
-    kk = k1l[...]
-    for i in range(4):
-        t1[16 * i : 16 * i + 16, :] = kk[2 * i] + kk[2 * i + 1]
-    k2l = (0.125 * dot(halve_rows(t1, 32), r12)).reshape(4, 8, 128)
+    dg1[...] = l1 + half1 * (CALL * k1l[2:10] + ring_sum(k1l[1:11]))
     for i in range(2):
-        t1[16 * i : 16 * i + 16, :] = l1[2 * i] + l1[2 * i + 1]
+        t1[16 * i : 16 * i + 16, :] = l1[2 * i + 2] + l1[2 * i + 3]
     l2own = (0.125 * dot(halve_rows(t1, 16), r12)).reshape(2, 8, 128)
     half2 = 0.5 * 0.0625
     diag2 = l2own + half2 * (CALL * k2l[1:3] + ring_sum(k2l))
@@ -446,11 +410,33 @@
     high = jnp.where(lane < 96, rot(both[2], 64, 1), rot(both[3], 96, 1))
     kd2[...] = jnp.where(lane < 64, low, high)
     l2sum = rot(l2own[0] + l2own[1], 64, 1)
+    for i in (*range(0, 7), *range(13, 20)):
+        first_main(i)
+    loop(0, 20, first_strip)
     ekd2 = send_far(kd2, kd2x)
-
-    evx = []
-    for ref in (bvm, bvs):
-        evx += [send(ref.at[8], ref.at[0], 1, 0), send(ref.at[3], ref.at[11], -1, 0)]
+    for i in (*range(1, 8), *range(12, 19)):
+        sweep(i, 0)
+    for i in range(1, 19):
+        sweep(i, 1)
+    for i in range(8):
+        pair = [early[n] if n in early else resid(field_b[0], on_main, n) for n in (2 * i + 2, 2 * i + 3)]
+        tm[32 * i : 32 * i + 32, :] = pair[0] + pair[1]
+        pair = [resid(field_b[1], on_strip, n) for n in (2 * i + 2, 2 * i + 3)]
+        pair = pair[0] + pair[1]
+        ts[32 * i : 32 * i + 32, :] = jnp.concatenate([pair] * 4, axis=0)
+    cell = jnp.where(lane < 96, 2 * lane, 2 * lane - 256)
+    pairs = halve_rows(tm, 128)
+    inner = from_lanes(pairs, cell & 127) + from_lanes(pairs, (cell + 1) & 127)
+    at = jnp.where(cell >= 64, cell - 120, cell + 24) & 31
+    tile = 32 * (row >> 2)
+    even_at, odd_at = (tile + at, tile + 64 + at), (tile + at + 1, tile + 65 + at)
+    pairs = halve_rows(ts, 128)
+    outer = from_lanes(pairs, even_at) + from_lanes(pairs, odd_at)
+    lane_all = iota((128, 128), 1)
+    use_inner = jnp.logical_and(lane_all >= 2, lane_all < 62)
+    use_outer = jnp.logical_or(lane_all < 68, lane_all >= 124)
+    rhs1 = jnp.where(use_inner, inner, jnp.where(use_outer, outer, 0.0))
+    f1[...] = (0.125 * rhs1).reshape(8, 16, 128)
 
     def pack_sides1(arr):
         left, right = jnp.zeros((8, 128), F32), jnp.zeros((8, 128), F32)
@@ -473,14 +459,9 @@
                 center = x_ref[0, x + 3, rows, :] if x < 0 else x_ref[1, x - 4, rows, :] if x > 3 else own[x, rows, :]
                 ref[p, 8 * t : 8 * t + 8, :] = jnp.where(lane < 64, center, side)
 
-    for c in ekd + e1x:
-        c.arrived()
-    k1[0:3], k1[3:7], k1[7:10] = kd1x[0, :, 0], own1, kd1x[1, :, 0]
-    dg1[0:2], dg1[2:6], dg1[6:8] = kd1x[0, 1:3, 1], diag1, kd1x[1, 0:2, 1]
-    f1[0:2], f1[2:6], f1[6:8] = gg1x[0], gg1[...], gg1x[1]
+    k1[...] = k1l[1:11]
     k1_all = k1[...]
     k1_all = (k1_all,) + beside(k1_all, 2)
-
     lane1 = iota((2, 16, 128), 2)
 
     def inverse1(lo, hi, step):
@@ -510,6 +491,10 @@
     ev1x = send_planes(vv1.at[0:3], vv1x.at[1], vv1.at[1:4], vv1x.at[0])
     ev1s = send_sides(pv1, rsv1)
 
+    later = e2 + ev1x + ev1s
+    for c in started:
+        if not any(c is other for other in later):
+            c.left()
     def around2(mine, ref, step):
         mid = mine if step == 4 else ref[step, 1]
         return mid, rot(ref[step, 2], 32, 1), rot(ref[step, 0], -32, 1)
@@ -610,11 +595,8 @@
     e1 = v.reshape(96, 128)
     double_rows(tm.at[0:192, :], from_lanes(e1, lane >> 1))
     double_rows(ts.at[0:192, :], from_lanes(e1, (strip_z(lane) >> 1) & 127))
-    for c in evx:
-        c.arrived()
-        c.left()
     def correct(i):
-        at = 32 * (i // 2)
+        at = 32 * ((i - 4) // 2)
         m = bvm[i] + tm[at : at + 32, :]
         s = ts[at : at + 8, :]
         for t in range(1, 4):
@@ -622,8 +604,8 @@
         ready(field_a[0], on_main, i, m)
         ready(field_a[1], on_strip, i, bvs[i] + s)
 
-    loop(0, 12, correct)
-    for i in range(1, 11):
+    loop(4, 16, correct)
+    for i in range(5, 15):
         sweep(i, 0)
         sweep(i, 1)
 
@@ -632,12 +614,11 @@
         s = bvs[i] + ds_[i] * resid(field_b[1], on_strip, i)
         s = jnp.where(place < 8, s, rot(s, -16, 1))
         ends = jnp.concatenate([rot(s, 120 - 32 * t, 1) for t in range(4)], axis=0)
-        out_ref[i - 2] = jnp.where(jnp.logical_or(lane32 < 4, lane32 >= 124), ends, m)
-
-    loop(2, 10, last)
-    for c in started:
-        if not any(c is done for done in evx):
-            c.left()
+        out_ref[i - 6] = jnp.where(jnp.logical_or(lane32 < 4, lane32 >= 124), ends, m)
+
+    loop(6, 14, last)
+    for c in later:
+        c.left()
 
 
 def solution(mesh):
@@ -650,15 +631,14 @@
         def pair(n):
             return [vm(n, 32, 128), vm(n, 8, 128)]
 
-        scratch = pair(16) * 4 + pair(12) * 4 + pair(12) * 8 + [vm(256, 128), vm(256, 128), vm(128, 128), vm(128, 128)]
+        scratch = pair(24) * 4 + pair(20) * 12 + [vm(384, 128), vm(384, 128), vm(256, 128), vm(256, 128)]
         scratch += [vm(2, 2, 3, 8, 128), vm(3, 2, 2, 3, 8, 128)]
-        scratch += [vm(4, 2, 16, 128), vm(2, 3, 2, 16, 128), vm(4, 16, 128), vm(2, 2, 16, 128)]
         scratch += [vm(2, 8, 128), vm(3, 2, 8, 128)]
         scratch += [vm(4, 16, 128), vm(2, 3, 16, 128)]
-        scratch += [vm(8, 16, 128), vm(10, 16, 128), vm(8, 16, 128), vm(8, 16, 128), vm(10, 16, 128), vm(128, 128)]
+        scratch += [vm(12, 16, 128), vm(10, 16, 128), vm(8, 16, 128), vm(8, 16, 128), vm(10, 16, 128), vm(128, 128)]
         scratch += [vm(8, 128), vm(9, 3, 8, 128), vm(8, 128), vm(9, 3, 8, 128)]
         scratch += [vm(18, 8, 128), vm(18, 8, 128), vm(18, 8, 128), vm(9, 8, 128), vm(18, 8, 128), vm(9, 8, 128)]
-        n = 12 + 2 + 2 + 26 + 4 + 26 + 8
+        n = 12 + 26 + 26 + 8
         scratch += [pltpu.SemaphoreType.REGULAR, pltpu.SemaphoreType.DMA((3,)), pltpu.SemaphoreType.DMA((n,)), pltpu.SemaphoreType.DMA((n,))]
 
         def body(*refs):

time: 28 us -> 27.1 us (0.968)
  the two profiles are of different devices: /device:TPU:134 before, /device:TPU:198 now
where the time goes in v9:
time: 27.1 us; the launch traced here: 27 us
  Pallas kernels  26.3 us (97%)
  local copies, waits for them, and re-layouts  0.66 us (2%)
    pallas_call x1, Pallas kernels, on_device(): pl.pallas_call(body, out_shape=pltpu.VMEM(source.shape, F32), in_specs=[p...  26.3 us
    unnamed x1, local copies, waits for them, and re-layouts  0.66 us

profile of v9, /device:TPU:198, one launch (start us, length us, event | category | flops | bytes accessed | tf_op | source)
XLA Modules:
  0.0 27.0 jit_solution(11194530078231993072)
XLA Ops:
  0.0 26.3 %vcycle.1 = f32[8,32,128]{2,1,0:T(8,128)S(1)} custom-call(f32[8,32,128]{2,1,0:T(8,128)} %refs_0_.1, f32[8,32,128]{2,1,0:T(8,128)} %refs_1_.1, f32[8,32,128]{2,1,0:T(8,128)} %refs_2_.1), custom_call_target="tpu_custom_call" | custom-call | tf_op jit(solution)/shard_map/vcycle/pallas_call | solution.py:647
  26.3 0.7 %copy.5 = f32[8,32,128]{2,1,0:T(8,128)} copy(f32[8,32,128]{2,1,0:T(8,128)S(1)} %vcycle.1) | data formatting | bytes 262144

commit v10 on v9

--- a/solution.py
+++ b/solution.py
@@ -205,7 +205,7 @@
         return body
 
     for a, b in FAR:
-        if b >= 0:
+        if b >= 0 and abs(a) <= 3:
             pl.when(in_grid(a, b))(greet(a, b))
     def own_strip(m):
         out = rot(m[0:8, :], 8, 1)
@@ -244,7 +244,7 @@
     def count(pos, reach, size):
         return jnp.minimum(pos, reach) + 1 + jnp.minimum(size - 1 - pos, reach)
 
-    pl.semaphore_wait(barrier, count(w, 4, nw) * (1 + has_left) - 1)
+    pl.semaphore_wait(barrier, count(w, 3, nw) * (1 + has_left) - 1)
 
     def say_hello():
         pl.semaphore_signal(hello, inc=1, device_id=device(0, -1), device_id_type=MESH)

time: 27.1 us -> 26.5 us (0.978)
  Pallas kernels: 26.3 us -> 25.7 us
    pallas_call x1, Pallas kernels: 26.3 us -> 25.7 us  [on_device(): pl.pallas_call(body, out_shape=pltpu.VMEM(source.shape, F32), in_specs=[p...]
where the time goes in v10:
time: 26.5 us; the launch traced here: 26.4 us
  Pallas kernels  25.7 us (97%)
  local copies, waits for them, and re-layouts  0.66 us (2%)
    pallas_call x1, Pallas kernels, on_device(): pl.pallas_call(body, out_shape=pltpu.VMEM(source.shape, F32), in_specs=[p...  25.7 us
    unnamed x1, local copies, waits for them, and re-layouts  0.66 us

profile of v10, /device:TPU:198, one launch (start us, length us, event | category | flops | bytes accessed | tf_op | source)
XLA Modules:
  0.0 26.4 jit_solution(2327348329383801585)
XLA Ops:
  0.0 25.7 %vcycle.1 = f32[8,32,128]{2,1,0:T(8,128)S(1)} custom-call(f32[8,32,128]{2,1,0:T(8,128)} %refs_0_.1, f32[8,32,128]{2,1,0:T(8,128)} %refs_1_.1, f32[8,32,128]{2,1,0:T(8,128)} %refs_2_.1), custom_call_target="tpu_custom_call" | custom-call | tf_op jit(solution)/shard_map/vcycle/pallas_call | solution.py:647
  25.7 0.7 %copy.5 = f32[8,32,128]{2,1,0:T(8,128)} copy(f32[8,32,128]{2,1,0:T(8,128)S(1)} %vcycle.1) | data formatting | bytes 262144

commit v11 on v10

--- a/solution.py
+++ b/solution.py
@@ -152,14 +152,17 @@
     class Message:
         def __init__(self, n, src, dst, a, b):
             self.to, self.origin = (a, b), (-a, -b)
-            self.copy = pltpu.make_async_remote_copy(
-                src_ref=src, dst_ref=dst, send_sem=send_sem.at[n], recv_sem=recv_sem.at[n],
-                device_id=device(a, b), device_id_type=MESH,
-            )
+            self.copy, self.same = [
+                pltpu.make_async_remote_copy(
+                    src_ref=src, dst_ref=dst, send_sem=send_sem.at[n], recv_sem=recv_sem.at[n],
+                    device_id=device(*other), device_id_type=MESH,
+                )
+                for other in (self.to, self.origin)
+            ]
             pl.when(in_grid(*self.to))(self.copy.start)
 
         def arrived(self):
-            pl.when(in_grid(*self.origin))(self.copy.wait_recv)
+            pl.when(in_grid(*self.origin))(self.same.wait_recv)
 
         def left(self):
             pl.when(in_grid(*self.to))(self.copy.wait_send)

time: 26.5 us -> 26.5 us (level)
  no operation moved by 1% of the time
where the time goes in v11:
time: 26.5 us; the launch traced here: 26.4 us
  Pallas kernels  25.7 us (97%)
  local copies, waits for them, and re-layouts  0.66 us (2%)
    pallas_call x1, Pallas kernels, on_device(): pl.pallas_call(body, out_shape=pltpu.VMEM(source.shape, F32), in_specs=[p...  25.7 us
    unnamed x1, local copies, waits for them, and re-layouts  0.66 us

profile of v11, /device:TPU:198, one launch (start us, length us, event | category | flops | bytes accessed | tf_op | source)
XLA Modules:
  0.0 26.4 jit_solution(2327348329383801585)
XLA Ops:
  0.0 25.7 %vcycle.1 = f32[8,32,128]{2,1,0:T(8,128)S(1)} custom-call(f32[8,32,128]{2,1,0:T(8,128)} %refs_0_.1, f32[8,32,128]{2,1,0:T(8,128)} %refs_1_.1, f32[8,32,128]{2,1,0:T(8,128)} %refs_2_.1), custom_call_target="tpu_custom_call" | custom-call | tf_op jit(solution)/shard_map/vcycle/pallas_call | solution.py:650
  25.7 0.7 %copy.5 = f32[8,32,128]{2,1,0:T(8,128)} copy(f32[8,32,128]{2,1,0:T(8,128)S(1)} %vcycle.1) | data formatting | bytes 262144

commit v12 on v11

--- a/solution.py
+++ b/solution.py
@@ -133,7 +133,7 @@
     km, ks, pkm, pks, kbm, kbs, kam, kas, fm, fs, lm, ls, dgm, dgs, dm, ds_,
     avm, avs, apm, aps, aqm, aqs, arm, ars, bvm, bvs, bpm, bps, bqm, bqs, brm, brs, tm, ts, tlm, tls,
     pack0, rs0, pv1, rsv1, vv1, vv1x,
-    k1l, k1, dg1, f1, va1, t1, kd2, kd2x, gl2, gl2x, k2, dg2, f2, l2, t2, t3, hello, loc_sem, send_sem, recv_sem,
+    k1l, dg1, f1, va1, t1, kd2, kd2x, gl2, gl2x, k2, dg2, f2, l2, t2, t3, hello, loc_sem, send_sem, recv_sem,
 ):
     w, z = lax.axis_index("wide"), lax.axis_index("narrow")
 
@@ -263,7 +263,7 @@
     def send_far(src, dst):
         return [send(src, dst.at[4 - a, 1 - b], a, b) for a, b in FAR]
 
-    e0k = send_planes(k_hbm, km.at[16:24], k_hbm, km.at[0:8])
+    e0k = send_planes(k_hbm.at[0:7], km.at[16:23], k_hbm.at[1:8], km.at[1:8])
 
     for load in loads:
         load.wait()
@@ -366,24 +366,24 @@
     for c in e0k + e0s:
         c.arrived()
     merged = merge(rs0, 0)
-    for p in range(24):
+    for p in range(1, 23):
         own = ks[p] if 8 <= p < 16 else own_strip(km[p])
         ks[p] = whole_strip(own, merged, p - 8)
 
-    for p in range(24):
+    for p in range(1, 23):
         below, above = beside(ks[p])
         kbs[p], kas[p], pks[p] = below, above, below + above
     for p in (*range(1, 8), *range(16, 23)):
         k_main(p)
-    for i in (0, 1, 2, 3, 8, 9, 10, 11):
+    for i in (1, 2, 3, 8, 9, 10):
         k_pair(i)
-    for i in range(12):
+    for i in range(1, 11):
         ts[32 * i : 32 * i + 32, :] = spread(ks[2 * i] + ks[2 * i + 1])
 
-    coarse = dot(halve_rows(tm, 192), rm01) + dot(halve_rows(ts, 192), rs01)
-    k1l[...] = (0.125 * coarse).reshape(12, 16, 128)
-
-    kk = k1l[2:10]
+    coarse = dot(halve_rows(tm.at[32:352, :], 160), rm01) + dot(halve_rows(ts.at[32:352, :], 160), rs01)
+    k1l[...] = (0.125 * coarse).reshape(10, 16, 128)
+
+    kk = k1l[1:9]
     for i in range(4):
         t1[16 * i : 16 * i + 16, :] = kk[2 * i] + kk[2 * i + 1]
     k2l = (0.125 * dot(halve_rows(t1, 32), r12)).reshape(4, 8, 128)
@@ -402,7 +402,7 @@
     l1 = dot(halve_rows(tlm, 128), rm01) + dot(halve_rows(tls, 128), rs01)
     l1 = (0.125 * l1).reshape(8, 16, 128)
     half1 = 0.5 * 0.25
-    dg1[...] = l1 + half1 * (CALL * k1l[2:10] + ring_sum(k1l[1:11]))
+    dg1[...] = l1 + half1 * (CALL * k1l[1:9] + ring_sum(k1l[...]))
     for i in range(2):
         t1[16 * i : 16 * i + 16, :] = l1[2 * i + 2] + l1[2 * i + 3]
     l2own = (0.125 * dot(halve_rows(t1, 16), r12)).reshape(2, 8, 128)
@@ -462,8 +462,7 @@
                 center = x_ref[0, x + 3, rows, :] if x < 0 else x_ref[1, x - 4, rows, :] if x > 3 else own[x, rows, :]
                 ref[p, 8 * t : 8 * t + 8, :] = jnp.where(lane < 64, center, side)
 
-    k1[...] = k1l[1:11]
-    k1_all = k1[...]
+    k1_all = k1l[...]
     k1_all = (k1_all,) + beside(k1_all, 2)
     lane1 = iota((2, 16, 128), 2)
 
@@ -638,7 +637,7 @@
         scratch += [vm(2, 2, 3, 8, 128), vm(3, 2, 2, 3, 8, 128)]
         scratch += [vm(2, 8, 128), vm(3, 2, 8, 128)]
         scratch += [vm(4, 16, 128), vm(2, 3, 16, 128)]
-        scratch += [vm(12, 16, 128), vm(10, 16, 128), vm(8, 16, 128), vm(8, 16, 128), vm(10, 16, 128), vm(128, 128)]
+        scratch += [vm(10, 16, 128), vm(8, 16, 128), vm(8, 16, 128), vm(10, 16, 128), vm(128, 128)]
         scratch += [vm(8, 128), vm(9, 3, 8, 128), vm(8, 128), vm(9, 3, 8, 128)]
         scratch += [vm(18, 8, 128), vm(18, 8, 128), vm(18, 8, 128), vm(9, 8, 128), vm(18, 8, 128), vm(9, 8, 128)]
         n = 12 + 26 + 26 + 8

time: 26.5 us -> 26.3 us (level)
  no operation moved by 1% of the time
where the time goes in v12:
time: 26.3 us; the launch traced here: 26.2 us
  Pallas kernels  25.5 us (97%)
  local copies, waits for them, and re-layouts  0.66 us (3%)
    pallas_call x1, Pallas kernels, on_device(): pl.pallas_call(body, out_shape=pltpu.VMEM(source.shape, F32), in_specs=[p...  25.5 us
    unnamed x1, local copies, waits for them, and re-layouts  0.66 us

profile of v12, /device:TPU:198, one launch (start us, length us, event | category | flops | bytes accessed | tf_op | source)
XLA Modules:
  0.0 26.2 jit_solution(15345940323983242421)
XLA Ops:
  0.0 25.5 %vcycle.1 = f32[8,32,128]{2,1,0:T(8,128)S(1)} custom-call(f32[8,32,128]{2,1,0:T(8,128)} %refs_0_.1, f32[8,32,128]{2,1,0:T(8,128)} %refs_1_.1, f32[8,32,128]{2,1,0:T(8,128)} %refs_2_.1), custom_call_target="tpu_custom_call" | custom-call | tf_op jit(solution)/shard_map/vcycle/pallas_call | solution.py:649
  25.5 0.7 %copy.5 = f32[8,32,128]{2,1,0:T(8,128)} copy(f32[8,32,128]{2,1,0:T(8,128)S(1)} %vcycle.1) | data formatting | bytes 262144
